TPU v7x, 512 devices: a whole 4x4x16 slice. The times are simulated.
512 devices in a mesh: expert: 64 (over y, x, z_hi, core), mp: 8 (over z_lo).
Axes of the slice: x: 4, y: 4, z: 16 (z_hi: 2, z_lo: 8; z = z_hi * 8 + z_lo), core: 2. Of those that a mesh axis runs over, the one named last changes fastest.
Arguments:
- tokens: bfloat16 [8192, 3584], P('expert'), may hold values from -6 to 6
- routes: int32 [8192, 2], P('expert'), may hold values from 0 to 31, all different within a row; in each aligned block of 128 rows (0 to 127, 128 to 255, ...) at most 16 rows name the same one
- gate_values: float32 [8192, 2], P('expert'), may hold values from 0.2 to 1
- expert_weights: bfloat16 [64, 3, 1792, 1024], P('expert', None, None, 'mp'), may hold values from -0.09375 to 0.09375
- old_owner: int32 [32], replicated, may hold values from 0 to 31, as said below
- new_owner: int32 [32], replicated, may hold values from 0 to 31, as said below
Outputs:
- mixed: bfloat16 [8192, 3584], P('expert', 'mp')
- relocated: bfloat16 [64, 3, 1792, 1024], P('expert', None, None, 'mp')
Inputs may be any that keep to these rules, and one draw needn't show every extreme that they name: `routes`: in each aligned block of 128 rows (the rows of one index of expert) no expert is named by more than 16 rows. `old_owner`: each slot holds exactly one expert. Each slot holds exactly one expert; exactly 2 experts have a new_owner other than their old_owner.
All inputs are finite; a program needn't handle non-finite values.
Results may differ from a plain program's by a relative error of at most 0.019.
Values may be sent and summed in bfloat16 or wider, within the bound.
No kernel may reach another device: no remote copies, remote signals or barrier semaphores. Data moves between devices by JAX's collectives and lax.ppermute only.
A program may use at most 64 MiB of HBM per device.

v0:
```python
import jax
import jax.numpy as jnp
from jax import lax
from jax.sharding import PartitionSpec as P


def from_partner(value, axis, bit):
    return lax.ppermute(value, axis, [(i, i ^ 1 << bit) for i in range(lax.axis_size(axis))])


def shards(tokens, routes, gate_values, expert_weights, old_owner, new_owner):
    slot_count = old_owner.shape[0]
    devices = lax.axis_size("expert")
    mp_count = lax.axis_size("mp")
    tok_rows = tokens.shape[0]
    top_count = routes.shape[1]
    capacity = 2 * tok_rows * top_count // slot_count
    model_width = tokens.shape[1]
    sub_cols = model_width // (2 * mp_count)
    own_weights = expert_weights[0]
    slot_ids = jnp.arange(slot_count, dtype=jnp.int32)
    newcomer = jnp.sum(
        jnp.where(new_owner[None, :] == slot_ids[:, None], slot_ids[None, :], 0), axis=1
    )
    source_slot = old_owner[newcomer]
    half_rows = own_weights.shape[1]
    pieces = own_weights.reshape(3, devices, half_rows // devices, own_weights.shape[2])
    spread = lax.all_to_all(pieces, "expert", split_axis=1, concat_axis=1, tiled=True)
    device_ids = jnp.arange(devices, dtype=jnp.int32)
    pick_rows = 2 * source_slot[device_ids // 2] + device_ids % 2
    chosen = jnp.take(spread, pick_rows, axis=1)
    arrived = lax.all_to_all(chosen, "expert", split_axis=1, concat_axis=1, tiled=True)
    relocated = arrived.reshape(own_weights.shape)
    flat_routes = routes.reshape(-1)
    onehot = (flat_routes[:, None] == slot_ids[None, :]).astype(jnp.int32)
    rank_in = jnp.sum((jnp.cumsum(onehot, axis=0) - onehot) * onehot, axis=1)
    target = jnp.sum(onehot * new_owner[None, :], axis=1)
    slot_match = target[:, None, None] == slot_ids[None, :, None]
    rank_match = rank_in[:, None, None] == jnp.arange(capacity, dtype=jnp.int32)[None, None, :]
    matches = (
        (slot_match & rank_match)
        .astype(jnp.bfloat16)
        .reshape(tok_rows, top_count, slot_count, capacity)
    )
    select = jnp.sum(matches, axis=1)
    mp_index = lax.axis_index("mp")
    columns = lax.dynamic_slice_in_dim(tokens, mp_index * 2 * sub_cols, 2 * sub_cols, 1).reshape(
        tok_rows, 2, sub_cols
    )
    outgoing = jnp.einsum(
        "tsc,thb->shcb", select, columns, preferred_element_type=jnp.float32
    ).astype(jnp.bfloat16)
    outgoing = outgoing.reshape(devices, capacity, sub_cols)
    incoming = lax.all_to_all(outgoing, "expert", split_axis=0, concat_axis=0, tiled=True)
    flat_rows = incoming.reshape(devices * capacity, sub_cols)
    pair_weights = relocated[0:2]
    weight_part = pair_weights
    halfsum = jnp.einsum(
        "rd,gdf->rgf",
        lax.all_gather(flat_rows, "mp", axis=1, tiled=True),
        weight_part,
        preferred_element_type=jnp.float32,
    )
    partner = from_partner(halfsum, "expert", 0)
    summed = halfsum + partner
    hidden = (jax.nn.silu(summed[:, 0]) * summed[:, 1]).astype(jnp.bfloat16)
    down_rows = relocated[2]
    weight_part = down_rows
    expert_out = lax.psum_scatter(
        lax.dot_general(
            weight_part, hidden, (((1,), (1,)), ((), ())), preferred_element_type=jnp.float32
        ).astype(jnp.bfloat16),
        "mp",
        scatter_dimension=0,
        tiled=True,
    )
    returning = expert_out.reshape(sub_cols, devices, capacity)
    arrived_out = lax.all_to_all(returning, "expert", split_axis=1, concat_axis=1, tiled=True)
    table = jnp.transpose(arrived_out.reshape(sub_cols, slot_count, 2, capacity), (1, 3, 2, 0))
    table = table.reshape(slot_count * capacity, 2, sub_cols)
    picked = jnp.take(table, target * capacity + rank_in, axis=0).astype(jnp.float32)
    picked = picked.reshape(tok_rows, top_count, 2 * sub_cols)
    mixed = jnp.sum(picked * gate_values[:, :, None], axis=1)
    return (mixed.astype(jnp.bfloat16), relocated[None])


def solution(mesh):
    in_specs = (
        P("expert", None),
        P("expert", None),
        P("expert", None),
        P("expert", None, None, "mp"),
        P(),
        P(),
    )
    out_specs = (P("expert", "mp"), P("expert", None, None, "mp"))
    return jax.shard_map(shards, mesh=mesh, in_specs=in_specs, out_specs=out_specs, check_vma=False)
```

profile of v0, /device:TPU:1, one launch (start us, length us, event | category | flops | bytes accessed | tf_op | source)
XLA Modules:
  0.0 436.8 jit_solution(7663514849411366818)
XLA Ops:
  7.2 0.9 copy.71
  8.0 0.1 eq.80
  8.2 0.1 eq.76
  8.3 0.6 reduce-window.6
  8.9 0.2 slice_reduce_fusion
  9.2 0.8 select_reduce_fusion
  9.9 0.1 reduce_sum.55
  10.2 0.1 reduce_sum.57
  10.4 0.1 constant_dynamic-slice_fusion
  10.5 0.1 copy.79
  10.7 0.3 fusion.2
  11.1 1.1 copy.83
  12.2 22.2 %all-to-all-start.2 = ((bf16[64,16,224]{2,1,0:T(8,128)(2,1)}), bf16[64,16,224]{2,1,0:T(8,128)(2,1)S(1)}, u32[]{:S(2)}, u32[]{:S(2)}) async-start(bf16[64,16,224]{2,1,0:T(8,128)(2,1)} %bitcast.12), calls=%async_computation.2 | async-start | bytes 1048576 | tf_op jit(solution)/shard_map/all_to_all | solution.py:54
  34.4 2.2 reshape_squeeze.3
  36.6 1.5 copy.77
  38.1 18.1 %all-to-all-done.2 = bf16[64,16,224]{2,1,0:T(8,128)(2,1)S(1)} async-done(((bf16[64,16,224]{2,1,0:T(8,128)(2,1)}), bf16[64,16,224]{2,1,0:T(8,128)(2,1)S(1)}, u32[]{:S(2)}, u32[]{:S(2)}) %all-to-all-start.2) | async-done | bytes 458784 | tf_op jit(solution)/shard_map/all_to_all | solution.py:54
  56.2 4.8 %all-to-all-start = ((bf16[3,64,28,128]{3,2,0,1:T(8,128)(2,1)}), bf16[3,64,28,128]{3,2,0,1:T(8,128)(2,1)S(1)}, u32[]{:S(2)}, u32[]{:S(2)}) async-start(bf16[3,64,28,128]{3,2,0,1:T(8,128)(2,1)} %copy.77), calls=%async_computation | async-start | bytes 3145728 | tf_op jit(solution)/shard_map/all_to_all | solution.py:28
  61.1 0.1 select_reduce_fusion.1
  61.2 1.0 copy.84
  62.3 0.7 gather_fusion
  63.0 0.8 gather_fusion.1
  63.8 30.3 %all-to-all-done = bf16[3,64,28,128]{3,2,0,1:T(8,128)(2,1)S(1)} async-done(((bf16[3,64,28,128]{3,2,0,1:T(8,128)(2,1)}), bf16[3,64,28,128]{3,2,0,1:T(8,128)(2,1)S(1)}, u32[]{:S(2)}, u32[]{:S(2)}) %all-to-all-start) | async-done | bytes 1376288 | tf_op jit(solution)/shard_map/all_to_all | solution.py:28
  94.1 1.5 copy.78
  95.6 2.3 gather_fusion.2
  97.9 0.2 select_bitcast_fusion
  98.1 80.5 %all_to_all.20 = bf16[3,64,28,128]{3,2,0,1:T(8,128)(2,1)S(1)} all-to-all(bf16[3,64,28,128]{3,2,0,1:T(8,128)(2,1)S(1)} %select_bitcast_fusion), channel_id=1, replica_groups=mesh['expert'=64,'mp'=8] {'expert'}, dimensions={1} | all-to-all | bytes 2752512 | tf_op jit(solution)/shard_map/all_to_all | solution.py:32
  178.6 0.1 slice.39
  178.7 0.7 copy.85
  179.4 88.9 %all-gather.2.cloned.1.call-done = bf16[1024,1792]{0,1:T(8,128)(2,1)} async-done(((bf16[1024,224]{0,1:T(8,128)(2,1)}), bf16[1024,1792]{0,1:T(8,128)(2,1)}) %all-gather.2.cloned.1.call-update) | async-done | bytes 3670032 | tf_op jit(solution)/shard_map/all_gather | solution.py:60
  268.3 4.2 fusion
  272.5 2.4 collective-permute-start
  275.0 0.1 squeeze.2
  275.1 2.5 collective-permute-done
  277.5 1.6 add.155
  279.2 3.0 convolution_convert_fusion
  282.2 100.8 %reduce-scatter.2.cloned.1.call-done = bf16[224,1024]{1,0:T(8,128)(2,1)} async-done(((bf16[1792,1024]{1,0:T(8,128)(2,1)}), bf16[224,1024]{1,0:T(8,128)(2,1)}) %reduce-scatter.2.cloned.1.call-update) | async-done | bytes 458768 | tf_op jit(solution)/shard_map/reduce_scatter | solution.py:69
  383.0 2.0 copy.87
  385.1 12.3 %all-to-all-start.3 = ((bf16[224,64,16]{0,2,1:T(8,128)(2,1)}), bf16[224,64,16]{0,2,1:T(8,128)(2,1)S(1)}, u32[]{:S(2)}, u32[]{:S(2)}) async-start(bf16[224,64,16]{0,2,1:T(8,128)(2,1)} %bitcast.17), calls=%async_computation.4 | async-start | bytes 1048576 | tf_op jit(solution)/shard_map/all_to_all | solution.py:78
  397.4 0.1 copy.76
  397.6 0.1 copy.90
  397.7 1.5 copy.91
  399.2 3.3 broadcast_in_dim_reshape.4
  402.5 23.7 %all-to-all-done.3 = bf16[224,64,16]{0,2,1:T(8,128)(2,1)S(1)} async-done(((bf16[224,64,16]{0,2,1:T(8,128)(2,1)}), bf16[224,64,16]{0,2,1:T(8,128)(2,1)S(1)}, u32[]{:S(2)}, u32[]{:S(2)}) %all-to-all-start.3) | async-done | bytes 458784 | tf_op jit(solution)/shard_map/all_to_all | solution.py:78
  426.2 0.5 copy.89
  426.8 1.2 gather_fusion.3
  428.0 0.3 gather.20
  428.3 0.9 multiply_reduce_fusion
  429.2 0.8 copy.92
  (33 shorter events, 0.6 us)
Async XLA Ops:
  7.2 3.2 copy-start
  12.2 44.1 %all-to-all-start.2 = ((bf16[64,16,224]{2,1,0:T(8,128)(2,1)}), bf16[64,16,224]{2,1,0:T(8,128)(2,1)S(1)}, u32[]{:S(2)}, u32[]{:S(2)}) async-start(bf16[64,16,224]{2,1,0:T(8,128)(2,1)} %bitcast.12), calls=%async_computation.2 | async-start | bytes 1048576 | tf_op jit(solution)/shard_map/all_to_all | solution.py:54
  38.1 23.0 %copy-start.3 = (s32[32]{0:T(128)S(1)}, s32[32]{0:T(128)}, u32[]{:S(2)}) copy-start(s32[32]{0:T(128)} %param.11) | copy-start | bytes 388
  38.1 24.2 %copy-start.1 = (s32[32]{0:T(128)S(1)}, s32[32]{0:T(128)}, u32[]{:S(2)}) copy-start(s32[32]{0:T(128)} %param.10) | copy-start | bytes 388
  56.2 37.9 %all-to-all-start = ((bf16[3,64,28,128]{3,2,0,1:T(8,128)(2,1)}), bf16[3,64,28,128]{3,2,0,1:T(8,128)(2,1)S(1)}, u32[]{:S(2)}, u32[]{:S(2)}) async-start(bf16[3,64,28,128]{3,2,0,1:T(8,128)(2,1)} %copy.77), calls=%async_computation | async-start | bytes 3145728 | tf_op jit(solution)/shard_map/all_to_all | solution.py:28
  61.0 207.3 %all-gather.2.cloned.1.call-start = ((), (), s32[]{:S(2)}) async-start(), calls=%async_computation.5 | async-start | bytes 4128768 | tf_op jit(solution)/shard_map/all_gather | solution.py:60
  62.2 320.8 %reduce-scatter.2.cloned.1.call-start = ((), (), s32[]{:S(2)}) async-start(), calls=%async_computation.6 | async-start | bytes 4128768 | tf_op jit(solution)/shard_map/reduce_scatter | solution.py:69
  272.5 5.0 %collective-permute-start = (f32[1024,2,128]{2,0,1:T(8,128)}, f32[1024,2,128]{2,0,1:T(8,128)}, u32[]{:S(2)}, u32[]{:S(2)}) collective-permute-start(f32[1024,2,128]{2,0,1:T(8,128)} %fusion), channel_id=1, source_target_pairs={{0,8},{8,0},{16,24},{24,16},{32,40},{40,32},{48,56},{56,48},{64,72... | collective-permute-start | bytes 3145736 | tf_op jit(solution)/shard_map/ppermute | solution.py:8
  282.2 115.4 %copy-start.2 = (f32[128,2]{0,1:T(2,128)S(1)}, f32[128,2]{0,1:T(2,128)}, u32[]{:S(2)}) copy-start(f32[128,2]{0,1:T(2,128)} %param.8) | copy-start | bytes 3076
  385.1 41.1 %all-to-all-start.3 = ((bf16[224,64,16]{0,2,1:T(8,128)(2,1)}), bf16[224,64,16]{0,2,1:T(8,128)(2,1)S(1)}, u32[]{:S(2)}, u32[]{:S(2)}) async-start(bf16[224,64,16]{0,2,1:T(8,128)(2,1)} %bitcast.17), calls=%async_computation.4 | async-start | bytes 1048576 | tf_op jit(solution)/shard_map/all_to_all | solution.py:78
Sparse Core Ops, SparseCore 0:
  64.5 203.7 all-gather.1
  282.3 100.6 reduce-scatter.1
where the time goes:
time: 439 us; the launch traced here: 437 us
  waiting for transfers between devices  264 us (60%)
  blocking collectives  80.5 us (18%)
  starting transfers between devices  41.9 us (10%)
  local copies, waits for them, and re-layouts  23.9 us (5%)
  between operations  14.3 us (3%)
  matrix products  7.46 us (2%)
  other arithmetic  4.43 us (1%)
    reduce_scatter x1, waiting for transfers between devices, shards(): lax.psum_scatter(lax.dot_general(weight_part, hidden, (((1,), (1,)), ((),...  101 us
    all_gather x1, waiting for transfers between devices, shards(): lax.all_gather(flat_rows, 'mp', axis=1, tiled=True)  88.9 us
    all_to_all x1, blocking collectives, shards(): lax.all_to_all(chosen, 'expert', split_axis=1, concat_axis=1, tiled=True)  80.5 us
    all_to_all x1, waiting for transfers between devices, shards(): lax.all_to_all(pieces, 'expert', split_axis=1, concat_axis=1, tiled=True)  30.3 us
    all_to_all x1, waiting for transfers between devices, shards(): lax.all_to_all(returning, 'expert', split_axis=1, concat_axis=1, tiled=True)  23.7 us
    all_to_all x1, starting transfers between devices, shards(): lax.all_to_all(outgoing, 'expert', split_axis=0, concat_axis=0, tiled=True)  22.2 us
    all_to_all x1, waiting for transfers between devices, shards(): lax.all_to_all(outgoing, 'expert', split_axis=0, concat_axis=0, tiled=True)  18.1 us
    all_to_all x1, starting transfers between devices, shards(): lax.all_to_all(returning, 'expert', split_axis=1, concat_axis=1, tiled=True)  12.3 us
  transfers between devices with their start and end apart: 6, of which 6 were waited for; matrix products, arithmetic and copies ran while one was open for 4% of the time, Pallas kernels for 0%

commit v1 on v0

v1 whole, which is shorter than its diff:
```python
import jax
import jax.numpy as jnp
from jax import lax
from jax.sharding import Mesh, PartitionSpec as P

PLANE = ("y", "x", "c")
RING = ("zh", "mp")
CAP = 16


def swap(value, axis):
    return lax.ppermute(value, axis, [(0, 1), (1, 0)])


def place_codes(routes, gate_values, owner):
    experts = owner.shape[0]
    flat = routes.T.reshape(-1)
    count = flat.shape[0]
    ids = jnp.arange(experts, dtype=jnp.int32)
    hot = (flat[:, None] == ids[None, :]).astype(jnp.bfloat16)
    at = jnp.arange(count, dtype=jnp.int32)
    earlier = (at[:, None] > at[None, :]).astype(jnp.bfloat16)
    before = jnp.dot(earlier, hot, preferred_element_type=jnp.float32)
    code = jnp.sum(hot.astype(jnp.float32) * (before + (owner * CAP).astype(jnp.float32)[None, :]), axis=1)
    return jnp.concatenate([code.reshape(routes.shape[1], -1), gate_values.T], axis=0)


def placed_rows(codes, zh):
    code = codes[:2].astype(jnp.int32)
    slot, rank = code // CAP, code % CAP
    row = jnp.where(slot % 2 == zh, (slot // 2) * (2 * CAP) + rank, -2 * CAP)
    return jnp.stack([row, row + CAP], axis=1).reshape(2, -1)


def send_rows(rows, table):
    total = 2 * CAP * lax.axis_size("y") * lax.axis_size("x")
    at = jnp.arange(total, dtype=jnp.int32)
    pick = ((rows[0][None, :] == at[:, None]) | (rows[1][None, :] == at[:, None])).astype(jnp.bfloat16)
    out = jnp.dot(pick, table, preferred_element_type=jnp.float32).astype(jnp.bfloat16)
    out = out.reshape(total // CAP, CAP, -1)
    return lax.all_to_all(out, PLANE, split_axis=0, concat_axis=0, tiled=True).reshape(total, -1)


def expert_part(rows, weights):
    half = jnp.einsum("rd,gdf->grf", rows, weights[:2], preferred_element_type=jnp.float32)
    total = half + swap(half, "c")
    hidden = (jax.nn.silu(total[0]) * total[1]).astype(jnp.bfloat16)
    return lax.dot_general(
        hidden, weights[2], (((1,), (1,)), ((), ())), preferred_element_type=jnp.float32
    ).astype(jnp.bfloat16)


def return_rows(out, codes, rows):
    total = out.shape[0]
    back = lax.all_to_all(
        out.reshape(total // CAP, CAP, -1), PLANE, split_axis=0, concat_axis=0, tiled=True
    ).reshape(total, -1)
    at = jnp.arange(total, dtype=jnp.int32)
    gate = jnp.concatenate([codes[2:4], codes[2:4]], axis=1)
    mix = sum(jnp.where(rows[k][:, None] == at[None, :], gate[k][:, None], 0.0) for k in range(2))
    high = mix.astype(jnp.bfloat16)
    low = (mix - high.astype(jnp.float32)).astype(jnp.bfloat16)
    return jnp.dot(high, back, preferred_element_type=jnp.float32) + jnp.dot(
        low, back, preferred_element_type=jnp.float32
    )


def by_columns(mixed, groups):
    parts = mixed.astype(jnp.bfloat16).reshape(2, mixed.shape[0] // 2, groups, -1)
    return jnp.transpose(parts, (2, 1, 0, 3)).reshape(groups, mixed.shape[0] // 2, -1)


def relocate(own, old_owner, new_owner):
    chips = lax.axis_size("y") * lax.axis_size("x")
    zh = lax.axis_index("zh")
    moved = new_owner != old_owner
    low = jnp.min(jnp.where(moved, old_owner, old_owner.shape[0]))
    high = jnp.max(jnp.where(moved, old_owner, -1))
    pieces = own.reshape(chips, -1, own.shape[-1])
    spread = lax.all_to_all(pieces, ("y", "x"), split_axis=0, concat_axis=0, tiled=True)
    low_piece = lax.dynamic_index_in_dim(spread, low // 2, 0, keepdims=False)
    high_piece = lax.dynamic_index_in_dim(spread, high // 2, 0, keepdims=False)
    low_here, high_here = low % 2 == zh, high % 2 == zh
    other = swap(jnp.where(low_here, low_piece, high_piece), "zh")
    to_low = jnp.where(high_here, high_piece, other)
    to_high = jnp.where(low_here, low_piece, other)
    slots = 2 * jnp.arange(chips, dtype=jnp.int32)[:, None, None] + zh
    chosen = jnp.where(slots == low, to_low[None], jnp.where(slots == high, to_high[None], spread))
    arrived = lax.all_to_all(chosen, ("y", "x"), split_axis=0, concat_axis=0, tiled=True)
    return arrived.reshape(own.shape)


def shards(tokens, routes, gate_values, expert_weights, old_owner, new_owner):
    zh, lane = lax.axis_index("zh"), lax.axis_index("mp")
    groups = lax.axis_size("mp")
    tok_rows, width = tokens.shape
    own = expert_weights[0]
    codes = place_codes(routes, gate_values, old_owner)
    other_codes = swap(codes, "zh")
    table = jnp.transpose(tokens.reshape(tok_rows, groups, 2, -1), (2, 0, 1, 3)).reshape(2 * tok_rows, -1)
    share = 2 * tok_rows // groups
    ring = lax.all_gather(lax.dynamic_slice_in_dim(table, lane * share, share, 0), RING)
    rows = placed_rows(codes, zh)
    mixed = return_rows(expert_part(send_rows(rows, table), own), codes, rows)
    mixed = by_columns(mixed, groups)

    other_table = lax.dynamic_slice_in_dim(ring, (1 - zh) * groups, groups, 0).reshape(2 * tok_rows, -1)
    other_rows = placed_rows(other_codes, zh)
    other_mixed = return_rows(expert_part(send_rows(other_rows, other_table), own), other_codes, other_rows)
    other_mixed = by_columns(other_mixed, groups)
    both = jnp.concatenate(
        [jnp.where(zh == 0, mixed, other_mixed), jnp.where(zh == 0, other_mixed, mixed)], axis=0
    )
    both, own = lax.optimization_barrier((both, own))
    out = lax.psum_scatter(both, RING, scatter_dimension=0, tiled=True)[0]
    return out, relocate(own, old_owner, new_owner)[None]


def solution(mesh):
    fine = Mesh(mesh.devices.reshape(4, 4, 2, 2, mesh.shape["mp"]), ("y", "x", "zh", "c", "mp"))
    expert = ("y", "x", "zh", "c")
    in_specs = (
        P(expert, None),
        P(expert, None),
        P(expert, None),
        P(expert, None, None, "mp"),
        P(),
        P(),
    )
    out_specs = (P(expert, "mp"), P(expert, None, None, "mp"))
    return jax.shard_map(shards, mesh=fine, in_specs=in_specs, out_specs=out_specs, check_vma=False)
```

time: 439 us -> 281 us (0.64)
  the two profiles are of different devices: /device:TPU:1 before, /device:TPU:28 now
where the time goes in v1:
time: 281 us; the launch traced here: 280 us
  waiting for transfers between devices  131 us (47%)
  starting transfers between devices  70.1 us (25%)
  blocking collectives  21.5 us (8%)
  matrix products  21.1 us (8%)
  between operations  19.5 us (7%)
  local copies, waits for them, and re-layouts  12.3 us (4%)
  other arithmetic  4.05 us (1%)
    all_gather x1, waiting for transfers between devices, shards(): lax.all_gather(lax.dynamic_slice_in_dim(table, lane * share, share, 0), R...  49.3 us
    all_to_all x2, waiting for transfers between devices, return_rows(): lax.all_to_all(out.reshape(total // CAP, CAP, -1), PLANE, split_axis=0, c...  33.3 us
    ppermute x4, starting transfers between devices, swap(): return lax.ppermute(value, axis, [(0, 1), (1, 0)])  26.2 us
    all_to_all x1, blocking collectives, relocate(): lax.all_to_all(chosen, ('y', 'x'), split_axis=0, concat_axis=0, tiled=True)  21.5 us
    all_to_all x2, starting transfers between devices, return_rows(): lax.all_to_all(out.reshape(total // CAP, CAP, -1), PLANE, split_axis=0, c...  18.3 us
    all_to_all x2, starting transfers between devices, send_rows(): lax.all_to_all(out, PLANE, split_axis=0, concat_axis=0, tiled=True)  16.8 us
    ppermute x4, waiting for transfers between devices, swap(): return lax.ppermute(value, axis, [(0, 1), (1, 0)])  16.8 us
    all_to_all x2, waiting for transfers between devices, send_rows(): lax.all_to_all(out, PLANE, split_axis=0, concat_axis=0, tiled=True)  13.5 us
  transfers between devices with their start and end apart: 11, of which 10 were waited for; matrix products, arithmetic and copies ran while one was open for 7% of the time, Pallas kernels for 0%

profile of v1, /device:TPU:28, one launch (start us, length us, event | category | flops | bytes accessed | tf_op | source)
XLA Modules:
  0.0 279.8 jit_solution(10180775529198229231)
XLA Ops:
  7.2 1.6 copy.21
  8.8 0.8 copy.22
  9.6 0.1 copy.33
  9.7 0.2 constant_dynamic-slice_fusion.1
  9.9 0.8 copy.23
  10.8 0.7 fusion.54
  11.5 0.2 fusion.3
  11.8 1.9 convolution_convert_fusion.1
  13.7 9.5 %all-to-all-start = ((bf16[32,16,1792]{2,1,0:T(8,128)(2,1)}), bf16[32,16,1792]{2,1,0:T(8,128)(2,1)S(1)}, u32[]{:S(2)}, u32[]{:S(2)}) async-start(bf16[32,16,1792]{2,1,0:T(8,128)(2,1)} %bitcast.10), calls=%async_computation | async-start | bytes 3670016 | tf_op jit(solution)/shard_map/all_to_all | solution.py:41
  23.3 13.7 %collective-permute-start.1 = (f32[4,128]{1,0:T(4,128)S(1)}, f32[4,128]{1,0:T(4,128)S(1)}, u32[]{:S(2)}, u32[]{:S(2)}) collective-permute-start(f32[4,128]{1,0:T(4,128)S(1)} %pad_maximum_fusion.1), channel_id=1, source_target_pairs={{0,16},{16,0},{1,17},{17,1},{2,18},{18,2},{3,19},{19,3},{4,20},{20... | collective-permute-start | bytes 6152 | tf_op jit(solution)/shard_map/ppermute | solution.py:12
  36.9 1.7 collective-permute-done.1
  38.6 49.3 %all-gather.3.cloned.1.call-done = bf16[512,1792]{1,0:T(8,128)(2,1)} async-done(((bf16[32,1792]{1,0:T(8,128)(2,1)}), bf16[512,1792]{1,0:T(8,128)(2,1)}) %all-gather.3.cloned.1.call-update) | async-done | bytes 1835024 | tf_op jit(solution)/shard_map/all_gather | solution.py:102
  88.0 1.2 constant_dynamic-slice_fusion
  89.2 1.9 convolution_convert_fusion
  91.1 7.3 %all-to-all-start.2 = ((bf16[32,16,1792]{2,1,0:T(8,128)(2,1)}), bf16[32,16,1792]{2,1,0:T(8,128)(2,1)}, u32[]{:S(2)}, u32[]{:S(2)}) async-start(bf16[32,16,1792]{2,1,0:T(8,128)(2,1)} %bitcast.28), calls=%async_computation.2 | async-start | bytes 3670016 | tf_op jit(solution)/shard_map/all_to_all | solution.py:41
  98.5 1.8 convolution_bitcast_fusion.1
  100.3 2.1 collective-permute-start
  102.4 1.7 collective-permute-done
  104.2 3.0 %convolution_convert_fusion.3 = bf16[512,1792]{1,0:T(8,128)(2,1)} fusion(bf16[1,3,1792,128]{3,2,1,0:T(8,128)(2,1)} %param.9, f32[2,512,128]{2,1,0:T(8,128)S(1)} %add.176), kind=kOutput, calls=%fused_computation.3 | convolution fusion | flops 236191744 | bytes 2818048 | tf_op jit(solution)/shard_map/dot_general | solution.py:48
  107.1 13.5 %all-to-all-done.2 = bf16[32,16,1792]{2,1,0:T(8,128)(2,1)} async-done(((bf16[32,16,1792]{2,1,0:T(8,128)(2,1)}), bf16[32,16,1792]{2,1,0:T(8,128)(2,1)}, u32[]{:S(2)}, u32[]{:S(2)}) %all-to-all-start.2) | async-done | bytes 1835040 | tf_op jit(solution)/shard_map/all_to_all | solution.py:41
  120.6 8.8 %all-to-all-start.1 = ((bf16[32,16,1792]{2,1,0:T(8,128)(2,1)}), bf16[32,16,1792]{2,1,0:T(8,128)(2,1)S(1)}, u32[]{:S(2)}, u32[]{:S(2)}) async-start(bf16[32,16,1792]{2,1,0:T(8,128)(2,1)} %bitcast.90), calls=%async_computation.1 | async-start | bytes 3670016 | tf_op jit(solution)/shard_map/all_to_all | solution.py:55
  129.4 2.4 convolution_bitcast_fusion
  131.8 2.1 collective-permute-start.2
  133.9 1.7 collective-permute-done.2
  135.7 2.9 %convolution_convert_fusion.2 = bf16[512,1792]{1,0:T(8,128)(2,1)} fusion(bf16[1,3,1792,128]{3,2,1,0:T(8,128)(2,1)} %param.9, f32[2,512,128]{2,1,0:T(8,128)S(1)} %add.186), kind=kOutput, calls=%fused_computation.2 | convolution fusion | flops 236191744 | bytes 2818048 | tf_op jit(solution)/shard_map/dot_general | solution.py:48
  138.6 12.9 %all-to-all-done.1 = bf16[32,16,1792]{2,1,0:T(8,128)(2,1)S(1)} async-done(((bf16[32,16,1792]{2,1,0:T(8,128)(2,1)}), bf16[32,16,1792]{2,1,0:T(8,128)(2,1)S(1)}, u32[]{:S(2)}, u32[]{:S(2)}) %all-to-all-start.1) | async-done | bytes 1835040 | tf_op jit(solution)/shard_map/all_to_all | solution.py:55
  151.6 9.5 %all-to-all-start.3 = ((bf16[32,16,1792]{2,1,0:T(8,128)(2,1)}), bf16[32,16,1792]{2,1,0:T(8,128)(2,1)}, u32[]{:S(2)}, u32[]{:S(2)}) async-start(bf16[32,16,1792]{2,1,0:T(8,128)(2,1)} %bitcast.89), calls=%async_computation.3 | async-start | bytes 3670016 | tf_op jit(solution)/shard_map/all_to_all | solution.py:55
  161.0 0.2 reduce-scatter.2.cloned.1.call-start
  161.3 0.8 fusion.35
  162.1 0.8 fusion
  162.8 20.4 %all-to-all-done.3 = bf16[32,16,1792]{2,1,0:T(8,128)(2,1)} async-done(((bf16[32,16,1792]{2,1,0:T(8,128)(2,1)}), bf16[32,16,1792]{2,1,0:T(8,128)(2,1)}, u32[]{:S(2)}, u32[]{:S(2)}) %all-to-all-start.3) | async-done | bytes 1835040 | tf_op jit(solution)/shard_map/all_to_all | solution.py:55
  183.2 2.2 fusion.38
  185.5 3.2 %broadcast_select_fusion.1 = (bf16[256,1792]{1,0:T(8,128)(2,1)}, bf16[256,1792]{1,0:T(8,128)(2,1)S(1)}) fusion(bf16[256,1792]{1,0:T(8,128)(2,1)S(1)} %fusion, pred[]{:T(512)S(6)} %eq.190, f32[256,1792]{1,0:T(8,128)S(1)} %fusion.38, bf16[512,1792]{1,0:T(8,128)(2,1)} %bitcast.34, f32[256]{0:T(256)S(1)} %bitcast.110, s32[256]{0:T(256)S(1)} %bitcast.106, ...), kind=kOutput, calls=%fused_computation.19 | convolution fusion | flops 472776704 | bytes 6426625 | tf_op jit(solution)/shard_map/dot_general | solution.py:63
  188.7 1.5 reshape.273
  190.2 1.1 copy.29
  191.4 2.7 reshape.272
  194.1 1.1 copy.28
  195.1 0.1 copy.25
  195.2 1.4 pad_maximum_fusion
  196.7 8.6 %all-to-all-start.4 = ((bf16[16,336,128]{2,1,0:T(8,128)(2,1)}), bf16[16,336,128]{2,1,0:T(8,128)(2,1)S(1)}, u32[]{:S(2)}, u32[]{:S(2)}) async-start(bf16[16,336,128]{2,1,0:T(8,128)(2,1)} %bitcast.41), calls=%async_computation.5 | async-start | bytes 2752512 | tf_op jit(solution)/shard_map/all_to_all | solution.py:80
  210.4 11.3 %all-to-all-done.4 = bf16[16,336,128]{2,1,0:T(8,128)(2,1)S(1)} async-done(((bf16[16,336,128]{2,1,0:T(8,128)(2,1)}), bf16[16,336,128]{2,1,0:T(8,128)(2,1)S(1)}, u32[]{:S(2)}, u32[]{:S(2)}) %all-to-all-start.4) | async-done | bytes 1376288 | tf_op jit(solution)/shard_map/all_to_all | solution.py:80
  221.7 8.4 %collective-permute-start.3 = (bf16[336,128]{1,0:T(8,128)(2,1)S(1)}, bf16[336,128]{1,0:T(8,128)(2,1)S(1)}, u32[]{:S(2)}, u32[]{:S(2)}) collective-permute-start(bf16[336,128]{1,0:T(8,128)(2,1)S(1)} %bitcast_select_fusion.1), channel_id=1, source_target_pairs={{0,16},{16,0},{1,17},{17,1},{2,18},{18,2},{3,19},{19,3},{4,20},{20... | collective-permute-start | bytes 258056 | tf_op jit(solution)/shard_map/ppermute | solution.py:12
  230.1 1.3 fusion.56
  231.4 11.6 %collective-permute-done.3 = bf16[336,128]{1,0:T(8,128)(2,1)S(1)} collective-permute-done((bf16[336,128]{1,0:T(8,128)(2,1)S(1)}, bf16[336,128]{1,0:T(8,128)(2,1)S(1)}, u32[]{:S(2)}, u32[]{:S(2)}) %collective-permute-start.3) | collective-permute-done | bytes 86048 | tf_op jit(solution)/shard_map/ppermute | solution.py:12
  243.0 0.3 select_select_fusion
  243.4 21.5 %all_to_all.30 = bf16[16,336,128]{2,1,0:T(8,128)(2,1)S(1)} all-to-all(bf16[16,336,128]{2,1,0:T(8,128)(2,1)S(1)} %select_select_fusion), channel_id=1, replica_groups=mesh['y'=4,'x'=4,'zh'=2,'c'=2,'mp'=8] {'y','x'}, dimensions={0} | all-to-all | bytes 2752512 | tf_op jit(solution)/shard_map/all_to_all | solution.py:89
  264.9 7.0 %reduce-scatter.2.cloned.1.call-done = bf16[1,128,448]{1,2,0:T(8,128)(2,1)} async-done(((bf16[16,128,448]{1,2,0:T(8,128)(2,1)}), bf16[1,128,448]{1,2,0:T(8,128)(2,1)}) %reduce-scatter.2.cloned.1.call-update) | async-done | bytes 114704 | tf_op jit(solution)/shard_map/reduce_scatter | solution.py:115
  271.9 1.1 copy.35
  (26 shorter events, 0.5 us)
Async XLA Ops:
  7.2 80.8 %all-gather.3.cloned.1.call-start = ((), (), s32[]{:S(2)}) async-start(), calls=%async_computation.8 | async-start | bytes 1949696 | tf_op jit(solution)/shard_map/all_gather | solution.py:102
  9.5 1.2 copy-start.1
  9.6 1.2 copy-start.2
  9.6 2.0 copy-start.3
  13.7 9.5 %copy-start = (f32[128,2]{0,1:T(2,128)S(1)}, f32[128,2]{0,1:T(2,128)}, u32[]{:S(2)}) copy-start(f32[128,2]{0,1:T(2,128)} %param.8) | copy-start | bytes 3076
  13.7 77.4 %all-to-all-start = ((bf16[32,16,1792]{2,1,0:T(8,128)(2,1)}), bf16[32,16,1792]{2,1,0:T(8,128)(2,1)S(1)}, u32[]{:S(2)}, u32[]{:S(2)}) async-start(bf16[32,16,1792]{2,1,0:T(8,128)(2,1)} %bitcast.10), calls=%async_computation | async-start | bytes 3670016 | tf_op jit(solution)/shard_map/all_to_all | solution.py:41
  23.3 15.3 %collective-permute-start.1 = (f32[4,128]{1,0:T(4,128)S(1)}, f32[4,128]{1,0:T(4,128)S(1)}, u32[]{:S(2)}, u32[]{:S(2)}) collective-permute-start(f32[4,128]{1,0:T(4,128)S(1)} %pad_maximum_fusion.1), channel_id=1, source_target_pairs={{0,16},{16,0},{1,17},{17,1},{2,18},{18,2},{3,19},{19,3},{4,20},{20... | collective-permute-start | bytes 6152 | tf_op jit(solution)/shard_map/ppermute | solution.py:12
  91.1 29.5 %all-to-all-start.2 = ((bf16[32,16,1792]{2,1,0:T(8,128)(2,1)}), bf16[32,16,1792]{2,1,0:T(8,128)(2,1)}, u32[]{:S(2)}, u32[]{:S(2)}) async-start(bf16[32,16,1792]{2,1,0:T(8,128)(2,1)} %bitcast.28), calls=%async_computation.2 | async-start | bytes 3670016 | tf_op jit(solution)/shard_map/all_to_all | solution.py:41
  100.3 3.8 %collective-permute-start = (f32[2,512,128]{2,1,0:T(8,128)S(1)}, f32[2,512,128]{2,1,0:T(8,128)S(1)}, u32[]{:S(2)}, u32[]{:S(2)}) collective-permute-start(f32[2,512,128]{2,1,0:T(8,128)S(1)} %convolution_bitcast_fusion.1), channel_id=1, source_target_pairs={{0,8},{8,0},{1,9},{9,1},{2,10},{10,2},{3,11},{11,3},{4,12},{12,4},... | collective-permute-start | bytes 1572872 | tf_op jit(solution)/shard_map/ppermute | solution.py:12
  120.6 30.9 %all-to-all-start.1 = ((bf16[32,16,1792]{2,1,0:T(8,128)(2,1)}), bf16[32,16,1792]{2,1,0:T(8,128)(2,1)S(1)}, u32[]{:S(2)}, u32[]{:S(2)}) async-start(bf16[32,16,1792]{2,1,0:T(8,128)(2,1)} %bitcast.90), calls=%async_computation.1 | async-start | bytes 3670016 | tf_op jit(solution)/shard_map/all_to_all | solution.py:55
  131.8 3.8 %collective-permute-start.2 = (f32[2,512,128]{2,1,0:T(8,128)S(1)}, f32[2,512,128]{2,1,0:T(8,128)S(1)}, u32[]{:S(2)}, u32[]{:S(2)}) collective-permute-start(f32[2,512,128]{2,1,0:T(8,128)S(1)} %convolution_bitcast_fusion), channel_id=1, source_target_pairs={{0,8},{8,0},{1,9},{9,1},{2,10},{10,2},{3,11},{11,3},{4,12},{12,4},... | collective-permute-start | bytes 1572872 | tf_op jit(solution)/shard_map/ppermute | solution.py:12
  151.6 31.7 %all-to-all-start.3 = ((bf16[32,16,1792]{2,1,0:T(8,128)(2,1)}), bf16[32,16,1792]{2,1,0:T(8,128)(2,1)}, u32[]{:S(2)}, u32[]{:S(2)}) async-start(bf16[32,16,1792]{2,1,0:T(8,128)(2,1)} %bitcast.89), calls=%async_computation.3 | async-start | bytes 3670016 | tf_op jit(solution)/shard_map/all_to_all | solution.py:55
  161.0 110.8 %reduce-scatter.2.cloned.1.call-start = ((), (), s32[]{:S(2)}) async-start(), calls=%async_computation.7 | async-start | bytes 1949696 | tf_op jit(solution)/shard_map/reduce_scatter | solution.py:115
  196.7 25.0 %all-to-all-start.4 = ((bf16[16,336,128]{2,1,0:T(8,128)(2,1)}), bf16[16,336,128]{2,1,0:T(8,128)(2,1)S(1)}, u32[]{:S(2)}, u32[]{:S(2)}) async-start(bf16[16,336,128]{2,1,0:T(8,128)(2,1)} %bitcast.41), calls=%async_computation.5 | async-start | bytes 2752512 | tf_op jit(solution)/shard_map/all_to_all | solution.py:80
  221.7 21.3 %collective-permute-start.3 = (bf16[336,128]{1,0:T(8,128)(2,1)S(1)}, bf16[336,128]{1,0:T(8,128)(2,1)S(1)}, u32[]{:S(2)}, u32[]{:S(2)}) collective-permute-start(bf16[336,128]{1,0:T(8,128)(2,1)S(1)} %bitcast_select_fusion.1), channel_id=1, source_target_pairs={{0,16},{16,0},{1,17},{17,1},{2,18},{18,2},{3,19},{19,3},{4,20},{20... | collective-permute-start | bytes 258056 | tf_op jit(solution)/shard_map/ppermute | solution.py:12
Sparse Core Ops, SparseCore 0:
  10.9 77.0 all-gather.2
  196.8 75.0 reduce-scatter.1

commit v2 on v1

v2 whole, which is shorter than its diff:
```python
import jax
import jax.numpy as jnp
from jax import lax
from jax.sharding import Mesh, PartitionSpec as P

PLANE = ("y", "x", "c")
NEAR = ("mb", "mc")
CAP = 16


def swap(value, axis):
    return lax.ppermute(value, axis, [(0, 1), (1, 0)])


def place_codes(routes, gate_values, owner):
    experts = owner.shape[0]
    flat = routes.T.reshape(-1)
    count = flat.shape[0]
    ids = jnp.arange(experts, dtype=jnp.int32)
    hot = (flat[:, None] == ids[None, :]).astype(jnp.bfloat16)
    at = jnp.arange(count, dtype=jnp.int32)
    earlier = (at[:, None] > at[None, :]).astype(jnp.bfloat16)
    before = jnp.dot(earlier, hot, preferred_element_type=jnp.float32)
    code = jnp.sum(hot.astype(jnp.float32) * (before + (owner * CAP).astype(jnp.float32)[None, :]), axis=1)
    return jnp.concatenate([code.reshape(routes.shape[1], -1), gate_values.T], axis=0)


def placed_rows(codes, zh):
    code = codes[:2].astype(jnp.int32)
    slot, rank = code // CAP, code % CAP
    row = jnp.where(slot % 2 == zh, (slot // 2) * (2 * CAP) + rank, -2 * CAP)
    return jnp.stack([row, row + CAP], axis=1).reshape(2, -1)


def plane_rows():
    return 2 * CAP * lax.axis_size("y") * lax.axis_size("x")


def gather_rows(rows, table):
    at = jnp.arange(plane_rows(), dtype=jnp.int32)
    pick = ((rows[0][None, :] == at[:, None]) | (rows[1][None, :] == at[:, None])).astype(jnp.bfloat16)
    return jnp.dot(pick, table, preferred_element_type=jnp.float32).astype(jnp.bfloat16)


def exchange(rows, axes=PLANE):
    blocks = rows.reshape((lax.axis_size(axes), -1, rows.shape[-1]))
    return lax.all_to_all(blocks, axes, split_axis=0, concat_axis=0, tiled=True).reshape(rows.shape)


def expert_part(rows, weights):
    half = jnp.einsum("rd,gdf->grf", rows, weights[:2], preferred_element_type=jnp.float32)
    total = half + swap(half, "c")
    hidden = (jax.nn.silu(total[0]) * total[1]).astype(jnp.bfloat16)
    return lax.dot_general(
        hidden, weights[2], (((1,), (1,)), ((), ())), preferred_element_type=jnp.float32
    ).astype(jnp.bfloat16)


def weighted(back, codes, rows):
    at = jnp.arange(back.shape[0], dtype=jnp.int32)
    gate = jnp.concatenate([codes[2:4], codes[2:4]], axis=1)
    mix = sum(jnp.where(rows[k][:, None] == at[None, :], gate[k][:, None], 0.0) for k in range(2))
    high = mix.astype(jnp.bfloat16)
    low = (mix - high.astype(jnp.float32)).astype(jnp.bfloat16)
    return jnp.dot(high, back, preferred_element_type=jnp.float32) + jnp.dot(
        low, back, preferred_element_type=jnp.float32
    )


def by_columns(mixed, near):
    tok_rows = mixed.shape[0] // 2
    parts = mixed.astype(jnp.bfloat16).reshape(2, tok_rows, 2, near, -1)
    return jnp.transpose(parts, (3, 2, 1, 0, 4)).reshape(near, 2, tok_rows, -1)


def near_sum(parts, place):
    total = lax.dynamic_index_in_dim(parts, place, 0, keepdims=False).astype(jnp.float32)
    count = parts.shape[0]
    for step in range(1, count):
        block = lax.dynamic_index_in_dim(parts, place ^ step, 0, keepdims=False)
        total += lax.ppermute(block, NEAR, [(i, i ^ step) for i in range(count)]).astype(jnp.float32)
    return total


def after(value, *others):
    return lax.optimization_barrier((value, *others))[0]


def pick_pieces(spread, old_owner, new_owner, zh):
    moved = new_owner != old_owner
    low = jnp.min(jnp.where(moved, old_owner, old_owner.shape[0]))
    high = jnp.max(jnp.where(moved, old_owner, -1))
    low_piece = lax.dynamic_index_in_dim(spread, low >> 1, 0, keepdims=False)
    high_piece = lax.dynamic_index_in_dim(spread, high >> 1, 0, keepdims=False)
    low_here, high_here = (low & 1) == zh, (high & 1) == zh
    other = swap(jnp.where(low_here, low_piece, high_piece), "zh")
    to_low = jnp.where(high_here, high_piece, other)
    to_high = jnp.where(low_here, low_piece, other)
    slots = 2 * jnp.arange(spread.shape[0], dtype=jnp.int32)[:, None, None] + zh
    return jnp.where(slots == low, to_low[None], jnp.where(slots == high, to_high[None], spread))


def shards(tokens, routes, gate_values, expert_weights, old_owner, new_owner):
    zh, far, place = lax.axis_index("zh"), lax.axis_index("ma"), lax.axis_index(NEAR)
    near = lax.axis_size(NEAR)
    tok_rows = tokens.shape[0]
    own = expert_weights[0]
    table = jnp.transpose(tokens.reshape(tok_rows, 2 * near, 2, -1), (2, 0, 1, 3)).reshape(2 * tok_rows, -1)
    share = 2 * tok_rows // near
    quarter = swap(lax.dynamic_slice_in_dim(table, place * share, share, 0), "zh")
    codes = place_codes(routes, gate_values, old_owner)
    other_codes = swap(codes, "zh")
    other_table = lax.all_gather(quarter, NEAR, tiled=True)

    chips = lax.axis_size("y") * lax.axis_size("x")
    pieces = own.reshape(chips, -1, own.shape[-1])
    spread = lax.all_to_all(pieces, ("y", "x"), split_axis=0, concat_axis=0, tiled=True)
    rows = placed_rows(codes, zh)
    sent = exchange(after(gather_rows(rows, table), spread, quarter, other_codes))
    other_rows = placed_rows(other_codes, zh)
    other_sent = exchange(after(gather_rows(other_rows, other_table), sent))
    back = exchange(after(expert_part(sent, own), other_sent))
    other_back = exchange(after(expert_part(other_sent, own), back))

    parts = by_columns(weighted(back, codes, rows), near)
    kept = lax.psum_scatter(parts, NEAR, scatter_dimension=0, tiled=True)[0]
    other_parts = by_columns(weighted(other_back, other_codes, other_rows), near)
    chosen = pick_pieces(spread, old_owner, new_owner, zh)
    arrived = lax.all_to_all(after(chosen, other_back), ("y", "x"), split_axis=0, concat_axis=0, tiled=True)
    other_kept = near_sum(other_parts, place).astype(jnp.bfloat16)

    def of(value, index):
        return lax.dynamic_index_in_dim(value, index, 0, keepdims=False)

    total = of(kept, far).astype(jnp.float32)
    total += swap(of(kept, 1 - far), "ma").astype(jnp.float32)
    total += swap(of(other_kept, far), "zh").astype(jnp.float32)
    total += lax.ppermute(of(other_kept, 1 - far), ("zh", "ma"), [(i, i ^ 3) for i in range(4)]).astype(jnp.float32)
    return total.astype(jnp.bfloat16), arrived.reshape(expert_weights.shape)


def solution(mesh):
    fine = Mesh(mesh.devices.reshape(4, 4, 2, 2, 2, 2, 2), ("y", "x", "zh", "c", "ma", "mb", "mc"))
    expert, mp = ("y", "x", "zh", "c"), ("ma", "mb", "mc")
    in_specs = (
        P(expert, None),
        P(expert, None),
        P(expert, None),
        P(expert, None, None, mp),
        P(),
        P(),
    )
    out_specs = (P(expert, mp), P(expert, None, None, mp))
    return jax.shard_map(shards, mesh=fine, in_specs=in_specs, out_specs=out_specs, check_vma=False)
```

time: 281 us -> 307 us (1.093)
  the two profiles are of different devices: /device:TPU:28 before, /device:TPU:1 now
where the time goes in v2:
time: 307 us; the launch traced here: 302 us
  starting transfers between devices  118 us (38%)
  waiting for transfers between devices  75.8 us (25%)
  blocking collectives  41.1 us (13%)
  local copies, waits for them, and re-layouts  24.3 us (8%)
  matrix products  19.9 us (6%)
  between operations  17.2 us (6%)
  other arithmetic  5.46 us (2%)
    ppermute x7, starting transfers between devices, swap(): return lax.ppermute(value, axis, [(0, 1), (1, 0)])  52.5 us
    all_gather x1, blocking collectives, shards(): other_table = lax.all_gather(quarter, NEAR, tiled=True)  41.1 us
    all_to_all x4, waiting for transfers between devices, exchange(): lax.all_to_all(blocks, axes, split_axis=0, concat_axis=0, tiled=True)  32.8 us
    all_to_all x4, starting transfers between devices, exchange(): lax.all_to_all(blocks, axes, split_axis=0, concat_axis=0, tiled=True)  31.2 us
    ppermute x3, starting transfers between devices, near_sum(): lax.ppermute(block, NEAR, [(i, i ^ step) for i in range(count)])  17.7 us
    ppermute x7, waiting for transfers between devices, swap(): return lax.ppermute(value, axis, [(0, 1), (1, 0)])  17.4 us
    reshape x4, local copies, waits for them, and re-layouts, by_columns(): parts = mixed.astype(jnp.bfloat16).reshape(2, tok_rows, 2, near, -1)  14 us
    ppermute x3, waiting for transfers between devices, near_sum(): lax.ppermute(block, NEAR, [(i, i ^ step) for i in range(count)])  13.2 us
  transfers between devices with their start and end apart: 18, of which 9 were waited for; matrix products, arithmetic and copies ran while one was open for 16% of the time, Pallas kernels for 0%

profile of v2, /device:TPU:1, one launch (start us, length us, event | category | flops | bytes accessed | tf_op | source)
XLA Modules:
  0.0 301.9 jit_solution(8555214055884387268)
XLA Ops:
  7.2 7.7 %all-to-all-start = ((bf16[16,336,128]{2,1,0:T(8,128)(2,1)}), bf16[16,336,128]{2,1,0:T(8,128)(2,1)S(1)}, u32[]{:S(2)}, u32[]{:S(2)}) async-start(bf16[16,336,128]{2,1,0:T(8,128)(2,1)} %bitcast.109), calls=%async_computation | async-start | bytes 2752512 | tf_op jit(solution)/shard_map/all_to_all | solution.py:117
  17.5 15.4 %collective-permute-start = (bf16[64,1792]{0,1:T(8,128)(2,1)}, bf16[64,1792]{0,1:T(8,128)(2,1)S(1)}, u32[]{:S(2)}, u32[]{:S(2)}) collective-permute-start(bf16[64,1792]{0,1:T(8,128)(2,1)} %constant_dynamic-slice_fusion), channel_id=1, source_target_pairs={{0,16},{16,0},{1,17},{17,1},{2,18},{18,2},{3,19},{19,3},{4,20},{20... | collective-permute-start | bytes 688136 | tf_op jit(solution)/shard_map/ppermute | solution.py:12
  33.9 1.9 collective-permute-start.1
  35.9 2.0 convolution_convert_fusion.1
  37.8 9.5 %collective-permute-done.1 = f32[4,128]{1,0:T(4,128)S(1)} collective-permute-done((f32[4,128]{1,0:T(4,128)S(1)}, f32[4,128]{1,0:T(4,128)S(1)}, u32[]{:S(2)}, u32[]{:S(2)}) %collective-permute-start.1) | collective-permute-done | bytes 2080 | tf_op jit(solution)/shard_map/ppermute | solution.py:12
  47.3 9.6 %all-to-all-start.1 = ((bf16[32,16,1792]{2,1,0:T(8,128)(2,1)}), bf16[32,16,1792]{2,1,0:T(8,128)(2,1)}, u32[]{:S(2)}, u32[]{:S(2)}) async-start(bf16[32,16,1792]{2,1,0:T(8,128)(2,1)} %bitcast.107), calls=%async_computation.1 | async-start | bytes 3670016 | tf_op jit(solution)/shard_map/all_to_all | solution.py:47
  57.2 41.1 %all_gather.3 = bf16[256,1792]{1,0:T(8,128)(2,1)S(1)} all-gather(bf16[64,1792]{1,0:T(8,128)(2,1)S(1)} %copy.22), channel_id=1, replica_groups=mesh['y'=4,'x'=4,'zh'=2,'c'=2,'ma'=2,'mb'=2,'mc'=2] {'mb','mc'}, dimensions={0}, use_global_device_ids=true | all-gather | bytes 1146880 | tf_op jit(solution)/shard_map/all_gather | solution.py:113
  98.3 1.9 convolution_convert_fusion
  100.2 9.8 %all-to-all-start.2 = ((bf16[32,16,1792]{2,1,0:T(8,128)(2,1)}), bf16[32,16,1792]{2,1,0:T(8,128)(2,1)}, u32[]{:S(2)}, u32[]{:S(2)}) async-start(bf16[32,16,1792]{2,1,0:T(8,128)(2,1)} %bitcast.23), calls=%async_computation.2 | async-start | bytes 3670016 | tf_op jit(solution)/shard_map/all_to_all | solution.py:47
  110.0 2.1 convolution_bitcast_fusion.1
  112.1 2.2 collective-permute-start.2
  114.4 1.6 collective-permute-done.2
  116.0 1.9 convolution_convert_fusion.3
  117.9 17.0 %all-to-all-done.2 = bf16[32,16,1792]{2,1,0:T(8,128)(2,1)} async-done(((bf16[32,16,1792]{2,1,0:T(8,128)(2,1)}), bf16[32,16,1792]{2,1,0:T(8,128)(2,1)}, u32[]{:S(2)}, u32[]{:S(2)}) %all-to-all-start.2) | async-done | bytes 1835040 | tf_op jit(solution)/shard_map/all_to_all | solution.py:47
  134.9 5.9 %all-to-all-start.3 = ((bf16[32,16,1792]{2,1,0:T(8,128)(2,1)}), bf16[32,16,1792]{2,1,0:T(8,128)(2,1)S(1)}, u32[]{:S(2)}, u32[]{:S(2)}) async-start(bf16[32,16,1792]{2,1,0:T(8,128)(2,1)} %bitcast.106), calls=%async_computation.3 | async-start | bytes 3670016 | tf_op jit(solution)/shard_map/all_to_all | solution.py:47
  140.9 2.4 convolution_bitcast_fusion
  143.2 2.3 collective-permute-start.4
  145.5 1.5 collective-permute-done.4
  147.1 2.9 convolution_convert_fusion.2
  150.1 15.8 %all-to-all-done.3 = bf16[32,16,1792]{2,1,0:T(8,128)(2,1)S(1)} async-done(((bf16[32,16,1792]{2,1,0:T(8,128)(2,1)}), bf16[32,16,1792]{2,1,0:T(8,128)(2,1)S(1)}, u32[]{:S(2)}, u32[]{:S(2)}) %all-to-all-start.3) | async-done | bytes 1835040 | tf_op jit(solution)/shard_map/all_to_all | solution.py:47
  165.8 1.2 copy-done
  167.1 5.9 %all-to-all-start.4 = ((bf16[32,16,1792]{2,1,0:T(8,128)(2,1)}), bf16[32,16,1792]{2,1,0:T(8,128)(2,1)S(1)}, u32[]{:S(2)}, u32[]{:S(2)}) async-start(bf16[32,16,1792]{2,1,0:T(8,128)(2,1)} %bitcast.105), calls=%async_computation.5 | async-start | bytes 3670016 | tf_op jit(solution)/shard_map/all_to_all | solution.py:47
  173.3 2.4 fusion.38
  175.7 1.7 fusion
  177.4 4.3 %reshape.281 = bf16[2,128,2,4,224]{4,3,2,1,0:T(4,128)(2,1)} reshape(bf16[256,1792]{1,0:T(8,128)(2,1)} %fusion) | data formatting | bytes 1835008 | tf_op jit(solution)/shard_map/reshape | solution.py:72
  181.7 3.9 %copy.27 = bf16[2,128,2,4,224]{1,0,4,3,2:T(2,128)(2,1)} copy(bf16[2,128,2,4,224]{4,3,2,1,0:T(4,128)(2,1)} %reshape.281) | data formatting | bytes 1835008 | tf_op jit(solution)/shard_map/reshape | solution.py:72
  185.5 2.2 copy.24
  190.5 1.3 fusion.62
  191.9 11.9 %collective-permute-start.10 = (bf16[336,128]{1,0:T(8,128)(2,1)S(1)}, bf16[336,128]{1,0:T(8,128)(2,1)S(1)}, u32[]{:S(2)}, u32[]{:S(2)}) collective-permute-start(bf16[336,128]{1,0:T(8,128)(2,1)S(1)} %bitcast_select_fusion.1), channel_id=1, source_target_pairs={{0,16},{16,0},{1,17},{17,1},{2,18},{18,2},{3,19},{19,3},{4,20},{20... | collective-permute-start | bytes 258056 | tf_op jit(solution)/shard_map/ppermute | solution.py:12
  203.8 2.5 collective-permute-done.10
  206.3 1.3 select_select_fusion
  207.6 6.8 %all-to-all-start.5 = ((bf16[16,336,128]{2,1,0:T(8,128)(2,1)}), bf16[16,336,128]{2,1,0:T(8,128)(2,1)S(1)}, u32[]{:S(2)}, u32[]{:S(2)}) async-start(bf16[16,336,128]{2,1,0:T(8,128)(2,1)} %select_select_fusion), calls=%async_computation.6 | async-start | bytes 2752512 | tf_op jit(solution)/shard_map/all_to_all | solution.py:129
  215.2 1.7 fusion.1
  216.9 3.5 %reshape.282 = bf16[2,128,2,4,224]{4,3,2,1,0:T(4,128)(2,1)S(1)} reshape(bf16[256,1792]{1,0:T(8,128)(2,1)} %fusion.1) | data formatting | bytes 1835008 | tf_op jit(solution)/shard_map/reshape | solution.py:72
  220.4 2.3 copy.28
  222.7 1.3 copy.26
  224.8 11.8 %collective-permute-start.5 = (bf16[2,128,448]{1,2,0:T(8,128)(2,1)}, bf16[2,128,448]{1,2,0:T(8,128)(2,1)S(1)}, u32[]{:S(2)}, u32[]{:S(2)}) collective-permute-start(bf16[2,128,448]{1,2,0:T(8,128)(2,1)} %get-tuple-element.20), channel_id=1, source_target_pairs={{0,1},{1,0},{2,3},{3,2},{4,5},{5,4},{6,7},{7,6},{8,9},{9,8},{10,11... | collective-permute-start | bytes 688136 | tf_op jit(solution)/shard_map/ppermute | solution.py:81
  236.6 1.9 collective-permute-start.6
  238.5 4.0 %collective-permute-start.7 = (bf16[2,128,448]{1,2,0:T(8,128)(2,1)S(1)}, bf16[2,128,448]{1,2,0:T(8,128)(2,1)}, u32[]{:S(2)}, u32[]{:S(2)}) collective-permute-start(bf16[2,128,448]{1,2,0:T(8,128)(2,1)S(1)} %get-tuple-element.21), channel_id=1, source_target_pairs={{0,3},{1,2},{2,1},{3,0},{4,7},{5,6},{6,5},{7,4},{8,11},{9,10},{10,... | collective-permute-start | bytes 688136 | tf_op jit(solution)/shard_map/ppermute | solution.py:81
  242.6 1.0 dynamic-slice_bitcast_fusion.5
  243.5 3.0 collective-permute-start.3
  246.5 13.2 %collective-permute-done.6 = bf16[2,128,448]{1,2,0:T(8,128)(2,1)S(1)} collective-permute-done((bf16[2,128,448]{1,2,0:T(8,128)(2,1)S(1)}, bf16[2,128,448]{1,2,0:T(8,128)(2,1)S(1)}, u32[]{:S(2)}, u32[]{:S(2)}) %collective-permute-start.6) | collective-permute-done | bytes 229408 | tf_op jit(solution)/shard_map/ppermute | solution.py:81
  259.8 1.1 fusion.16
  260.9 15.8 %collective-permute-start.8 = (bf16[128,448]{0,1:T(8,128)(2,1)S(1)}, bf16[128,448]{0,1:T(8,128)(2,1)S(1)}, u32[]{:S(2)}, u32[]{:S(2)}) collective-permute-start(bf16[128,448]{0,1:T(8,128)(2,1)S(1)} %get-tuple-element.23), channel_id=1, source_target_pairs={{0,16},{16,0},{1,17},{17,1},{2,18},{18,2},{3,19},{19,3},{4,20},{20... | collective-permute-start | bytes 344072 | tf_op jit(solution)/shard_map/ppermute | solution.py:12
  276.7 1.9 collective-permute-start.9
  278.6 2.2 collective-permute-done.8
  280.9 12.4 %collective-permute-done.9 = bf16[128,448]{0,1:T(8,128)(2,1)S(1)} collective-permute-done((bf16[128,448]{0,1:T(8,128)(2,1)S(1)}, bf16[128,448]{0,1:T(8,128)(2,1)S(1)}, u32[]{:S(2)}, u32[]{:S(2)}) %collective-permute-start.9) | collective-permute-done | bytes 114720 | tf_op jit(solution)/shard_map/ppermute | solution.py:138
  294.0 1.1 copy.34
  (52 shorter events, 6.4 us)
Async XLA Ops:
  7.2 7.8 %copy-start.3 = (bf16[128,3584]{1,0:T(8,128)(2,1)S(1)}, bf16[128,3584]{1,0:T(8,128)(2,1)}, u32[]{:S(2)}) copy-start(bf16[128,3584]{1,0:T(8,128)(2,1)} %param.6) | copy-start | bytes 2752516
  7.2 40.2 %all-to-all-start = ((bf16[16,336,128]{2,1,0:T(8,128)(2,1)}), bf16[16,336,128]{2,1,0:T(8,128)(2,1)S(1)}, u32[]{:S(2)}, u32[]{:S(2)}) async-start(bf16[16,336,128]{2,1,0:T(8,128)(2,1)} %bitcast.109), calls=%async_computation | async-start | bytes 2752512 | tf_op jit(solution)/shard_map/all_to_all | solution.py:117
  16.3 16.6 %copy-start.6 = (s32[32]{0:T(128)S(1)}, s32[32]{0:T(128)}, u32[]{:S(2)}) copy-start(s32[32]{0:T(128)} %param.10) | copy-start | bytes 388
  16.3 16.6 %copy-start.7 = (s32[32]{0:T(128)S(1)}, s32[32]{0:T(128)}, u32[]{:S(2)}) copy-start(s32[32]{0:T(128)} %param.11) | copy-start | bytes 388
  16.3 17.3 %copy-start.8 = (s32[128,2]{0,1:T(2,128)S(1)}, s32[128,2]{0,1:T(2,128)}, u32[]{:S(2)}) copy-start(s32[128,2]{0,1:T(2,128)} %param.7) | copy-start | bytes 3076
  16.4 17.5 %copy-start.5 = (f32[128,2]{0,1:T(2,128)S(1)}, f32[128,2]{0,1:T(2,128)}, u32[]{:S(2)}) copy-start(f32[128,2]{0,1:T(2,128)} %param.8) | copy-start | bytes 3076
  17.5 29.9 %collective-permute-start = (bf16[64,1792]{0,1:T(8,128)(2,1)}, bf16[64,1792]{0,1:T(8,128)(2,1)S(1)}, u32[]{:S(2)}, u32[]{:S(2)}) collective-permute-start(bf16[64,1792]{0,1:T(8,128)(2,1)} %constant_dynamic-slice_fusion), channel_id=1, source_target_pairs={{0,16},{16,0},{1,17},{17,1},{2,18},{18,2},{3,19},{19,3},{4,20},{20... | collective-permute-start | bytes 688136 | tf_op jit(solution)/shard_map/ppermute | solution.py:12
  33.9 13.4 %collective-permute-start.1 = (f32[4,128]{1,0:T(4,128)S(1)}, f32[4,128]{1,0:T(4,128)S(1)}, u32[]{:S(2)}, u32[]{:S(2)}) collective-permute-start(f32[4,128]{1,0:T(4,128)S(1)} %pad_maximum_fusion), channel_id=1, source_target_pairs={{0,16},{16,0},{1,17},{17,1},{2,18},{18,2},{3,19},{19,3},{4,20},{20... | collective-permute-start | bytes 6152 | tf_op jit(solution)/shard_map/ppermute | solution.py:12
  47.3 52.9 %all-to-all-start.1 = ((bf16[32,16,1792]{2,1,0:T(8,128)(2,1)}), bf16[32,16,1792]{2,1,0:T(8,128)(2,1)}, u32[]{:S(2)}, u32[]{:S(2)}) async-start(bf16[32,16,1792]{2,1,0:T(8,128)(2,1)} %bitcast.107), calls=%async_computation.1 | async-start | bytes 3670016 | tf_op jit(solution)/shard_map/all_to_all | solution.py:47
  100.2 9.8 %copy-start.2 = (bf16[1,3,1792,128]{3,2,1,0:T(8,128)(2,1)S(1)}, bf16[1,3,1792,128]{3,2,1,0:T(8,128)(2,1)}, u32[]{:S(2)}) copy-start(bf16[1,3,1792,128]{3,2,1,0:T(8,128)(2,1)} %param.9) | copy-start | bytes 4128772
  100.2 34.8 %all-to-all-start.2 = ((bf16[32,16,1792]{2,1,0:T(8,128)(2,1)}), bf16[32,16,1792]{2,1,0:T(8,128)(2,1)}, u32[]{:S(2)}, u32[]{:S(2)}) async-start(bf16[32,16,1792]{2,1,0:T(8,128)(2,1)} %bitcast.23), calls=%async_computation.2 | async-start | bytes 3670016 | tf_op jit(solution)/shard_map/all_to_all | solution.py:47
  112.1 3.8 %collective-permute-start.2 = (f32[2,512,128]{2,1,0:T(8,128)S(1)}, f32[2,512,128]{2,1,0:T(8,128)S(1)}, u32[]{:S(2)}, u32[]{:S(2)}) collective-permute-start(f32[2,512,128]{2,1,0:T(8,128)S(1)} %convolution_bitcast_fusion.1), channel_id=1, source_target_pairs={{0,8},{8,0},{1,9},{9,1},{2,10},{10,2},{3,11},{11,3},{4,12},{12,4},... | collective-permute-start | bytes 1572872 | tf_op jit(solution)/shard_map/ppermute | solution.py:12
  134.9 30.9 %all-to-all-start.3 = ((bf16[32,16,1792]{2,1,0:T(8,128)(2,1)}), bf16[32,16,1792]{2,1,0:T(8,128)(2,1)S(1)}, u32[]{:S(2)}, u32[]{:S(2)}) async-start(bf16[32,16,1792]{2,1,0:T(8,128)(2,1)} %bitcast.106), calls=%async_computation.3 | async-start | bytes 3670016 | tf_op jit(solution)/shard_map/all_to_all | solution.py:47
  143.2 3.8 %collective-permute-start.4 = (f32[2,512,128]{2,1,0:T(8,128)S(1)}, f32[2,512,128]{2,1,0:T(8,128)S(1)}, u32[]{:S(2)}, u32[]{:S(2)}) collective-permute-start(f32[2,512,128]{2,1,0:T(8,128)S(1)} %convolution_bitcast_fusion), channel_id=1, source_target_pairs={{0,8},{8,0},{1,9},{9,1},{2,10},{10,2},{3,11},{11,3},{4,12},{12,4},... | collective-permute-start | bytes 1572872 | tf_op jit(solution)/shard_map/ppermute | solution.py:12
  165.8 1.2 copy-start
  167.1 40.6 %all-to-all-start.4 = ((bf16[32,16,1792]{2,1,0:T(8,128)(2,1)}), bf16[32,16,1792]{2,1,0:T(8,128)(2,1)S(1)}, u32[]{:S(2)}, u32[]{:S(2)}) async-start(bf16[32,16,1792]{2,1,0:T(8,128)(2,1)} %bitcast.105), calls=%async_computation.5 | async-start | bytes 3670016 | tf_op jit(solution)/shard_map/all_to_all | solution.py:47
  173.0 69.5 %reduce-scatter.2.cloned.1.call-start = ((), (), s32[]{:S(2)}) async-start(), calls=%async_computation.7 | async-start | bytes 1146880 | tf_op jit(solution)/shard_map/reduce_scatter | solution.py:126
  173.3 2.4 copy-start.1
  191.9 14.4 %collective-permute-start.10 = (bf16[336,128]{1,0:T(8,128)(2,1)S(1)}, bf16[336,128]{1,0:T(8,128)(2,1)S(1)}, u32[]{:S(2)}, u32[]{:S(2)}) collective-permute-start(bf16[336,128]{1,0:T(8,128)(2,1)S(1)} %bitcast_select_fusion.1), channel_id=1, source_target_pairs={{0,16},{16,0},{1,17},{17,1},{2,18},{18,2},{3,19},{19,3},{4,20},{20... | collective-permute-start | bytes 258056 | tf_op jit(solution)/shard_map/ppermute | solution.py:12
  207.6 86.3 %all-to-all-start.5 = ((bf16[16,336,128]{2,1,0:T(8,128)(2,1)}), bf16[16,336,128]{2,1,0:T(8,128)(2,1)S(1)}, u32[]{:S(2)}, u32[]{:S(2)}) async-start(bf16[16,336,128]{2,1,0:T(8,128)(2,1)} %select_select_fusion), calls=%async_computation.6 | async-start | bytes 2752512 | tf_op jit(solution)/shard_map/all_to_all | solution.py:129
  224.8 21.7 %collective-permute-start.5 = (bf16[2,128,448]{1,2,0:T(8,128)(2,1)}, bf16[2,128,448]{1,2,0:T(8,128)(2,1)S(1)}, u32[]{:S(2)}, u32[]{:S(2)}) collective-permute-start(bf16[2,128,448]{1,2,0:T(8,128)(2,1)} %get-tuple-element.20), channel_id=1, source_target_pairs={{0,1},{1,0},{2,3},{3,2},{4,5},{5,4},{6,7},{7,6},{8,9},{9,8},{10,11... | collective-permute-start | bytes 688136 | tf_op jit(solution)/shard_map/ppermute | solution.py:81
  236.6 23.2 %collective-permute-start.6 = (bf16[2,128,448]{1,2,0:T(8,128)(2,1)S(1)}, bf16[2,128,448]{1,2,0:T(8,128)(2,1)S(1)}, u32[]{:S(2)}, u32[]{:S(2)}) collective-permute-start(bf16[2,128,448]{1,2,0:T(8,128)(2,1)S(1)} %get-tuple-element.22), channel_id=1, source_target_pairs={{0,2},{1,3},{2,0},{3,1},{4,6},{5,7},{6,4},{7,5},{8,10},{9,11},{10,... | collective-permute-start | bytes 688136 | tf_op jit(solution)/shard_map/ppermute | solution.py:81
  238.5 21.3 %collective-permute-start.7 = (bf16[2,128,448]{1,2,0:T(8,128)(2,1)S(1)}, bf16[2,128,448]{1,2,0:T(8,128)(2,1)}, u32[]{:S(2)}, u32[]{:S(2)}) collective-permute-start(bf16[2,128,448]{1,2,0:T(8,128)(2,1)S(1)} %get-tuple-element.21), channel_id=1, source_target_pairs={{0,3},{1,2},{2,1},{3,0},{4,7},{5,6},{6,5},{7,4},{8,11},{9,10},{10,... | collective-permute-start | bytes 688136 | tf_op jit(solution)/shard_map/ppermute | solution.py:81
  242.5 50.7 %copy-start.4 = (bf16[1,2,128,448]{2,3,1,0:T(8,128)(2,1)S(1)}, bf16[1,2,128,448]{2,3,1,0:T(8,128)(2,1)}, u32[]{:S(2)}) copy-start(bf16[1,2,128,448]{2,3,1,0:T(8,128)(2,1)} %reduce-scatter.2.cloned.1.call-done) | copy-start | bytes 688132
  243.5 35.1 %collective-permute-start.3 = (bf16[128,448]{0,1:T(8,128)(2,1)S(1)}, bf16[128,448]{0,1:T(8,128)(2,1)S(1)}, u32[]{:S(2)}, u32[]{:S(2)}) collective-permute-start(bf16[128,448]{0,1:T(8,128)(2,1)S(1)} %dynamic-slice_bitcast_fusion.5), channel_id=1, source_target_pairs={{0,4},{4,0},{1,5},{5,1},{2,6},{6,2},{3,7},{7,3},{8,12},{12,8},{9,1... | collective-permute-start | bytes 344072 | tf_op jit(solution)/shard_map/ppermute | solution.py:12
  260.9 20.0 %collective-permute-start.8 = (bf16[128,448]{0,1:T(8,128)(2,1)S(1)}, bf16[128,448]{0,1:T(8,128)(2,1)S(1)}, u32[]{:S(2)}, u32[]{:S(2)}) collective-permute-start(bf16[128,448]{0,1:T(8,128)(2,1)S(1)} %get-tuple-element.23), channel_id=1, source_target_pairs={{0,16},{16,0},{1,17},{17,1},{2,18},{18,2},{3,19},{19,3},{4,20},{20... | collective-permute-start | bytes 344072 | tf_op jit(solution)/shard_map/ppermute | solution.py:12
  276.7 16.6 %collective-permute-start.9 = (bf16[128,448]{0,1:T(8,128)(2,1)S(1)}, bf16[128,448]{0,1:T(8,128)(2,1)S(1)}, u32[]{:S(2)}, u32[]{:S(2)}) collective-permute-start(bf16[128,448]{0,1:T(8,128)(2,1)S(1)} %get-tuple-element.24), channel_id=1, source_target_pairs={{0,20},{4,16},{16,4},{20,0},{1,21},{5,17},{17,5},{21,1},{2,22},{6,... | collective-permute-start | bytes 344072 | tf_op jit(solution)/shard_map/ppermute | solution.py:138
Sparse Core Ops, SparseCore 0:
  187.9 42.1 reduce-scatter.1

commit v3 on v1

--- a/solution.py
+++ b/solution.py
@@ -32,13 +32,19 @@
     return jnp.stack([row, row + CAP], axis=1).reshape(2, -1)
 
 
-def send_rows(rows, table):
-    total = 2 * CAP * lax.axis_size("y") * lax.axis_size("x")
-    at = jnp.arange(total, dtype=jnp.int32)
+def plane_rows():
+    return 2 * CAP * lax.axis_size("y") * lax.axis_size("x")
+
+
+def gather_rows(rows, table):
+    at = jnp.arange(plane_rows(), dtype=jnp.int32)
     pick = ((rows[0][None, :] == at[:, None]) | (rows[1][None, :] == at[:, None])).astype(jnp.bfloat16)
-    out = jnp.dot(pick, table, preferred_element_type=jnp.float32).astype(jnp.bfloat16)
-    out = out.reshape(total // CAP, CAP, -1)
-    return lax.all_to_all(out, PLANE, split_axis=0, concat_axis=0, tiled=True).reshape(total, -1)
+    return jnp.dot(pick, table, preferred_element_type=jnp.float32).astype(jnp.bfloat16)
+
+
+def exchange(rows, axes=PLANE):
+    blocks = rows.reshape((lax.axis_size(axes), -1, rows.shape[-1]))
+    return lax.all_to_all(blocks, axes, split_axis=0, concat_axis=0, tiled=True).reshape(rows.shape)
 
 
 def expert_part(rows, weights):
@@ -50,12 +56,8 @@
     ).astype(jnp.bfloat16)
 
 
-def return_rows(out, codes, rows):
-    total = out.shape[0]
-    back = lax.all_to_all(
-        out.reshape(total // CAP, CAP, -1), PLANE, split_axis=0, concat_axis=0, tiled=True
-    ).reshape(total, -1)
-    at = jnp.arange(total, dtype=jnp.int32)
+def weighted(back, codes, rows):
+    at = jnp.arange(back.shape[0], dtype=jnp.int32)
     gate = jnp.concatenate([codes[2:4], codes[2:4]], axis=1)
     mix = sum(jnp.where(rows[k][:, None] == at[None, :], gate[k][:, None], 0.0) for k in range(2))
     high = mix.astype(jnp.bfloat16)
@@ -70,24 +72,22 @@
     return jnp.transpose(parts, (2, 1, 0, 3)).reshape(groups, mixed.shape[0] // 2, -1)
 
 
-def relocate(own, old_owner, new_owner):
-    chips = lax.axis_size("y") * lax.axis_size("x")
-    zh = lax.axis_index("zh")
+def after(value, *others):
+    return lax.optimization_barrier((value, *others))[0]
+
+
+def pick_pieces(spread, old_owner, new_owner, zh):
     moved = new_owner != old_owner
     low = jnp.min(jnp.where(moved, old_owner, old_owner.shape[0]))
     high = jnp.max(jnp.where(moved, old_owner, -1))
-    pieces = own.reshape(chips, -1, own.shape[-1])
-    spread = lax.all_to_all(pieces, ("y", "x"), split_axis=0, concat_axis=0, tiled=True)
-    low_piece = lax.dynamic_index_in_dim(spread, low // 2, 0, keepdims=False)
-    high_piece = lax.dynamic_index_in_dim(spread, high // 2, 0, keepdims=False)
-    low_here, high_here = low % 2 == zh, high % 2 == zh
+    low_piece = lax.dynamic_index_in_dim(spread, low >> 1, 0, keepdims=False)
+    high_piece = lax.dynamic_index_in_dim(spread, high >> 1, 0, keepdims=False)
+    low_here, high_here = (low & 1) == zh, (high & 1) == zh
     other = swap(jnp.where(low_here, low_piece, high_piece), "zh")
     to_low = jnp.where(high_here, high_piece, other)
     to_high = jnp.where(low_here, low_piece, other)
-    slots = 2 * jnp.arange(chips, dtype=jnp.int32)[:, None, None] + zh
-    chosen = jnp.where(slots == low, to_low[None], jnp.where(slots == high, to_high[None], spread))
-    arrived = lax.all_to_all(chosen, ("y", "x"), split_axis=0, concat_axis=0, tiled=True)
-    return arrived.reshape(own.shape)
+    slots = 2 * jnp.arange(spread.shape[0], dtype=jnp.int32)[:, None, None] + zh
+    return jnp.where(slots == low, to_low[None], jnp.where(slots == high, to_high[None], spread))
 
 
 def shards(tokens, routes, gate_values, expert_weights, old_owner, new_owner):
@@ -99,21 +99,29 @@
     other_codes = swap(codes, "zh")
     table = jnp.transpose(tokens.reshape(tok_rows, groups, 2, -1), (2, 0, 1, 3)).reshape(2 * tok_rows, -1)
     share = 2 * tok_rows // groups
-    ring = lax.all_gather(lax.dynamic_slice_in_dim(table, lane * share, share, 0), RING)
-    rows = placed_rows(codes, zh)
-    mixed = return_rows(expert_part(send_rows(rows, table), own), codes, rows)
-    mixed = by_columns(mixed, groups)
+    part = lax.dynamic_slice_in_dim(table, lane * share, share, 0)
+    ring = lax.all_gather(part, RING)
+    rows, other_rows = placed_rows(codes, zh), placed_rows(other_codes, zh)
+    back = exchange(expert_part(exchange(after(gather_rows(rows, table), part)), own))
 
+    ring = after(ring, back)
     other_table = lax.dynamic_slice_in_dim(ring, (1 - zh) * groups, groups, 0).reshape(2 * tok_rows, -1)
-    other_rows = placed_rows(other_codes, zh)
-    other_mixed = return_rows(expert_part(send_rows(other_rows, other_table), own), other_codes, other_rows)
-    other_mixed = by_columns(other_mixed, groups)
-    both = jnp.concatenate(
-        [jnp.where(zh == 0, mixed, other_mixed), jnp.where(zh == 0, other_mixed, mixed)], axis=0
-    )
-    both, own = lax.optimization_barrier((both, own))
+    other_sent = exchange(gather_rows(other_rows, other_table))
+    mixed = by_columns(weighted(back, codes, rows), groups)
+    both = jnp.zeros((2 * groups,) + mixed.shape[1:], mixed.dtype)
+    both = lax.dynamic_update_slice_in_dim(both, mixed, zh * groups, 0)
+    both, other_sent = lax.optimization_barrier((both, other_sent))
+    other_back = exchange(expert_part(other_sent, own))
+    other_mixed = by_columns(weighted(other_back, other_codes, other_rows), groups)
+    both = lax.dynamic_update_slice_in_dim(both, other_mixed, (1 - zh) * groups, 0)
     out = lax.psum_scatter(both, RING, scatter_dimension=0, tiled=True)[0]
-    return out, relocate(own, old_owner, new_owner)[None]
+
+    plane = ("y", "x")
+    pieces = own.reshape(lax.axis_size(plane), -1, own.shape[-1])
+    spread = lax.all_to_all(after(pieces, other_back), plane, split_axis=0, concat_axis=0, tiled=True)
+    chosen = pick_pieces(spread, old_owner, new_owner, zh)
+    arrived = lax.all_to_all(chosen, plane, split_axis=0, concat_axis=0, tiled=True)
+    return out, arrived.reshape(expert_weights.shape)
 
 
 def solution(mesh):

time: 281 us -> 264 us (0.940)
  the two profiles are of different devices: /device:TPU:28 before, /device:TPU:1 now
where the time goes in v3:
time: 264 us; the launch traced here: 260 us
  waiting for transfers between devices  108 us (41%)
  starting transfers between devices  70.1 us (27%)
  blocking collectives  29.2 us (11%)
  matrix products  17.8 us (7%)
  between operations  16.8 us (6%)
  local copies, waits for them, and re-layouts  14.9 us (6%)
  other arithmetic  3.16 us (1%)
    all_to_all x4, waiting for transfers between devices, exchange(): lax.all_to_all(blocks, axes, split_axis=0, concat_axis=0, tiled=True)  66.9 us
    all_to_all x4, starting transfers between devices, exchange(): lax.all_to_all(blocks, axes, split_axis=0, concat_axis=0, tiled=True)  35.7 us
    ppermute x4, starting transfers between devices, swap(): return lax.ppermute(value, axis, [(0, 1), (1, 0)])  29.6 us
    all_to_all x1, blocking collectives, shards(): lax.all_to_all(chosen, plane, split_axis=0, concat_axis=0, tiled=True)  29.2 us
    all_to_all x1, waiting for transfers between devices, shards(): lax.all_to_all(after(pieces, other_back), plane, split_axis=0, concat_axi...  16.6 us
    all_gather x1, waiting for transfers between devices, shards(): ring = lax.all_gather(part, RING)  14.9 us
    ppermute x4, waiting for transfers between devices, swap(): return lax.ppermute(value, axis, [(0, 1), (1, 0)])  9.66 us
    dot_general x2, matrix products, expert_part(): lax.dot_general(hidden, weights[2], (((1,), (1,)), ((), ())), preferred_e...  5.86 us
  transfers between devices with their start and end apart: 11, of which 9 were waited for; matrix products, arithmetic and copies ran while one was open for 5% of the time, Pallas kernels for 0%

profile of v3, /device:TPU:1, one launch (start us, length us, event | category | flops | bytes accessed | tf_op | source)
XLA Modules:
  0.0 260.0 jit_solution(9624687144257154485)
XLA Ops:
  7.2 1.3 fusion.59
  8.5 1.0 fusion.8
  9.5 1.6 copy.21
  11.0 0.8 copy.22
  11.8 0.1 copy.33
  12.0 1.9 convolution_convert_fusion.1
  13.9 0.2 constant_dynamic-slice_fusion.1
  14.1 10.5 %all-to-all-start = ((bf16[32,16,1792]{2,1,0:T(8,128)(2,1)}), bf16[32,16,1792]{2,1,0:T(8,128)(2,1)S(1)}, u32[]{:S(2)}, u32[]{:S(2)}) async-start(bf16[32,16,1792]{2,1,0:T(8,128)(2,1)} %bitcast.10), calls=%async_computation | async-start | bytes 3670016 | tf_op jit(solution)/shard_map/all_to_all | solution.py:47
  24.7 0.8 copy.25
  25.5 24.1 %all-to-all-done = bf16[32,16,1792]{2,1,0:T(8,128)(2,1)S(1)} async-done(((bf16[32,16,1792]{2,1,0:T(8,128)(2,1)}), bf16[32,16,1792]{2,1,0:T(8,128)(2,1)S(1)}, u32[]{:S(2)}, u32[]{:S(2)}) %all-to-all-start) | async-done | bytes 1835040 | tf_op jit(solution)/shard_map/all_to_all | solution.py:47
  49.6 1.8 convolution_bitcast_fusion
  51.4 4.2 %collective-permute-start = (f32[2,512,128]{2,1,0:T(8,128)S(1)}, f32[2,512,128]{2,1,0:T(8,128)S(1)}, u32[]{:S(2)}, u32[]{:S(2)}) collective-permute-start(f32[2,512,128]{2,1,0:T(8,128)S(1)} %convolution_bitcast_fusion), channel_id=1, source_target_pairs={{0,8},{8,0},{1,9},{9,1},{2,10},{10,2},{3,11},{11,3},{4,12},{12,4},... | collective-permute-start | bytes 1572872 | tf_op jit(solution)/shard_map/ppermute | solution.py:12
  55.6 1.5 collective-permute-done
  57.2 2.9 %convolution_convert_fusion.3 = bf16[512,1792]{1,0:T(8,128)(2,1)} fusion(bf16[1,3,1792,128]{3,2,1,0:T(8,128)(2,1)} %param.9, f32[2,512,128]{2,1,0:T(8,128)S(1)} %add.172), kind=kOutput, calls=%fused_computation.3 | convolution fusion | flops 236191744 | bytes 2818048 | tf_op jit(solution)/shard_map/dot_general | solution.py:54
  60.1 4.2 %all-to-all-start.1 = ((bf16[32,16,1792]{2,1,0:T(8,128)(2,1)}), bf16[32,16,1792]{2,1,0:T(8,128)(2,1)S(1)}, u32[]{:S(2)}, u32[]{:S(2)}) async-start(bf16[32,16,1792]{2,1,0:T(8,128)(2,1)} %bitcast.92), calls=%async_computation.1 | async-start | bytes 3670016 | tf_op jit(solution)/shard_map/all_to_all | solution.py:47
  64.3 13.4 %collective-permute-start.1 = (f32[4,128]{1,0:T(4,128)S(1)}, f32[4,128]{1,0:T(4,128)S(1)}, u32[]{:S(2)}, u32[]{:S(2)}) collective-permute-start(f32[4,128]{1,0:T(4,128)S(1)} %pad_maximum_fusion), channel_id=1, source_target_pairs={{0,16},{16,0},{1,17},{17,1},{2,18},{18,2},{3,19},{19,3},{4,20},{20... | collective-permute-start | bytes 6152 | tf_op jit(solution)/shard_map/ppermute | solution.py:12
  77.7 1.1 collective-permute-done.1
  78.8 14.9 %all-gather.3.cloned.1.call-done = bf16[512,1792]{1,0:T(8,128)(2,1)} async-done(((bf16[32,1792]{1,0:T(8,128)(2,1)}), bf16[512,1792]{1,0:T(8,128)(2,1)}) %all-gather.3.cloned.1.call-update) | async-done | bytes 1835024 | tf_op jit(solution)/shard_map/all_gather | solution.py:103
  93.8 1.2 constant_dynamic-slice_fusion
  95.0 1.9 convolution_convert_fusion
  96.9 17.0 %all-to-all-start.2 = ((bf16[32,16,1792]{2,1,0:T(8,128)(2,1)}), bf16[32,16,1792]{2,1,0:T(8,128)(2,1)}, u32[]{:S(2)}, u32[]{:S(2)}) async-start(bf16[32,16,1792]{2,1,0:T(8,128)(2,1)} %bitcast.94), calls=%async_computation.2 | async-start | bytes 3670016 | tf_op jit(solution)/shard_map/all_to_all | solution.py:47
  114.0 0.8 fusion.40
  114.7 0.8 fusion
  115.5 1.5 reshape.276
  117.0 1.1 copy.28
  118.2 1.6 broadcast_in_dim.96
  119.9 1.0 constant_dynamic-update-slice_fusion.1
  120.9 18.1 %all-to-all-done.2 = bf16[32,16,1792]{2,1,0:T(8,128)(2,1)} async-done(((bf16[32,16,1792]{2,1,0:T(8,128)(2,1)}), bf16[32,16,1792]{2,1,0:T(8,128)(2,1)}, u32[]{:S(2)}, u32[]{:S(2)}) %all-to-all-start.2) | async-done | bytes 1835040 | tf_op jit(solution)/shard_map/all_to_all | solution.py:47
  138.9 2.4 fusion.4
  141.3 4.2 %collective-permute-start.2 = (f32[2,512,128]{2,1,0:T(8,128)S(1)}, f32[2,512,128]{2,1,0:T(8,128)S(1)}, u32[]{:S(2)}, u32[]{:S(2)}) collective-permute-start(f32[2,512,128]{2,1,0:T(8,128)S(1)} %fusion.4), channel_id=1, source_target_pairs={{0,8},{8,0},{1,9},{9,1},{2,10},{10,2},{3,11},{11,3},{4,12},{12,4},... | collective-permute-start | bytes 1572872 | tf_op jit(solution)/shard_map/ppermute | solution.py:12
  145.5 1.5 collective-permute-done.2
  147.1 2.9 %convolution_convert_fusion.2 = bf16[512,1792]{1,0:T(8,128)(2,1)} fusion(bf16[1,3,1792,128]{3,2,1,0:T(8,128)(2,1)} %param.9, f32[2,512,128]{2,1,0:T(8,128)S(1)} %add.182), kind=kOutput, calls=%fused_computation.2 | convolution fusion | flops 236191744 | bytes 2818048 | tf_op jit(solution)/shard_map/dot_general | solution.py:54
  150.0 4.0 %all-to-all-start.3 = ((bf16[32,16,1792]{2,1,0:T(8,128)(2,1)}), bf16[32,16,1792]{2,1,0:T(8,128)(2,1)S(1)}, u32[]{:S(2)}, u32[]{:S(2)}) async-start(bf16[32,16,1792]{2,1,0:T(8,128)(2,1)} %bitcast.93), calls=%async_computation.3 | async-start | bytes 3670016 | tf_op jit(solution)/shard_map/all_to_all | solution.py:47
  154.0 0.2 reduce-scatter.2.cloned.1.call-start
  154.3 24.7 %all-to-all-done.3 = bf16[32,16,1792]{2,1,0:T(8,128)(2,1)S(1)} async-done(((bf16[32,16,1792]{2,1,0:T(8,128)(2,1)}), bf16[32,16,1792]{2,1,0:T(8,128)(2,1)S(1)}, u32[]{:S(2)}, u32[]{:S(2)}) %all-to-all-start.3) | async-done | bytes 1835040 | tf_op jit(solution)/shard_map/all_to_all | solution.py:47
  179.0 0.7 fusion.43
  179.8 0.8 fusion.1
  180.5 1.5 reshape.277
  182.1 1.1 copy.29
  183.3 1.1 constant_dynamic-update-slice_fusion
  184.4 4.5 %all-to-all-start.4 = ((bf16[16,336,128]{2,1,0:T(8,128)(2,1)}), bf16[16,336,128]{2,1,0:T(8,128)(2,1)S(1)}, u32[]{:S(2)}, u32[]{:S(2)}) async-start(bf16[16,336,128]{2,1,0:T(8,128)(2,1)} %bitcast.40), calls=%async_computation.5 | async-start | bytes 2752512 | tf_op jit(solution)/shard_map/all_to_all | solution.py:121
  191.3 16.6 %all-to-all-done.4 = bf16[16,336,128]{2,1,0:T(8,128)(2,1)S(1)} async-done(((bf16[16,336,128]{2,1,0:T(8,128)(2,1)}), bf16[16,336,128]{2,1,0:T(8,128)(2,1)S(1)}, u32[]{:S(2)}, u32[]{:S(2)}) %all-to-all-start.4) | async-done | bytes 1376288 | tf_op jit(solution)/shard_map/all_to_all | solution.py:121
  207.9 7.8 %collective-permute-start.3 = (bf16[336,128]{1,0:T(8,128)(2,1)S(1)}, bf16[336,128]{1,0:T(8,128)(2,1)S(1)}, u32[]{:S(2)}, u32[]{:S(2)}) collective-permute-start(bf16[336,128]{1,0:T(8,128)(2,1)S(1)} %bitcast_select_fusion.1), channel_id=1, source_target_pairs={{0,16},{16,0},{1,17},{17,1},{2,18},{18,2},{3,19},{19,3},{4,20},{20... | collective-permute-start | bytes 258056 | tf_op jit(solution)/shard_map/ppermute | solution.py:12
  215.7 1.2 fusion.61
  216.9 5.6 %collective-permute-done.3 = bf16[336,128]{1,0:T(8,128)(2,1)S(1)} collective-permute-done((bf16[336,128]{1,0:T(8,128)(2,1)S(1)}, bf16[336,128]{1,0:T(8,128)(2,1)S(1)}, u32[]{:S(2)}, u32[]{:S(2)}) %collective-permute-start.3) | collective-permute-done | bytes 86048 | tf_op jit(solution)/shard_map/ppermute | solution.py:12
  222.5 0.3 select_select_fusion
  222.9 29.2 %all_to_all.30 = bf16[16,336,128]{2,1,0:T(8,128)(2,1)S(1)} all-to-all(bf16[16,336,128]{2,1,0:T(8,128)(2,1)S(1)} %select_select_fusion), channel_id=1, replica_groups=mesh['y'=4,'x'=4,'zh'=2,'c'=2,'mp'=8] {'y','x'}, dimensions={0} | all-to-all | bytes 2752512 | tf_op jit(solution)/shard_map/all_to_all | solution.py:123
  252.1 1.1 copy.37
  (22 shorter events, 0.6 us)
Async XLA Ops:
  14.1 35.5 %all-to-all-start = ((bf16[32,16,1792]{2,1,0:T(8,128)(2,1)}), bf16[32,16,1792]{2,1,0:T(8,128)(2,1)S(1)}, u32[]{:S(2)}, u32[]{:S(2)}) async-start(bf16[32,16,1792]{2,1,0:T(8,128)(2,1)} %bitcast.10), calls=%async_computation | async-start | bytes 3670016 | tf_op jit(solution)/shard_map/all_to_all | solution.py:47
  24.6 69.2 %all-gather.3.cloned.1.call-start = ((), (), s32[]{:S(2)}) async-start(), calls=%async_computation.8 | async-start | bytes 1949696 | tf_op jit(solution)/shard_map/all_gather | solution.py:103
  51.4 5.7 %collective-permute-start = (f32[2,512,128]{2,1,0:T(8,128)S(1)}, f32[2,512,128]{2,1,0:T(8,128)S(1)}, u32[]{:S(2)}, u32[]{:S(2)}) collective-permute-start(f32[2,512,128]{2,1,0:T(8,128)S(1)} %convolution_bitcast_fusion), channel_id=1, source_target_pairs={{0,8},{8,0},{1,9},{9,1},{2,10},{10,2},{3,11},{11,3},{4,12},{12,4},... | collective-permute-start | bytes 1572872 | tf_op jit(solution)/shard_map/ppermute | solution.py:12
  60.1 4.2 %copy-start = (f32[128,2]{0,1:T(2,128)S(1)}, f32[128,2]{0,1:T(2,128)}, u32[]{:S(2)}) copy-start(f32[128,2]{0,1:T(2,128)} %param.8) | copy-start | bytes 3076
  60.1 33.7 %all-to-all-start.1 = ((bf16[32,16,1792]{2,1,0:T(8,128)(2,1)}), bf16[32,16,1792]{2,1,0:T(8,128)(2,1)S(1)}, u32[]{:S(2)}, u32[]{:S(2)}) async-start(bf16[32,16,1792]{2,1,0:T(8,128)(2,1)} %bitcast.92), calls=%async_computation.1 | async-start | bytes 3670016 | tf_op jit(solution)/shard_map/all_to_all | solution.py:47
  64.3 14.5 %collective-permute-start.1 = (f32[4,128]{1,0:T(4,128)S(1)}, f32[4,128]{1,0:T(4,128)S(1)}, u32[]{:S(2)}, u32[]{:S(2)}) collective-permute-start(f32[4,128]{1,0:T(4,128)S(1)} %pad_maximum_fusion), channel_id=1, source_target_pairs={{0,16},{16,0},{1,17},{17,1},{2,18},{18,2},{3,19},{19,3},{4,20},{20... | collective-permute-start | bytes 6152 | tf_op jit(solution)/shard_map/ppermute | solution.py:12
  96.9 42.0 %all-to-all-start.2 = ((bf16[32,16,1792]{2,1,0:T(8,128)(2,1)}), bf16[32,16,1792]{2,1,0:T(8,128)(2,1)}, u32[]{:S(2)}, u32[]{:S(2)}) async-start(bf16[32,16,1792]{2,1,0:T(8,128)(2,1)} %bitcast.94), calls=%async_computation.2 | async-start | bytes 3670016 | tf_op jit(solution)/shard_map/all_to_all | solution.py:47
  141.3 5.7 %collective-permute-start.2 = (f32[2,512,128]{2,1,0:T(8,128)S(1)}, f32[2,512,128]{2,1,0:T(8,128)S(1)}, u32[]{:S(2)}, u32[]{:S(2)}) collective-permute-start(f32[2,512,128]{2,1,0:T(8,128)S(1)} %fusion.4), channel_id=1, source_target_pairs={{0,8},{8,0},{1,9},{9,1},{2,10},{10,2},{3,11},{11,3},{4,12},{12,4},... | collective-permute-start | bytes 1572872 | tf_op jit(solution)/shard_map/ppermute | solution.py:12
  150.0 29.0 %all-to-all-start.3 = ((bf16[32,16,1792]{2,1,0:T(8,128)(2,1)}), bf16[32,16,1792]{2,1,0:T(8,128)(2,1)S(1)}, u32[]{:S(2)}, u32[]{:S(2)}) async-start(bf16[32,16,1792]{2,1,0:T(8,128)(2,1)} %bitcast.93), calls=%async_computation.3 | async-start | bytes 3670016 | tf_op jit(solution)/shard_map/all_to_all | solution.py:47
  154.0 98.0 %reduce-scatter.2.cloned.1.call-start = ((), (), s32[]{:S(2)}) async-start(), calls=%async_computation.7 | async-start | bytes 1949696 | tf_op jit(solution)/shard_map/reduce_scatter | solution.py:117
  184.4 23.5 %all-to-all-start.4 = ((bf16[16,336,128]{2,1,0:T(8,128)(2,1)}), bf16[16,336,128]{2,1,0:T(8,128)(2,1)S(1)}, u32[]{:S(2)}, u32[]{:S(2)}) async-start(bf16[16,336,128]{2,1,0:T(8,128)(2,1)} %bitcast.40), calls=%async_computation.5 | async-start | bytes 2752512 | tf_op jit(solution)/shard_map/all_to_all | solution.py:121
  207.9 14.6 %collective-permute-start.3 = (bf16[336,128]{1,0:T(8,128)(2,1)S(1)}, bf16[336,128]{1,0:T(8,128)(2,1)S(1)}, u32[]{:S(2)}, u32[]{:S(2)}) collective-permute-start(bf16[336,128]{1,0:T(8,128)(2,1)S(1)} %bitcast_select_fusion.1), channel_id=1, source_target_pairs={{0,16},{16,0},{1,17},{17,1},{2,18},{18,2},{3,19},{19,3},{4,20},{20... | collective-permute-start | bytes 258056 | tf_op jit(solution)/shard_map/ppermute | solution.py:12
Sparse Core Ops, SparseCore 0:
  28.1 65.6 all-gather.2
  184.5 61.9 reduce-scatter.1

commit v4 on v2

--- a/solution.py
+++ b/solution.py
@@ -82,8 +82,7 @@
     return total
 
 
-def after(value, *others):
-    return lax.optimization_barrier((value, *others))[0]
+tied = lax.optimization_barrier
 
 
 def pick_pieces(spread, old_owner, new_owner, zh):
@@ -107,27 +106,35 @@
     own = expert_weights[0]
     table = jnp.transpose(tokens.reshape(tok_rows, 2 * near, 2, -1), (2, 0, 1, 3)).reshape(2 * tok_rows, -1)
     share = 2 * tok_rows // near
-    quarter = swap(lax.dynamic_slice_in_dim(table, place * share, share, 0), "zh")
+    part = lax.dynamic_slice_in_dim(table, place * share, share, 0)
     codes = place_codes(routes, gate_values, old_owner)
-    other_codes = swap(codes, "zh")
+    rows = placed_rows(codes, zh)
+    part, payload = tied((part, gather_rows(rows, table)))
+    quarter = swap(part, "zh")
+    sent = exchange(payload)
+    chips = lax.axis_size("y") * lax.axis_size("x")
+    pieces, sent, quarter = tied((own.reshape(chips, -1, own.shape[-1]), sent, quarter))
+    spread = lax.all_to_all(pieces, ("y", "x"), split_axis=0, concat_axis=0, tiled=True)
+    quarter, later_codes = tied((quarter, codes))
+    other_codes = swap(later_codes, "zh")
+    other_rows = placed_rows(other_codes, zh)
     other_table = lax.all_gather(quarter, NEAR, tiled=True)
-
-    chips = lax.axis_size("y") * lax.axis_size("x")
-    pieces = own.reshape(chips, -1, own.shape[-1])
-    spread = lax.all_to_all(pieces, ("y", "x"), split_axis=0, concat_axis=0, tiled=True)
-    rows = placed_rows(codes, zh)
-    sent = exchange(after(gather_rows(rows, table), spread, quarter, other_codes))
-    other_rows = placed_rows(other_codes, zh)
-    other_sent = exchange(after(gather_rows(other_rows, other_table), sent))
-    back = exchange(after(expert_part(sent, own), other_sent))
-    other_back = exchange(after(expert_part(other_sent, own), back))
+    payload, spread = tied((gather_rows(other_rows, other_table), spread))
+    other_sent = exchange(payload)
+    payload, other_sent = tied((expert_part(sent, own), other_sent))
+    back = exchange(payload)
+    chosen = pick_pieces(spread, old_owner, new_owner, zh)
+    payload, back, chosen = tied((expert_part(other_sent, own), back, chosen))
+    other_back = exchange(payload)
 
     parts = by_columns(weighted(back, codes, rows), near)
-    kept = lax.psum_scatter(parts, NEAR, scatter_dimension=0, tiled=True)[0]
+    kept = near_sum(parts, place).astype(jnp.bfloat16)
+    other_back, kept = tied((other_back, kept))
     other_parts = by_columns(weighted(other_back, other_codes, other_rows), near)
-    chosen = pick_pieces(spread, old_owner, new_owner, zh)
-    arrived = lax.all_to_all(after(chosen, other_back), ("y", "x"), split_axis=0, concat_axis=0, tiled=True)
-    other_kept = near_sum(other_parts, place).astype(jnp.bfloat16)
+    near_parts = lax.all_to_all(other_parts, NEAR, split_axis=0, concat_axis=0, tiled=True)
+    near_parts, chosen = tied((near_parts, chosen))
+    arrived = lax.all_to_all(chosen, ("y", "x"), split_axis=0, concat_axis=0, tiled=True)
+    other_kept = jnp.sum(near_parts.astype(jnp.float32), axis=0).astype(jnp.bfloat16)
 
     def of(value, index):
         return lax.dynamic_index_in_dim(value, index, 0, keepdims=False)

time: 307 us -> 290 us (0.945)
  blocking collectives: 41.1 us -> 69.9 us
  between operations: 17.2 us -> 3.68 us
  local copies, waits for them, and re-layouts: 24.3 us -> 12.5 us
  waiting for transfers between devices: 75.8 us -> 65.7 us
  starting transfers between devices: 118 us -> 108 us
    all_to_all x0 -> x1, blocking collectives: none -> 30.4 us  [shards(): lax.all_to_all(other_parts, NEAR, split_axis=0, concat_axis=0, tiled=True)]
    all_to_all x4, waiting for transfers between devices: 32.8 us -> 16.8 us  [exchange(): lax.all_to_all(blocks, axes, split_axis=0, concat_axis=0, tiled=True)]
    ppermute x7, waiting for transfers between devices: 17.4 us -> 32.7 us  [swap(): return lax.ppermute(value, axis, [(0, 1), (1, 0)])]
    ppermute x1, waiting for transfers between devices: 12.4 us -> 4.11 us  [shards(): lax.ppermute(of(other_kept, 1 - far), ('zh', 'ma'), [(i, i ^ 3) for i in...]
    ppermute x3, starting transfers between devices: 17.7 us -> 9.45 us  [near_sum(): lax.ppermute(block, NEAR, [(i, i ^ step) for i in range(count)])]
    reshape x4, local copies, waits for them, and re-layouts: 14 us -> 5.78 us  [by_columns(): parts = mixed.astype(jnp.bfloat16).reshape(2, tok_rows, 2, near, -1)]
    ppermute x7, starting transfers between devices: 52.5 us -> 46.9 us  [swap(): return lax.ppermute(value, axis, [(0, 1), (1, 0)])]
    all_to_all x4, starting transfers between devices: 31.2 us -> 36.4 us  [exchange(): lax.all_to_all(blocks, axes, split_axis=0, concat_axis=0, tiled=True)]
  transfers between devices with their start and end apart: 18 -> 17, of which waited for: 9 -> 10; matrix products, arithmetic and copies ran while one was open for 16% -> 7% of each run, Pallas kernels for 0% -> 0%
where the time goes in v4:
time: 290 us; the launch traced here: 286 us
  starting transfers between devices  108 us (37%)
  blocking collectives  69.9 us (24%)
  waiting for transfers between devices  65.7 us (23%)
  matrix products  21.4 us (7%)
  local copies, waits for them, and re-layouts  12.5 us (4%)
  other arithmetic  5.27 us (2%)
  between operations  3.68 us (1%)
    ppermute x7, starting transfers between devices, swap(): return lax.ppermute(value, axis, [(0, 1), (1, 0)])  46.9 us
    all_gather x1, blocking collectives, shards(): other_table = lax.all_gather(quarter, NEAR, tiled=True)  39.5 us
    all_to_all x4, starting transfers between devices, exchange(): lax.all_to_all(blocks, axes, split_axis=0, concat_axis=0, tiled=True)  36.4 us
    ppermute x7, waiting for transfers between devices, swap(): return lax.ppermute(value, axis, [(0, 1), (1, 0)])  32.7 us
    all_to_all x1, blocking collectives, shards(): lax.all_to_all(other_parts, NEAR, split_axis=0, concat_axis=0, tiled=True)  30.4 us
    all_to_all x4, waiting for transfers between devices, exchange(): lax.all_to_all(blocks, axes, split_axis=0, concat_axis=0, tiled=True)  16.8 us
    ppermute x3, waiting for transfers between devices, near_sum(): lax.ppermute(block, NEAR, [(i, i ^ step) for i in range(count)])  12.1 us
    ppermute x3, starting transfers between devices, near_sum(): lax.ppermute(block, NEAR, [(i, i ^ step) for i in range(count)])  9.45 us
  transfers between devices with their start and end apart: 17, of which 10 were waited for; matrix products, arithmetic and copies ran while one was open for 7% of the time, Pallas kernels for 0%

profile of v4, /device:TPU:1, one launch (start us, length us, event | category | flops | bytes accessed | tf_op | source)
XLA Modules:
  0.0 286.4 jit_solution(11150770959970571647)
XLA Ops:
  0.6 1.3 fusion.70
  2.9 1.6 copy.20
  5.4 1.9 convolution_convert_fusion.1
  7.6 10.5 %all-to-all-start = ((bf16[32,16,1792]{2,1,0:T(8,128)(2,1)}), bf16[32,16,1792]{2,1,0:T(8,128)(2,1)S(1)}, u32[]{:S(2)}, u32[]{:S(2)}) async-start(bf16[32,16,1792]{2,1,0:T(8,128)(2,1)} %bitcast.8), calls=%async_computation | async-start | bytes 3670016 | tf_op jit(solution)/shard_map/all_to_all | solution.py:47
  18.1 13.5 %collective-permute-start = (bf16[64,1792]{0,1:T(8,128)(2,1)S(1)}, bf16[64,1792]{0,1:T(8,128)(2,1)S(1)}, u32[]{:S(2)}, u32[]{:S(2)}) collective-permute-start(bf16[64,1792]{0,1:T(8,128)(2,1)S(1)} %constant_dynamic-slice_fusion), channel_id=1, source_target_pairs={{0,16},{16,0},{1,17},{17,1},{2,18},{18,2},{3,19},{19,3},{4,20},{20... | collective-permute-start | bytes 688136 | tf_op jit(solution)/shard_map/ppermute | solution.py:12
  31.6 15.0 %collective-permute-done = bf16[64,1792]{0,1:T(8,128)(2,1)S(1)} collective-permute-done((bf16[64,1792]{0,1:T(8,128)(2,1)S(1)}, bf16[64,1792]{0,1:T(8,128)(2,1)S(1)}, u32[]{:S(2)}, u32[]{:S(2)}) %collective-permute-start) | collective-permute-done | bytes 229408 | tf_op jit(solution)/shard_map/ppermute | solution.py:12
  46.6 1.3 copy-done.1
  47.9 6.5 %all-to-all-start.1 = ((bf16[16,336,128]{2,1,0:T(8,128)(2,1)}), bf16[16,336,128]{2,1,0:T(8,128)(2,1)S(1)}, u32[]{:S(2)}, u32[]{:S(2)}) async-start(bf16[16,336,128]{2,1,0:T(8,128)(2,1)} %bitcast), calls=%async_computation.1 | async-start | bytes 2752512 | tf_op jit(solution)/shard_map/all_to_all | solution.py:117
  54.5 12.0 %collective-permute-start.2 = (f32[4,128]{1,0:T(4,128)S(1)}, f32[4,128]{1,0:T(4,128)S(1)}, u32[]{:S(2)}, u32[]{:S(2)}) collective-permute-start(f32[4,128]{1,0:T(4,128)S(1)} %pad_maximum_fusion), channel_id=1, source_target_pairs={{0,16},{16,0},{1,17},{17,1},{2,18},{18,2},{3,19},{19,3},{4,20},{20... | collective-permute-start | bytes 6152 | tf_op jit(solution)/shard_map/ppermute | solution.py:12
  66.6 39.5 %all_gather.3 = bf16[256,1792]{1,0:T(8,128)(2,1)S(1)} all-gather(bf16[64,1792]{1,0:T(8,128)(2,1)S(1)} %copy.22), channel_id=1, replica_groups=mesh['y'=4,'x'=4,'zh'=2,'c'=2,'ma'=2,'mb'=2,'mc'=2] {'mb','mc'}, dimensions={0}, use_global_device_ids=true | all-gather | bytes 1146880 | tf_op jit(solution)/shard_map/all_gather | solution.py:121
  106.2 1.9 convolution_convert_fusion
  108.1 13.1 %all-to-all-start.2 = ((bf16[32,16,1792]{2,1,0:T(8,128)(2,1)}), bf16[32,16,1792]{2,1,0:T(8,128)(2,1)S(1)}, u32[]{:S(2)}, u32[]{:S(2)}) async-start(bf16[32,16,1792]{2,1,0:T(8,128)(2,1)} %bitcast.21), calls=%async_computation.2 | async-start | bytes 3670016 | tf_op jit(solution)/shard_map/all_to_all | solution.py:47
  121.2 2.4 fusion.6
  123.5 2.1 collective-permute-start.1
  125.7 1.7 collective-permute-done.1
  127.4 2.9 %convolution_convert_fusion.3 = bf16[512,1792]{1,0:T(8,128)(2,1)} fusion(bf16[1,3,1792,128]{3,2,1,0:T(8,128)(2,1)} %param.9, f32[2,512,128]{2,1,0:T(8,128)S(1)} %add.207), kind=kOutput, calls=%fused_computation.3 | convolution fusion | flops 236191744 | bytes 2818048 | tf_op jit(solution)/shard_map/dot_general | solution.py:54
  130.4 15.7 %all-to-all-done.2 = bf16[32,16,1792]{2,1,0:T(8,128)(2,1)S(1)} async-done(((bf16[32,16,1792]{2,1,0:T(8,128)(2,1)}), bf16[32,16,1792]{2,1,0:T(8,128)(2,1)S(1)}, u32[]{:S(2)}, u32[]{:S(2)}) %all-to-all-start.2) | async-done | bytes 1835040 | tf_op jit(solution)/shard_map/all_to_all | solution.py:47
  146.1 1.2 copy-done
  147.3 5.9 %all-to-all-start.3 = ((bf16[32,16,1792]{2,1,0:T(8,128)(2,1)}), bf16[32,16,1792]{2,1,0:T(8,128)(2,1)S(1)}, u32[]{:S(2)}, u32[]{:S(2)}) async-start(bf16[32,16,1792]{2,1,0:T(8,128)(2,1)} %bitcast.108), calls=%async_computation.3 | async-start | bytes 3670016 | tf_op jit(solution)/shard_map/all_to_all | solution.py:47
  155.8 1.3 fusion.72
  157.1 2.5 collective-permute-start.4
  159.7 2.4 fusion.9
  162.0 2.5 collective-permute-start.3
  164.6 8.2 %collective-permute-done.4 = bf16[336,128]{1,0:T(8,128)(2,1)S(1)} collective-permute-done((bf16[336,128]{1,0:T(8,128)(2,1)S(1)}, bf16[336,128]{1,0:T(8,128)(2,1)S(1)}, u32[]{:S(2)}, u32[]{:S(2)}) %collective-permute-start.4) | collective-permute-done | bytes 86048 | tf_op jit(solution)/shard_map/ppermute | solution.py:12
  172.8 1.3 select_select_fusion
  174.2 2.9 %convolution_convert_fusion.2 = bf16[512,1792]{1,0:T(8,128)(2,1)} fusion(bf16[1,3,1792,128]{3,2,1,0:T(8,128)(2,1)} %param.9, f32[2,512,128]{2,1,0:T(8,128)S(1)} %add.213), kind=kOutput, calls=%fused_computation.2 | convolution fusion | flops 236191744 | bytes 2818048 | tf_op jit(solution)/shard_map/dot_general | solution.py:54
  177.1 1.1 all-to-all-done.3
  178.2 6.9 %all-to-all-start.4 = ((bf16[32,16,1792]{2,1,0:T(8,128)(2,1)}), bf16[32,16,1792]{2,1,0:T(8,128)(2,1)}, u32[]{:S(2)}, u32[]{:S(2)}) async-start(bf16[32,16,1792]{2,1,0:T(8,128)(2,1)} %bitcast.107), calls=%async_computation.4 | async-start | bytes 3670016 | tf_op jit(solution)/shard_map/all_to_all | solution.py:47
  186.6 1.5 reshape.277
  188.1 1.4 copy.27
  189.7 1.9 collective-permute-start.5
  191.6 4.1 %collective-permute-start.6 = (bf16[2,128,448]{1,2,0:T(8,128)(2,1)S(1)}, bf16[2,128,448]{1,2,0:T(8,128)(2,1)S(1)}, u32[]{:S(2)}, u32[]{:S(2)}) collective-permute-start(bf16[2,128,448]{1,2,0:T(8,128)(2,1)S(1)} %get-tuple-element.48), channel_id=1, source_target_pairs={{0,2},{1,3},{2,0},{3,1},{4,6},{5,7},{6,4},{7,5},{8,10},{9,11},{10,... | collective-permute-start | bytes 688136 | tf_op jit(solution)/shard_map/ppermute | solution.py:81
  195.7 3.4 %collective-permute-start.7 = (bf16[2,128,448]{1,2,0:T(8,128)(2,1)S(1)}, bf16[2,128,448]{1,2,0:T(8,128)(2,1)S(1)}, u32[]{:S(2)}, u32[]{:S(2)}) collective-permute-start(bf16[2,128,448]{1,2,0:T(8,128)(2,1)S(1)} %get-tuple-element.47), channel_id=1, source_target_pairs={{0,3},{1,2},{2,1},{3,0},{4,7},{5,6},{6,5},{7,4},{8,11},{9,10},{10,... | collective-permute-start | bytes 688136 | tf_op jit(solution)/shard_map/ppermute | solution.py:81
  199.2 3.4 %collective-permute-done.5 = bf16[2,128,448]{1,2,0:T(8,128)(2,1)S(1)} collective-permute-done((bf16[2,128,448]{1,2,0:T(8,128)(2,1)S(1)}, bf16[2,128,448]{1,2,0:T(8,128)(2,1)S(1)}, u32[]{:S(2)}, u32[]{:S(2)}) %collective-permute-start.5) | collective-permute-done | bytes 229408 | tf_op jit(solution)/shard_map/ppermute | solution.py:81
  202.6 8.7 %collective-permute-done.6 = bf16[2,128,448]{1,2,0:T(8,128)(2,1)S(1)} collective-permute-done((bf16[2,128,448]{1,2,0:T(8,128)(2,1)S(1)}, bf16[2,128,448]{1,2,0:T(8,128)(2,1)S(1)}, u32[]{:S(2)}, u32[]{:S(2)}) %collective-permute-start.6) | collective-permute-done | bytes 229408 | tf_op jit(solution)/shard_map/ppermute | solution.py:81
  211.4 2.2 fusion.51
  213.7 2.3 fusion.1
  215.9 1.5 reshape.278
  217.4 1.4 copy.28
  219.0 30.4 %all_to_all.35 = bf16[4,2,128,448]{2,3,1,0:T(8,128)(2,1)S(1)} all-to-all(bf16[4,2,128,448]{2,3,1,0:T(8,128)(2,1)S(1)} %bitcast.110), channel_id=1, replica_groups=mesh['y'=4,'x'=4,'zh'=2,'c'=2,'ma'=2,'mb'=2,'mc'=2] {'mb','mc'}, dimensions={0} | all-to-all | bytes 1835008 | tf_op jit(solution)/shard_map/all_to_all | solution.py:134
  249.4 6.7 %all-to-all-start.6 = ((bf16[16,336,128]{2,1,0:T(8,128)(2,1)}), bf16[16,336,128]{2,1,0:T(8,128)(2,1)S(1)}, u32[]{:S(2)}, u32[]{:S(2)}) async-start(bf16[16,336,128]{2,1,0:T(8,128)(2,1)} %select_select_fusion), calls=%async_computation.6 | async-start | bytes 2752512 | tf_op jit(solution)/shard_map/all_to_all | solution.py:136
  256.1 5.2 %collective-permute-start.8 = (bf16[128,448]{0,1:T(8,128)(2,1)S(1)}, bf16[128,448]{0,1:T(8,128)(2,1)S(1)}, u32[]{:S(2)}, u32[]{:S(2)}) collective-permute-start(bf16[128,448]{0,1:T(8,128)(2,1)S(1)} %dynamic-slice_bitcast_fusion.5), channel_id=1, source_target_pairs={{0,4},{4,0},{1,5},{5,1},{2,6},{6,2},{3,7},{7,3},{8,12},{12,8},{9,1... | collective-permute-start | bytes 344072 | tf_op jit(solution)/shard_map/ppermute | solution.py:12
  261.6 1.9 collective-permute-start.10
  263.5 9.0 %collective-permute-start.9 = (bf16[128,448]{0,1:T(8,128)(2,1)S(1)}, bf16[128,448]{0,1:T(8,128)(2,1)S(1)}, u32[]{:S(2)}, u32[]{:S(2)}) collective-permute-start(bf16[128,448]{0,1:T(8,128)(2,1)S(1)} %get-tuple-element.49), channel_id=1, source_target_pairs={{0,16},{16,0},{1,17},{17,1},{2,18},{18,2},{3,19},{19,3},{4,20},{20... | collective-permute-start | bytes 344072 | tf_op jit(solution)/shard_map/ppermute | solution.py:12
  272.6 1.1 collective-permute-done.8
  273.7 4.1 %collective-permute-done.10 = bf16[128,448]{0,1:T(8,128)(2,1)S(1)} collective-permute-done((bf16[128,448]{0,1:T(8,128)(2,1)S(1)}, bf16[128,448]{0,1:T(8,128)(2,1)S(1)}, u32[]{:S(2)}, u32[]{:S(2)}) %collective-permute-start.10) | collective-permute-done | bytes 114720 | tf_op jit(solution)/shard_map/ppermute | solution.py:145
  277.8 6.8 %collective-permute-done.9 = bf16[128,448]{0,1:T(8,128)(2,1)S(1)} collective-permute-done((bf16[128,448]{0,1:T(8,128)(2,1)S(1)}, bf16[128,448]{0,1:T(8,128)(2,1)S(1)}, u32[]{:S(2)}, u32[]{:S(2)}) %collective-permute-start.9) | collective-permute-done | bytes 114720 | tf_op jit(solution)/shard_map/ppermute | solution.py:12
  285.3 1.1 copy.34
  (39 shorter events, 5.4 us)
Async XLA Ops:
  7.6 39.0 %all-to-all-start = ((bf16[32,16,1792]{2,1,0:T(8,128)(2,1)}), bf16[32,16,1792]{2,1,0:T(8,128)(2,1)S(1)}, u32[]{:S(2)}, u32[]{:S(2)}) async-start(bf16[32,16,1792]{2,1,0:T(8,128)(2,1)} %bitcast.8), calls=%async_computation | async-start | bytes 3670016 | tf_op jit(solution)/shard_map/all_to_all | solution.py:47
  18.1 36.3 %copy-start.2 = (f32[128,2]{0,1:T(2,128)S(1)}, f32[128,2]{0,1:T(2,128)}, u32[]{:S(2)}) copy-start(f32[128,2]{0,1:T(2,128)} %param.8) | copy-start | bytes 3076
  18.1 28.5 %collective-permute-start = (bf16[64,1792]{0,1:T(8,128)(2,1)S(1)}, bf16[64,1792]{0,1:T(8,128)(2,1)S(1)}, u32[]{:S(2)}, u32[]{:S(2)}) collective-permute-start(bf16[64,1792]{0,1:T(8,128)(2,1)S(1)} %constant_dynamic-slice_fusion), channel_id=1, source_target_pairs={{0,16},{16,0},{1,17},{17,1},{2,18},{18,2},{3,19},{19,3},{4,20},{20... | collective-permute-start | bytes 688136 | tf_op jit(solution)/shard_map/ppermute | solution.py:12
  46.6 1.3 copy-start.1
  47.9 60.2 %all-to-all-start.1 = ((bf16[16,336,128]{2,1,0:T(8,128)(2,1)}), bf16[16,336,128]{2,1,0:T(8,128)(2,1)S(1)}, u32[]{:S(2)}, u32[]{:S(2)}) async-start(bf16[16,336,128]{2,1,0:T(8,128)(2,1)} %bitcast), calls=%async_computation.1 | async-start | bytes 2752512 | tf_op jit(solution)/shard_map/all_to_all | solution.py:117
  54.5 51.7 %collective-permute-start.2 = (f32[4,128]{1,0:T(4,128)S(1)}, f32[4,128]{1,0:T(4,128)S(1)}, u32[]{:S(2)}, u32[]{:S(2)}) collective-permute-start(f32[4,128]{1,0:T(4,128)S(1)} %pad_maximum_fusion), channel_id=1, source_target_pairs={{0,16},{16,0},{1,17},{17,1},{2,18},{18,2},{3,19},{19,3},{4,20},{20... | collective-permute-start | bytes 6152 | tf_op jit(solution)/shard_map/ppermute | solution.py:12
  108.1 38.0 %all-to-all-start.2 = ((bf16[32,16,1792]{2,1,0:T(8,128)(2,1)}), bf16[32,16,1792]{2,1,0:T(8,128)(2,1)S(1)}, u32[]{:S(2)}, u32[]{:S(2)}) async-start(bf16[32,16,1792]{2,1,0:T(8,128)(2,1)} %bitcast.21), calls=%async_computation.2 | async-start | bytes 3670016 | tf_op jit(solution)/shard_map/all_to_all | solution.py:47
  123.5 3.8 %collective-permute-start.1 = (f32[2,512,128]{2,1,0:T(8,128)S(1)}, f32[2,512,128]{2,1,0:T(8,128)S(1)}, u32[]{:S(2)}, u32[]{:S(2)}) collective-permute-start(f32[2,512,128]{2,1,0:T(8,128)S(1)} %fusion.6), channel_id=1, source_target_pairs={{0,8},{8,0},{1,9},{9,1},{2,10},{10,2},{3,11},{11,3},{4,12},{12,4},... | collective-permute-start | bytes 1572872 | tf_op jit(solution)/shard_map/ppermute | solution.py:12
  146.1 1.2 copy-start
  147.3 30.9 %all-to-all-start.3 = ((bf16[32,16,1792]{2,1,0:T(8,128)(2,1)}), bf16[32,16,1792]{2,1,0:T(8,128)(2,1)S(1)}, u32[]{:S(2)}, u32[]{:S(2)}) async-start(bf16[32,16,1792]{2,1,0:T(8,128)(2,1)} %bitcast.108), calls=%async_computation.3 | async-start | bytes 3670016 | tf_op jit(solution)/shard_map/all_to_all | solution.py:47
  157.1 15.6 %collective-permute-start.4 = (bf16[336,128]{1,0:T(8,128)(2,1)S(1)}, bf16[336,128]{1,0:T(8,128)(2,1)S(1)}, u32[]{:S(2)}, u32[]{:S(2)}) collective-permute-start(bf16[336,128]{1,0:T(8,128)(2,1)S(1)} %bitcast_select_fusion.1), channel_id=1, source_target_pairs={{0,16},{16,0},{1,17},{17,1},{2,18},{18,2},{3,19},{19,3},{4,20},{20... | collective-permute-start | bytes 258056 | tf_op jit(solution)/shard_map/ppermute | solution.py:12
  162.0 12.1 %collective-permute-start.3 = (f32[2,512,128]{2,1,0:T(8,128)S(1)}, f32[2,512,128]{2,1,0:T(8,128)S(1)}, u32[]{:S(2)}, u32[]{:S(2)}) collective-permute-start(f32[2,512,128]{2,1,0:T(8,128)S(1)} %fusion.9), channel_id=1, source_target_pairs={{0,8},{8,0},{1,9},{9,1},{2,10},{10,2},{3,11},{11,3},{4,12},{12,4},... | collective-permute-start | bytes 1572872 | tf_op jit(solution)/shard_map/ppermute | solution.py:12
  178.2 33.2 %all-to-all-start.4 = ((bf16[32,16,1792]{2,1,0:T(8,128)(2,1)}), bf16[32,16,1792]{2,1,0:T(8,128)(2,1)}, u32[]{:S(2)}, u32[]{:S(2)}) async-start(bf16[32,16,1792]{2,1,0:T(8,128)(2,1)} %bitcast.107), calls=%async_computation.4 | async-start | bytes 3670016 | tf_op jit(solution)/shard_map/all_to_all | solution.py:47
  189.7 12.9 %collective-permute-start.5 = (bf16[2,128,448]{1,2,0:T(8,128)(2,1)S(1)}, bf16[2,128,448]{1,2,0:T(8,128)(2,1)S(1)}, u32[]{:S(2)}, u32[]{:S(2)}) collective-permute-start(bf16[2,128,448]{1,2,0:T(8,128)(2,1)S(1)} %get-tuple-element.46), channel_id=1, source_target_pairs={{0,1},{1,0},{2,3},{3,2},{4,5},{5,4},{6,7},{7,6},{8,9},{9,8},{10,11... | collective-permute-start | bytes 688136 | tf_op jit(solution)/shard_map/ppermute | solution.py:81
  191.6 19.7 %collective-permute-start.6 = (bf16[2,128,448]{1,2,0:T(8,128)(2,1)S(1)}, bf16[2,128,448]{1,2,0:T(8,128)(2,1)S(1)}, u32[]{:S(2)}, u32[]{:S(2)}) collective-permute-start(bf16[2,128,448]{1,2,0:T(8,128)(2,1)S(1)} %get-tuple-element.48), channel_id=1, source_target_pairs={{0,2},{1,3},{2,0},{3,1},{4,6},{5,7},{6,4},{7,5},{8,10},{9,11},{10,... | collective-permute-start | bytes 688136 | tf_op jit(solution)/shard_map/ppermute | solution.py:81
  195.7 15.6 %collective-permute-start.7 = (bf16[2,128,448]{1,2,0:T(8,128)(2,1)S(1)}, bf16[2,128,448]{1,2,0:T(8,128)(2,1)S(1)}, u32[]{:S(2)}, u32[]{:S(2)}) collective-permute-start(bf16[2,128,448]{1,2,0:T(8,128)(2,1)S(1)} %get-tuple-element.47), channel_id=1, source_target_pairs={{0,3},{1,2},{2,1},{3,0},{4,7},{5,6},{6,5},{7,4},{8,11},{9,10},{10,... | collective-permute-start | bytes 688136 | tf_op jit(solution)/shard_map/ppermute | solution.py:81
  249.4 35.9 %all-to-all-start.6 = ((bf16[16,336,128]{2,1,0:T(8,128)(2,1)}), bf16[16,336,128]{2,1,0:T(8,128)(2,1)S(1)}, u32[]{:S(2)}, u32[]{:S(2)}) async-start(bf16[16,336,128]{2,1,0:T(8,128)(2,1)} %select_select_fusion), calls=%async_computation.6 | async-start | bytes 2752512 | tf_op jit(solution)/shard_map/all_to_all | solution.py:136
  256.1 17.6 %collective-permute-start.8 = (bf16[128,448]{0,1:T(8,128)(2,1)S(1)}, bf16[128,448]{0,1:T(8,128)(2,1)S(1)}, u32[]{:S(2)}, u32[]{:S(2)}) collective-permute-start(bf16[128,448]{0,1:T(8,128)(2,1)S(1)} %dynamic-slice_bitcast_fusion.5), channel_id=1, source_target_pairs={{0,4},{4,0},{1,5},{5,1},{2,6},{6,2},{3,7},{7,3},{8,12},{12,8},{9,1... | collective-permute-start | bytes 344072 | tf_op jit(solution)/shard_map/ppermute | solution.py:12
  261.6 16.2 %collective-permute-start.10 = (bf16[128,448]{0,1:T(8,128)(2,1)S(1)}, bf16[128,448]{0,1:T(8,128)(2,1)S(1)}, u32[]{:S(2)}, u32[]{:S(2)}) collective-permute-start(bf16[128,448]{0,1:T(8,128)(2,1)S(1)} %get-tuple-element.50), channel_id=1, source_target_pairs={{0,20},{4,16},{16,4},{20,0},{1,21},{5,17},{17,5},{21,1},{2,22},{6,... | collective-permute-start | bytes 344072 | tf_op jit(solution)/shard_map/ppermute | solution.py:145
  263.5 21.0 %collective-permute-start.9 = (bf16[128,448]{0,1:T(8,128)(2,1)S(1)}, bf16[128,448]{0,1:T(8,128)(2,1)S(1)}, u32[]{:S(2)}, u32[]{:S(2)}) collective-permute-start(bf16[128,448]{0,1:T(8,128)(2,1)S(1)} %get-tuple-element.49), channel_id=1, source_target_pairs={{0,16},{16,0},{1,17},{17,1},{2,18},{18,2},{3,19},{19,3},{4,20},{20... | collective-permute-start | bytes 344072 | tf_op jit(solution)/shard_map/ppermute | solution.py:12

commit v5 on v4

--- a/solution.py
+++ b/solution.py
@@ -5,11 +5,16 @@
 
 PLANE = ("y", "x", "c")
 NEAR = ("mb", "mc")
+RING = ("zh", "ma", "mb", "mc")
 CAP = 16
 
 
 def swap(value, axis):
     return lax.ppermute(value, axis, [(0, 1), (1, 0)])
+
+
+def mirrored(value):
+    return lax.ppermute(value, RING, [(i, 15 - i) for i in range(16)])
 
 
 def place_codes(routes, gate_values, owner):
@@ -67,19 +72,9 @@
     )
 
 
-def by_columns(mixed, near):
-    tok_rows = mixed.shape[0] // 2
-    parts = mixed.astype(jnp.bfloat16).reshape(2, tok_rows, 2, near, -1)
-    return jnp.transpose(parts, (3, 2, 1, 0, 4)).reshape(near, 2, tok_rows, -1)
-
-
-def near_sum(parts, place):
-    total = lax.dynamic_index_in_dim(parts, place, 0, keepdims=False).astype(jnp.float32)
-    count = parts.shape[0]
-    for step in range(1, count):
-        block = lax.dynamic_index_in_dim(parts, place ^ step, 0, keepdims=False)
-        total += lax.ppermute(block, NEAR, [(i, i ^ step) for i in range(count)]).astype(jnp.float32)
-    return total
+def by_columns(mixed, groups):
+    parts = mixed.astype(jnp.bfloat16).reshape(2, mixed.shape[0] // 2, groups, -1)
+    return jnp.transpose(parts, (2, 1, 0, 3)).reshape(groups, mixed.shape[0] // 2, -1)
 
 
 tied = lax.optimization_barrier
@@ -100,50 +95,41 @@
 
 
 def shards(tokens, routes, gate_values, expert_weights, old_owner, new_owner):
-    zh, far, place = lax.axis_index("zh"), lax.axis_index("ma"), lax.axis_index(NEAR)
+    zh, place = lax.axis_index("zh"), lax.axis_index(NEAR)
     near = lax.axis_size(NEAR)
     tok_rows = tokens.shape[0]
     own = expert_weights[0]
     table = jnp.transpose(tokens.reshape(tok_rows, 2 * near, 2, -1), (2, 0, 1, 3)).reshape(2 * tok_rows, -1)
     share = 2 * tok_rows // near
-    part = lax.dynamic_slice_in_dim(table, place * share, share, 0)
+    part = lax.dynamic_slice_in_dim(table, (near - 1 - place) * share, share, 0)
     codes = place_codes(routes, gate_values, old_owner)
     rows = placed_rows(codes, zh)
     part, payload = tied((part, gather_rows(rows, table)))
-    quarter = swap(part, "zh")
+    quarter = mirrored(part)
     sent = exchange(payload)
-    chips = lax.axis_size("y") * lax.axis_size("x")
-    pieces, sent, quarter = tied((own.reshape(chips, -1, own.shape[-1]), sent, quarter))
-    spread = lax.all_to_all(pieces, ("y", "x"), split_axis=0, concat_axis=0, tiled=True)
-    quarter, later_codes = tied((quarter, codes))
-    other_codes = swap(later_codes, "zh")
+    sent, quarter = tied((sent, quarter))
+    quarter, payload, later_codes = tied((quarter, expert_part(sent, own), codes))
+    back = exchange(payload)
+    other_codes = mirrored(later_codes)
     other_rows = placed_rows(other_codes, zh)
     other_table = lax.all_gather(quarter, NEAR, tiled=True)
-    payload, spread = tied((gather_rows(other_rows, other_table), spread))
+    payload, back = tied((gather_rows(other_rows, other_table), back))
     other_sent = exchange(payload)
-    payload, other_sent = tied((expert_part(sent, own), other_sent))
-    back = exchange(payload)
+
+    mixed = by_columns(weighted(back, codes, rows), 2 * near)
+    both = jnp.zeros((4 * near,) + mixed.shape[1:], mixed.dtype)
+    both = lax.dynamic_update_slice_in_dim(both, mixed, zh * 2 * near, 0)
+    both, other_sent = tied((both, other_sent))
+    other_back = exchange(expert_part(other_sent, own))
+    chips = lax.axis_size("y") * lax.axis_size("x")
+    pieces, other_back = tied((own.reshape(chips, -1, own.shape[-1]), other_back))
+    spread = lax.all_to_all(pieces, ("y", "x"), split_axis=0, concat_axis=0, tiled=True)
+    other_mixed = by_columns(weighted(other_back, other_codes, other_rows), 2 * near)
+    both = lax.dynamic_update_slice_in_dim(both, other_mixed, (1 - zh) * 2 * near, 0)
+    out = lax.psum_scatter(both, RING, scatter_dimension=0, tiled=True)[0]
     chosen = pick_pieces(spread, old_owner, new_owner, zh)
-    payload, back, chosen = tied((expert_part(other_sent, own), back, chosen))
-    other_back = exchange(payload)
-
-    parts = by_columns(weighted(back, codes, rows), near)
-    kept = near_sum(parts, place).astype(jnp.bfloat16)
-    other_back, kept = tied((other_back, kept))
-    other_parts = by_columns(weighted(other_back, other_codes, other_rows), near)
-    near_parts = lax.all_to_all(other_parts, NEAR, split_axis=0, concat_axis=0, tiled=True)
-    near_parts, chosen = tied((near_parts, chosen))
     arrived = lax.all_to_all(chosen, ("y", "x"), split_axis=0, concat_axis=0, tiled=True)
-    other_kept = jnp.sum(near_parts.astype(jnp.float32), axis=0).astype(jnp.bfloat16)
-
-    def of(value, index):
-        return lax.dynamic_index_in_dim(value, index, 0, keepdims=False)
-
-    total = of(kept, far).astype(jnp.float32)
-    total += swap(of(kept, 1 - far), "ma").astype(jnp.float32)
-    total += swap(of(other_kept, far), "zh").astype(jnp.float32)
-    total += lax.ppermute(of(other_kept, 1 - far), ("zh", "ma"), [(i, i ^ 3) for i in range(4)]).astype(jnp.float32)
-    return total.astype(jnp.bfloat16), arrived.reshape(expert_weights.shape)
+    return out, arrived.reshape(expert_weights.shape)
 
 
 def solution(mesh):

time: 290 us -> 275 us (0.948)
  waiting for transfers between devices: 65.7 us -> 113 us
  starting transfers between devices: 108 us -> 62.8 us
  blocking collectives: 69.9 us -> 45.4 us
  between operations: 3.68 us -> 16.8 us
  matrix products: 21.4 us -> 17.9 us
    ppermute x7 -> x3, starting transfers between devices: 46.9 us -> 13.5 us  [swap(): return lax.ppermute(value, axis, [(0, 1), (1, 0)])]
    all_to_all x4, waiting for transfers between devices: 16.8 us -> 42.9 us  [exchange(): lax.all_to_all(blocks, axes, split_axis=0, concat_axis=0, tiled=True)]
    ppermute x4 -> x2, waiting for transfers between devices: 16.2 us -> 40.2 us  [mirrored(): return lax.ppermute(value, RING, [(i, 15 - i) for i in range(16)])]
    all_gather x1, blocking collectives: 39.5 us -> 18 us  [shards(): other_table = lax.all_gather(quarter, NEAR, tiled=True)]
    ppermute x7 -> x3, waiting for transfers between devices: 32.7 us -> 13.3 us  [swap(): return lax.ppermute(value, axis, [(0, 1), (1, 0)])]
    all_to_all x1, waiting for transfers between devices: 0.01 us -> 16.6 us  [shards(): lax.all_to_all(pieces, ('y', 'x'), split_axis=0, concat_axis=0, tiled=True)]
    all_to_all x1 -> x0, starting transfers between devices: 6.69 us -> none  [shards(): lax.all_to_all(chosen, ('y', 'x'), split_axis=0, concat_axis=0, tiled=True)]
    all_to_all x4, starting transfers between devices: 36.4 us -> 30.8 us  [exchange(): lax.all_to_all(blocks, axes, split_axis=0, concat_axis=0, tiled=True)]
  transfers between devices with their start and end apart: 17 -> 11, of which waited for: 10 -> 8; matrix products, arithmetic and copies ran while one was open for 7% -> 4% of each run, Pallas kernels for 0% -> 0%
where the time goes in v5:
time: 275 us; the launch traced here: 272 us
  waiting for transfers between devices  113 us (41%)
  starting transfers between devices  62.8 us (23%)
  blocking collectives  45.4 us (17%)
  matrix products  17.9 us (7%)
  between operations  16.8 us (6%)
  local copies, waits for them, and re-layouts  13 us (5%)
  other arithmetic  3.16 us (1%)
    all_to_all x4, waiting for transfers between devices, exchange(): lax.all_to_all(blocks, axes, split_axis=0, concat_axis=0, tiled=True)  42.9 us
    ppermute x2, waiting for transfers between devices, mirrored(): return lax.ppermute(value, RING, [(i, 15 - i) for i in range(16)])  40.2 us
    all_to_all x4, starting transfers between devices, exchange(): lax.all_to_all(blocks, axes, split_axis=0, concat_axis=0, tiled=True)  30.8 us
    all_to_all x1, blocking collectives, shards(): lax.all_to_all(chosen, ('y', 'x'), split_axis=0, concat_axis=0, tiled=True)  27.4 us
    all_gather x1, blocking collectives, shards(): other_table = lax.all_gather(quarter, NEAR, tiled=True)  18 us
    all_to_all x1, waiting for transfers between devices, shards(): lax.all_to_all(pieces, ('y', 'x'), split_axis=0, concat_axis=0, tiled=True)  16.6 us
    ppermute x2, starting transfers between devices, mirrored(): return lax.ppermute(value, RING, [(i, 15 - i) for i in range(16)])  13.8 us
    ppermute x3, starting transfers between devices, swap(): return lax.ppermute(value, axis, [(0, 1), (1, 0)])  13.5 us
  transfers between devices with their start and end apart: 11, of which 8 were waited for; matrix products, arithmetic and copies ran while one was open for 4% of the time, Pallas kernels for 0%

profile of v5, /device:TPU:1, one launch (start us, length us, event | category | flops | bytes accessed | tf_op | source)
XLA Modules:
  0.0 272.1 jit_solution(2233193359819270183)
XLA Ops:
  7.2 1.3 fusion.64
  8.5 1.0 fusion.13
  9.5 1.6 copy.20
  11.0 0.8 copy.21
  11.8 0.1 copy.32
  12.0 0.2 constant_dynamic-slice_fusion
  12.2 2.0 convolution_convert_fusion.1
  14.1 10.5 %all-to-all-start = ((bf16[32,16,1792]{2,1,0:T(8,128)(2,1)}), bf16[32,16,1792]{2,1,0:T(8,128)(2,1)S(1)}, u32[]{:S(2)}, u32[]{:S(2)}) async-start(bf16[32,16,1792]{2,1,0:T(8,128)(2,1)} %bitcast.10), calls=%async_computation | async-start | bytes 3670016 | tf_op jit(solution)/shard_map/all_to_all | solution.py:52
  24.7 9.2 %collective-permute-start = (bf16[64,1792]{0,1:T(8,128)(2,1)S(1)}, bf16[64,1792]{0,1:T(8,128)(2,1)S(1)}, u32[]{:S(2)}, u32[]{:S(2)}) collective-permute-start(bf16[64,1792]{0,1:T(8,128)(2,1)S(1)} %constant_dynamic-slice_fusion), channel_id=1, source_target_pairs={{0,23},{1,22},{2,21},{3,20},{4,19},{5,18},{6,17},{7,16},{16,7},{17... | collective-permute-start | bytes 688136 | tf_op jit(solution)/shard_map/ppermute | solution.py:17
  33.9 40.2 %collective-permute-done = bf16[64,1792]{0,1:T(8,128)(2,1)S(1)} collective-permute-done((bf16[64,1792]{0,1:T(8,128)(2,1)S(1)}, bf16[64,1792]{0,1:T(8,128)(2,1)S(1)}, u32[]{:S(2)}, u32[]{:S(2)}) %collective-permute-start) | collective-permute-done | bytes 229408 | tf_op jit(solution)/shard_map/ppermute | solution.py:17
  74.1 1.8 fusion.6
  75.9 2.6 collective-permute-start.1
  78.6 1.5 collective-permute-done.1
  80.2 2.9 %convolution_convert_fusion.3 = bf16[512,1792]{1,0:T(8,128)(2,1)} fusion(bf16[1,3,1792,128]{3,2,1,0:T(8,128)(2,1)} %param.9, f32[2,512,128]{2,1,0:T(8,128)S(1)} %add.175), kind=kOutput, calls=%fused_computation.3 | convolution fusion | flops 236191744 | bytes 2818048 | tf_op jit(solution)/shard_map/dot_general | solution.py:59
  83.1 7.4 %all-to-all-start.1 = ((bf16[32,16,1792]{2,1,0:T(8,128)(2,1)}), bf16[32,16,1792]{2,1,0:T(8,128)(2,1)S(1)}, u32[]{:S(2)}, u32[]{:S(2)}) async-start(bf16[32,16,1792]{2,1,0:T(8,128)(2,1)} %bitcast.92), calls=%async_computation.1 | async-start | bytes 3670016 | tf_op jit(solution)/shard_map/all_to_all | solution.py:52
  90.5 4.6 %collective-permute-start.2 = (f32[4,128]{1,0:T(4,128)S(1)}, f32[4,128]{1,0:T(4,128)S(1)}, u32[]{:S(2)}, u32[]{:S(2)}) collective-permute-start(f32[4,128]{1,0:T(4,128)S(1)} %pad_maximum_fusion), channel_id=1, source_target_pairs={{0,23},{1,22},{2,21},{3,20},{4,19},{5,18},{6,17},{7,16},{16,7},{17... | collective-permute-start | bytes 6152 | tf_op jit(solution)/shard_map/ppermute | solution.py:17
  95.1 0.2 copy.22
  95.3 18.0 %all_gather.3 = bf16[256,1792]{1,0:T(8,128)(2,1)S(1)} all-gather(bf16[64,1792]{1,0:T(8,128)(2,1)S(1)} %copy.22), channel_id=1, replica_groups=mesh['y'=4,'x'=4,'zh'=2,'c'=2,'ma'=2,'mb'=2,'mc'=2] {'mb','mc'}, dimensions={0}, use_global_device_ids=true | all-gather | bytes 1146880 | tf_op jit(solution)/shard_map/all_gather | solution.py:115
  113.3 1.9 convolution_convert_fusion
  115.3 0.1 all-to-all-done.1
  115.4 8.9 %all-to-all-start.2 = ((bf16[32,16,1792]{2,1,0:T(8,128)(2,1)}), bf16[32,16,1792]{2,1,0:T(8,128)(2,1)}, u32[]{:S(2)}, u32[]{:S(2)}) async-start(bf16[32,16,1792]{2,1,0:T(8,128)(2,1)} %bitcast.94), calls=%async_computation.2 | async-start | bytes 3670016 | tf_op jit(solution)/shard_map/all_to_all | solution.py:52
  124.3 0.7 fusion.45
  125.1 0.8 fusion
  125.8 1.5 reshape.271
  127.4 1.1 copy.27
  128.6 1.6 broadcast_in_dim.96
  130.2 1.0 constant_dynamic-update-slice_fusion.1
  131.2 18.1 %all-to-all-done.2 = bf16[32,16,1792]{2,1,0:T(8,128)(2,1)} async-done(((bf16[32,16,1792]{2,1,0:T(8,128)(2,1)}), bf16[32,16,1792]{2,1,0:T(8,128)(2,1)}, u32[]{:S(2)}, u32[]{:S(2)}) %all-to-all-start.2) | async-done | bytes 1835040 | tf_op jit(solution)/shard_map/all_to_all | solution.py:52
  149.3 2.4 fusion.9
  151.7 4.2 %collective-permute-start.3 = (f32[2,512,128]{2,1,0:T(8,128)S(1)}, f32[2,512,128]{2,1,0:T(8,128)S(1)}, u32[]{:S(2)}, u32[]{:S(2)}) collective-permute-start(f32[2,512,128]{2,1,0:T(8,128)S(1)} %fusion.9), channel_id=1, source_target_pairs={{0,8},{8,0},{1,9},{9,1},{2,10},{10,2},{3,11},{11,3},{4,12},{12,4},... | collective-permute-start | bytes 1572872 | tf_op jit(solution)/shard_map/ppermute | solution.py:13
  155.8 1.5 collective-permute-done.3
  157.4 3.0 %convolution_convert_fusion.2 = bf16[512,1792]{1,0:T(8,128)(2,1)} fusion(bf16[1,3,1792,128]{3,2,1,0:T(8,128)(2,1)} %param.9, f32[2,512,128]{2,1,0:T(8,128)S(1)} %add.184), kind=kOutput, calls=%fused_computation.2 | convolution fusion | flops 236191744 | bytes 2818048 | tf_op jit(solution)/shard_map/dot_general | solution.py:59
  160.4 4.0 %all-to-all-start.3 = ((bf16[32,16,1792]{2,1,0:T(8,128)(2,1)}), bf16[32,16,1792]{2,1,0:T(8,128)(2,1)S(1)}, u32[]{:S(2)}, u32[]{:S(2)}) async-start(bf16[32,16,1792]{2,1,0:T(8,128)(2,1)} %bitcast.93), calls=%async_computation.3 | async-start | bytes 3670016 | tf_op jit(solution)/shard_map/all_to_all | solution.py:52
  164.4 0.2 reduce-scatter.2.cloned.1.call-start
  164.7 24.7 %all-to-all-done.3 = bf16[32,16,1792]{2,1,0:T(8,128)(2,1)S(1)} async-done(((bf16[32,16,1792]{2,1,0:T(8,128)(2,1)}), bf16[32,16,1792]{2,1,0:T(8,128)(2,1)S(1)}, u32[]{:S(2)}, u32[]{:S(2)}) %all-to-all-start.3) | async-done | bytes 1835040 | tf_op jit(solution)/shard_map/all_to_all | solution.py:52
  189.4 0.7 fusion.48
  190.1 0.8 fusion.1
  190.9 1.5 reshape.272
  192.4 1.1 copy.28
  193.6 1.0 constant_dynamic-update-slice_fusion
  194.7 4.5 %all-to-all-start.4 = ((bf16[16,336,128]{2,1,0:T(8,128)(2,1)}), bf16[16,336,128]{2,1,0:T(8,128)(2,1)S(1)}, u32[]{:S(2)}, u32[]{:S(2)}) async-start(bf16[16,336,128]{2,1,0:T(8,128)(2,1)} %bitcast.30), calls=%async_computation.5 | async-start | bytes 2752512 | tf_op jit(solution)/shard_map/all_to_all | solution.py:126
  201.7 16.6 %all-to-all-done.4 = bf16[16,336,128]{2,1,0:T(8,128)(2,1)S(1)} async-done(((bf16[16,336,128]{2,1,0:T(8,128)(2,1)}), bf16[16,336,128]{2,1,0:T(8,128)(2,1)S(1)}, u32[]{:S(2)}, u32[]{:S(2)}) %all-to-all-start.4) | async-done | bytes 1376288 | tf_op jit(solution)/shard_map/all_to_all | solution.py:126
  218.2 6.7 %collective-permute-start.4 = (bf16[336,128]{1,0:T(8,128)(2,1)S(1)}, bf16[336,128]{1,0:T(8,128)(2,1)S(1)}, u32[]{:S(2)}, u32[]{:S(2)}) collective-permute-start(bf16[336,128]{1,0:T(8,128)(2,1)S(1)} %bitcast_select_fusion.1), channel_id=1, source_target_pairs={{0,16},{16,0},{1,17},{17,1},{2,18},{18,2},{3,19},{19,3},{4,20},{20... | collective-permute-start | bytes 258056 | tf_op jit(solution)/shard_map/ppermute | solution.py:13
  224.9 1.2 fusion.66
  226.1 10.3 %collective-permute-done.4 = bf16[336,128]{1,0:T(8,128)(2,1)S(1)} collective-permute-done((bf16[336,128]{1,0:T(8,128)(2,1)S(1)}, bf16[336,128]{1,0:T(8,128)(2,1)S(1)}, u32[]{:S(2)}, u32[]{:S(2)}) %collective-permute-start.4) | collective-permute-done | bytes 86048 | tf_op jit(solution)/shard_map/ppermute | solution.py:13
  236.4 0.3 select_select_fusion
  236.8 27.4 %all_to_all.30 = bf16[16,336,128]{2,1,0:T(8,128)(2,1)S(1)} all-to-all(bf16[16,336,128]{2,1,0:T(8,128)(2,1)S(1)} %select_select_fusion), channel_id=1, replica_groups=mesh['y'=4,'x'=4,'zh'=2,'c'=2,'ma'=2,'mb'=2,'mc'=2] {'y','x'}, dimensions={0} | all-to-all | bytes 2752512 | tf_op jit(solution)/shard_map/all_to_all | solution.py:131
  264.2 1.1 copy.36
  (21 shorter events, 0.6 us)
Async XLA Ops:
  14.1 60.0 %all-to-all-start = ((bf16[32,16,1792]{2,1,0:T(8,128)(2,1)}), bf16[32,16,1792]{2,1,0:T(8,128)(2,1)S(1)}, u32[]{:S(2)}, u32[]{:S(2)}) async-start(bf16[32,16,1792]{2,1,0:T(8,128)(2,1)} %bitcast.10), calls=%async_computation | async-start | bytes 3670016 | tf_op jit(solution)/shard_map/all_to_all | solution.py:52
  24.7 49.4 %collective-permute-start = (bf16[64,1792]{0,1:T(8,128)(2,1)S(1)}, bf16[64,1792]{0,1:T(8,128)(2,1)S(1)}, u32[]{:S(2)}, u32[]{:S(2)}) collective-permute-start(bf16[64,1792]{0,1:T(8,128)(2,1)S(1)} %constant_dynamic-slice_fusion), channel_id=1, source_target_pairs={{0,23},{1,22},{2,21},{3,20},{4,19},{5,18},{6,17},{7,16},{16,7},{17... | collective-permute-start | bytes 688136 | tf_op jit(solution)/shard_map/ppermute | solution.py:17
  74.1 4.5 %copy-start = (f32[128,2]{0,1:T(2,128)S(1)}, f32[128,2]{0,1:T(2,128)}, u32[]{:S(2)}) copy-start(f32[128,2]{0,1:T(2,128)} %param.8) | copy-start | bytes 3076
  75.9 4.2 %collective-permute-start.1 = (f32[2,512,128]{2,1,0:T(8,128)S(1)}, f32[2,512,128]{2,1,0:T(8,128)S(1)}, u32[]{:S(2)}, u32[]{:S(2)}) collective-permute-start(f32[2,512,128]{2,1,0:T(8,128)S(1)} %fusion.6), channel_id=1, source_target_pairs={{0,8},{8,0},{1,9},{9,1},{2,10},{10,2},{3,11},{11,3},{4,12},{12,4},... | collective-permute-start | bytes 1572872 | tf_op jit(solution)/shard_map/ppermute | solution.py:13
  83.1 32.3 %all-to-all-start.1 = ((bf16[32,16,1792]{2,1,0:T(8,128)(2,1)}), bf16[32,16,1792]{2,1,0:T(8,128)(2,1)S(1)}, u32[]{:S(2)}, u32[]{:S(2)}) async-start(bf16[32,16,1792]{2,1,0:T(8,128)(2,1)} %bitcast.92), calls=%async_computation.1 | async-start | bytes 3670016 | tf_op jit(solution)/shard_map/all_to_all | solution.py:52
  90.5 22.8 %collective-permute-start.2 = (f32[4,128]{1,0:T(4,128)S(1)}, f32[4,128]{1,0:T(4,128)S(1)}, u32[]{:S(2)}, u32[]{:S(2)}) collective-permute-start(f32[4,128]{1,0:T(4,128)S(1)} %pad_maximum_fusion), channel_id=1, source_target_pairs={{0,23},{1,22},{2,21},{3,20},{4,19},{5,18},{6,17},{7,16},{16,7},{17... | collective-permute-start | bytes 6152 | tf_op jit(solution)/shard_map/ppermute | solution.py:17
  115.4 33.9 %all-to-all-start.2 = ((bf16[32,16,1792]{2,1,0:T(8,128)(2,1)}), bf16[32,16,1792]{2,1,0:T(8,128)(2,1)}, u32[]{:S(2)}, u32[]{:S(2)}) async-start(bf16[32,16,1792]{2,1,0:T(8,128)(2,1)} %bitcast.94), calls=%async_computation.2 | async-start | bytes 3670016 | tf_op jit(solution)/shard_map/all_to_all | solution.py:52
  151.7 5.7 %collective-permute-start.3 = (f32[2,512,128]{2,1,0:T(8,128)S(1)}, f32[2,512,128]{2,1,0:T(8,128)S(1)}, u32[]{:S(2)}, u32[]{:S(2)}) collective-permute-start(f32[2,512,128]{2,1,0:T(8,128)S(1)} %fusion.9), channel_id=1, source_target_pairs={{0,8},{8,0},{1,9},{9,1},{2,10},{10,2},{3,11},{11,3},{4,12},{12,4},... | collective-permute-start | bytes 1572872 | tf_op jit(solution)/shard_map/ppermute | solution.py:13
  160.4 29.0 %all-to-all-start.3 = ((bf16[32,16,1792]{2,1,0:T(8,128)(2,1)}), bf16[32,16,1792]{2,1,0:T(8,128)(2,1)S(1)}, u32[]{:S(2)}, u32[]{:S(2)}) async-start(bf16[32,16,1792]{2,1,0:T(8,128)(2,1)} %bitcast.93), calls=%async_computation.3 | async-start | bytes 3670016 | tf_op jit(solution)/shard_map/all_to_all | solution.py:52
  164.4 99.8 %reduce-scatter.2.cloned.1.call-start = ((), (), s32[]{:S(2)}) async-start(), calls=%async_computation.7 | async-start | bytes 1949696 | tf_op jit(solution)/shard_map/reduce_scatter | solution.py:129
  194.7 23.5 %all-to-all-start.4 = ((bf16[16,336,128]{2,1,0:T(8,128)(2,1)}), bf16[16,336,128]{2,1,0:T(8,128)(2,1)S(1)}, u32[]{:S(2)}, u32[]{:S(2)}) async-start(bf16[16,336,128]{2,1,0:T(8,128)(2,1)} %bitcast.30), calls=%async_computation.5 | async-start | bytes 2752512 | tf_op jit(solution)/shard_map/all_to_all | solution.py:126
  218.2 18.2 %collective-permute-start.4 = (bf16[336,128]{1,0:T(8,128)(2,1)S(1)}, bf16[336,128]{1,0:T(8,128)(2,1)S(1)}, u32[]{:S(2)}, u32[]{:S(2)}) collective-permute-start(bf16[336,128]{1,0:T(8,128)(2,1)S(1)} %bitcast_select_fusion.1), channel_id=1, source_target_pairs={{0,16},{16,0},{1,17},{17,1},{2,18},{18,2},{3,19},{19,3},{4,20},{20... | collective-permute-start | bytes 258056 | tf_op jit(solution)/shard_map/ppermute | solution.py:13
Sparse Core Ops, SparseCore 0:
  194.8 59.6 reduce-scatter.1

commit v6 on v5

--- a/solution.py
+++ b/solution.py
@@ -1,6 +1,7 @@
 import jax
 import jax.numpy as jnp
 from jax import lax
+from jax.experimental.layout import Layout, with_layout_constraint
 from jax.sharding import Mesh, PartitionSpec as P
 
 PLANE = ("y", "x", "c")
@@ -100,6 +101,7 @@
     tok_rows = tokens.shape[0]
     own = expert_weights[0]
     table = jnp.transpose(tokens.reshape(tok_rows, 2 * near, 2, -1), (2, 0, 1, 3)).reshape(2 * tok_rows, -1)
+    table = with_layout_constraint(table, Layout(major_to_minor=(0, 1)))
     share = 2 * tok_rows // near
     part = lax.dynamic_slice_in_dim(table, (near - 1 - place) * share, share, 0)
     codes = place_codes(routes, gate_values, old_owner)

time: 275 us -> 256 us (0.931)
  waiting for transfers between devices: 113 us -> 96.5 us
    ppermute x2, waiting for transfers between devices: 40.2 us -> 20.6 us  [mirrored(): return lax.ppermute(value, RING, [(i, 15 - i) for i in range(16)])]
where the time goes in v6:
time: 256 us; the launch traced here: 255 us
  waiting for transfers between devices  96.5 us (38%)
  starting transfers between devices  62.8 us (25%)
  blocking collectives  43.8 us (17%)
  matrix products  17.9 us (7%)
  between operations  16.8 us (7%)
  local copies, waits for them, and re-layouts  14 us (5%)
  other arithmetic  3.16 us (1%)
    all_to_all x4, waiting for transfers between devices, exchange(): lax.all_to_all(blocks, axes, split_axis=0, concat_axis=0, tiled=True)  43.5 us
    all_to_all x4, starting transfers between devices, exchange(): lax.all_to_all(blocks, axes, split_axis=0, concat_axis=0, tiled=True)  31.8 us
    all_to_all x1, blocking collectives, shards(): lax.all_to_all(chosen, ('y', 'x'), split_axis=0, concat_axis=0, tiled=True)  26 us
    ppermute x2, waiting for transfers between devices, mirrored(): return lax.ppermute(value, RING, [(i, 15 - i) for i in range(16)])  20.6 us
    all_gather x1, blocking collectives, shards(): other_table = lax.all_gather(quarter, NEAR, tiled=True)  17.8 us
    all_to_all x1, waiting for transfers between devices, shards(): lax.all_to_all(pieces, ('y', 'x'), split_axis=0, concat_axis=0, tiled=True)  16.6 us
    ppermute x3, waiting for transfers between devices, swap(): return lax.ppermute(value, axis, [(0, 1), (1, 0)])  15.8 us
    ppermute x2, starting transfers between devices, mirrored(): return lax.ppermute(value, RING, [(i, 15 - i) for i in range(16)])  13.8 us
  transfers between devices with their start and end apart: 11, of which 8 were waited for; matrix products, arithmetic and copies ran while one was open for 4% of the time, Pallas kernels for 0%

profile of v6, /device:TPU:1, one launch (start us, length us, event | category | flops | bytes accessed | tf_op | source)
XLA Modules:
  0.0 254.9 jit_solution(7778292624296561512)
XLA Ops:
  7.2 1.3 fusion.64
  8.5 1.0 fusion.13
  9.5 1.6 copy.16
  11.0 0.9 copy.23
  11.9 1.3 reshape.271
  13.3 1.9 convolution_convert_fusion.1
  15.2 10.5 %all-to-all-start = ((bf16[32,16,1792]{2,1,0:T(8,128)(2,1)}), bf16[32,16,1792]{2,1,0:T(8,128)(2,1)S(1)}, u32[]{:S(2)}, u32[]{:S(2)}) async-start(bf16[32,16,1792]{2,1,0:T(8,128)(2,1)} %bitcast.10), calls=%async_computation | async-start | bytes 3670016 | tf_op jit(solution)/shard_map/all_to_all | solution.py:53
  25.8 9.2 %collective-permute-start = (bf16[64,1792]{1,0:T(8,128)(2,1)S(1)}, bf16[64,1792]{1,0:T(8,128)(2,1)S(1)}, u32[]{:S(2)}, u32[]{:S(2)}) collective-permute-start(bf16[64,1792]{1,0:T(8,128)(2,1)S(1)} %constant_dynamic-slice_fusion), channel_id=1, source_target_pairs={{0,23},{1,22},{2,21},{3,20},{4,19},{5,18},{6,17},{7,16},{16,7},{17... | collective-permute-start | bytes 688136 | tf_op jit(solution)/shard_map/ppermute | solution.py:18
  35.0 20.6 %collective-permute-done = bf16[64,1792]{1,0:T(8,128)(2,1)S(1)} collective-permute-done((bf16[64,1792]{1,0:T(8,128)(2,1)S(1)}, bf16[64,1792]{1,0:T(8,128)(2,1)S(1)}, u32[]{:S(2)}, u32[]{:S(2)}) %collective-permute-start) | collective-permute-done | bytes 229408 | tf_op jit(solution)/shard_map/ppermute | solution.py:18
  55.5 1.8 fusion.6
  57.4 2.6 %collective-permute-start.1 = (f32[2,512,128]{2,1,0:T(8,128)S(1)}, f32[2,512,128]{2,1,0:T(8,128)S(1)}, u32[]{:S(2)}, u32[]{:S(2)}) collective-permute-start(f32[2,512,128]{2,1,0:T(8,128)S(1)} %fusion.6), channel_id=1, source_target_pairs={{0,8},{8,0},{1,9},{9,1},{2,10},{10,2},{3,11},{11,3},{4,12},{12,4},... | collective-permute-start | bytes 1572872 | tf_op jit(solution)/shard_map/ppermute | solution.py:14
  60.0 1.5 collective-permute-done.1
  61.5 0.1 add.175
  61.6 2.9 %convolution_convert_fusion.3 = bf16[512,1792]{1,0:T(8,128)(2,1)} fusion(bf16[1,3,1792,128]{3,2,1,0:T(8,128)(2,1)} %param.9, f32[2,512,128]{2,1,0:T(8,128)S(1)} %add.175), kind=kOutput, calls=%fused_computation.3 | convolution fusion | flops 236191744 | bytes 2818048 | tf_op jit(solution)/shard_map/dot_general | solution.py:60
  64.5 7.4 %all-to-all-start.1 = ((bf16[32,16,1792]{2,1,0:T(8,128)(2,1)}), bf16[32,16,1792]{2,1,0:T(8,128)(2,1)S(1)}, u32[]{:S(2)}, u32[]{:S(2)}) async-start(bf16[32,16,1792]{2,1,0:T(8,128)(2,1)} %bitcast.85), calls=%async_computation.1 | async-start | bytes 3670016 | tf_op jit(solution)/shard_map/all_to_all | solution.py:53
  71.9 4.6 %collective-permute-start.2 = (f32[4,128]{1,0:T(4,128)S(1)}, f32[4,128]{1,0:T(4,128)S(1)}, u32[]{:S(2)}, u32[]{:S(2)}) collective-permute-start(f32[4,128]{1,0:T(4,128)S(1)} %pad_maximum_fusion), channel_id=1, source_target_pairs={{0,23},{1,22},{2,21},{3,20},{4,19},{5,18},{6,17},{7,16},{16,7},{17... | collective-permute-start | bytes 6152 | tf_op jit(solution)/shard_map/ppermute | solution.py:18
  76.5 17.8 %all_gather.3 = bf16[256,1792]{1,0:T(8,128)(2,1)S(1)} all-gather(bf16[64,1792]{1,0:T(8,128)(2,1)S(1)} %collective-permute-done), channel_id=1, replica_groups=mesh['y'=4,'x'=4,'zh'=2,'c'=2,'ma'=2,'mb'=2,'mc'=2] {'mb','mc'}, dimensions={0}, use_global_device_ids=true | all-gather | bytes 1146880 | tf_op jit(solution)/shard_map/all_gather | solution.py:117
  94.3 1.9 convolution_convert_fusion
  96.3 0.6 all-to-all-done.1
  96.8 9.7 %all-to-all-start.2 = ((bf16[32,16,1792]{2,1,0:T(8,128)(2,1)}), bf16[32,16,1792]{2,1,0:T(8,128)(2,1)}, u32[]{:S(2)}, u32[]{:S(2)}) async-start(bf16[32,16,1792]{2,1,0:T(8,128)(2,1)} %bitcast.87), calls=%async_computation.2 | async-start | bytes 3670016 | tf_op jit(solution)/shard_map/all_to_all | solution.py:53
  106.5 0.8 fusion.45
  107.3 0.8 fusion
  108.1 1.5 reshape.272
  109.6 1.1 copy.25
  110.6 0.1 copy.20
  110.8 1.6 broadcast_in_dim.96
  112.4 1.0 constant_dynamic-update-slice_fusion.1
  113.4 18.1 %all-to-all-done.2 = bf16[32,16,1792]{2,1,0:T(8,128)(2,1)} async-done(((bf16[32,16,1792]{2,1,0:T(8,128)(2,1)}), bf16[32,16,1792]{2,1,0:T(8,128)(2,1)}, u32[]{:S(2)}, u32[]{:S(2)}) %all-to-all-start.2) | async-done | bytes 1835040 | tf_op jit(solution)/shard_map/all_to_all | solution.py:53
  131.5 2.4 fusion.9
  133.9 4.2 %collective-permute-start.3 = (f32[2,512,128]{2,1,0:T(8,128)S(1)}, f32[2,512,128]{2,1,0:T(8,128)S(1)}, u32[]{:S(2)}, u32[]{:S(2)}) collective-permute-start(f32[2,512,128]{2,1,0:T(8,128)S(1)} %fusion.9), channel_id=1, source_target_pairs={{0,8},{8,0},{1,9},{9,1},{2,10},{10,2},{3,11},{11,3},{4,12},{12,4},... | collective-permute-start | bytes 1572872 | tf_op jit(solution)/shard_map/ppermute | solution.py:14
  138.0 1.5 collective-permute-done.3
  139.6 3.0 %convolution_convert_fusion.2 = bf16[512,1792]{1,0:T(8,128)(2,1)} fusion(bf16[1,3,1792,128]{3,2,1,0:T(8,128)(2,1)} %param.9, f32[2,512,128]{2,1,0:T(8,128)S(1)} %add.184), kind=kOutput, calls=%fused_computation.2 | convolution fusion | flops 236191744 | bytes 2818048 | tf_op jit(solution)/shard_map/dot_general | solution.py:60
  142.6 4.2 %all-to-all-start.3 = ((bf16[32,16,1792]{2,1,0:T(8,128)(2,1)}), bf16[32,16,1792]{2,1,0:T(8,128)(2,1)S(1)}, u32[]{:S(2)}, u32[]{:S(2)}) async-start(bf16[32,16,1792]{2,1,0:T(8,128)(2,1)} %bitcast.86), calls=%async_computation.3 | async-start | bytes 3670016 | tf_op jit(solution)/shard_map/all_to_all | solution.py:53
  146.9 24.9 %all-to-all-done.3 = bf16[32,16,1792]{2,1,0:T(8,128)(2,1)S(1)} async-done(((bf16[32,16,1792]{2,1,0:T(8,128)(2,1)}), bf16[32,16,1792]{2,1,0:T(8,128)(2,1)S(1)}, u32[]{:S(2)}, u32[]{:S(2)}) %all-to-all-start.3) | async-done | bytes 1835040 | tf_op jit(solution)/shard_map/all_to_all | solution.py:53
  171.8 0.7 fusion.48
  172.5 0.8 fusion.1
  173.3 1.5 reshape.273
  174.8 1.1 copy.26
  175.9 0.1 copy.22
  176.0 1.0 constant_dynamic-update-slice_fusion
  177.1 4.5 %all-to-all-start.4 = ((bf16[16,336,128]{2,1,0:T(8,128)(2,1)}), bf16[16,336,128]{2,1,0:T(8,128)(2,1)S(1)}, u32[]{:S(2)}, u32[]{:S(2)}) async-start(bf16[16,336,128]{2,1,0:T(8,128)(2,1)} %bitcast.30), calls=%async_computation.5 | async-start | bytes 2752512 | tf_op jit(solution)/shard_map/all_to_all | solution.py:128
  184.0 16.6 %all-to-all-done.4 = bf16[16,336,128]{2,1,0:T(8,128)(2,1)S(1)} async-done(((bf16[16,336,128]{2,1,0:T(8,128)(2,1)}), bf16[16,336,128]{2,1,0:T(8,128)(2,1)S(1)}, u32[]{:S(2)}, u32[]{:S(2)}) %all-to-all-start.4) | async-done | bytes 1376288 | tf_op jit(solution)/shard_map/all_to_all | solution.py:128
  200.6 5.9 %collective-permute-start.4 = (bf16[336,128]{1,0:T(8,128)(2,1)S(1)}, bf16[336,128]{1,0:T(8,128)(2,1)S(1)}, u32[]{:S(2)}, u32[]{:S(2)}) collective-permute-start(bf16[336,128]{1,0:T(8,128)(2,1)S(1)} %bitcast_select_fusion.1), channel_id=1, source_target_pairs={{0,16},{16,0},{1,17},{17,1},{2,18},{18,2},{3,19},{19,3},{4,20},{20... | collective-permute-start | bytes 258056 | tf_op jit(solution)/shard_map/ppermute | solution.py:14
  206.5 1.2 fusion.66
  207.7 12.8 %collective-permute-done.4 = bf16[336,128]{1,0:T(8,128)(2,1)S(1)} collective-permute-done((bf16[336,128]{1,0:T(8,128)(2,1)S(1)}, bf16[336,128]{1,0:T(8,128)(2,1)S(1)}, u32[]{:S(2)}, u32[]{:S(2)}) %collective-permute-start.4) | collective-permute-done | bytes 86048 | tf_op jit(solution)/shard_map/ppermute | solution.py:14
  220.5 0.3 select_select_fusion
  220.9 26.0 %all_to_all.30 = bf16[16,336,128]{2,1,0:T(8,128)(2,1)S(1)} all-to-all(bf16[16,336,128]{2,1,0:T(8,128)(2,1)S(1)} %select_select_fusion), channel_id=1, replica_groups=mesh['y'=4,'x'=4,'zh'=2,'c'=2,'ma'=2,'mb'=2,'mc'=2] {'y','x'}, dimensions={0} | all-to-all | bytes 2752512 | tf_op jit(solution)/shard_map/all_to_all | solution.py:133
  246.9 1.1 copy.30
  (20 shorter events, 0.3 us)
Async XLA Ops:
  15.2 40.3 %all-to-all-start = ((bf16[32,16,1792]{2,1,0:T(8,128)(2,1)}), bf16[32,16,1792]{2,1,0:T(8,128)(2,1)S(1)}, u32[]{:S(2)}, u32[]{:S(2)}) async-start(bf16[32,16,1792]{2,1,0:T(8,128)(2,1)} %bitcast.10), calls=%async_computation | async-start | bytes 3670016 | tf_op jit(solution)/shard_map/all_to_all | solution.py:53
  25.8 29.8 %collective-permute-start = (bf16[64,1792]{1,0:T(8,128)(2,1)S(1)}, bf16[64,1792]{1,0:T(8,128)(2,1)S(1)}, u32[]{:S(2)}, u32[]{:S(2)}) collective-permute-start(bf16[64,1792]{1,0:T(8,128)(2,1)S(1)} %constant_dynamic-slice_fusion), channel_id=1, source_target_pairs={{0,23},{1,22},{2,21},{3,20},{4,19},{5,18},{6,17},{7,16},{16,7},{17... | collective-permute-start | bytes 688136 | tf_op jit(solution)/shard_map/ppermute | solution.py:18
  55.5 4.5 %copy-start = (f32[128,2]{0,1:T(2,128)S(1)}, f32[128,2]{0,1:T(2,128)}, u32[]{:S(2)}) copy-start(f32[128,2]{0,1:T(2,128)} %param.8) | copy-start | bytes 3076
  57.4 4.2 %collective-permute-start.1 = (f32[2,512,128]{2,1,0:T(8,128)S(1)}, f32[2,512,128]{2,1,0:T(8,128)S(1)}, u32[]{:S(2)}, u32[]{:S(2)}) collective-permute-start(f32[2,512,128]{2,1,0:T(8,128)S(1)} %fusion.6), channel_id=1, source_target_pairs={{0,8},{8,0},{1,9},{9,1},{2,10},{10,2},{3,11},{11,3},{4,12},{12,4},... | collective-permute-start | bytes 1572872 | tf_op jit(solution)/shard_map/ppermute | solution.py:14
  64.5 32.3 %all-to-all-start.1 = ((bf16[32,16,1792]{2,1,0:T(8,128)(2,1)}), bf16[32,16,1792]{2,1,0:T(8,128)(2,1)S(1)}, u32[]{:S(2)}, u32[]{:S(2)}) async-start(bf16[32,16,1792]{2,1,0:T(8,128)(2,1)} %bitcast.85), calls=%async_computation.1 | async-start | bytes 3670016 | tf_op jit(solution)/shard_map/all_to_all | solution.py:53
  71.9 22.4 %collective-permute-start.2 = (f32[4,128]{1,0:T(4,128)S(1)}, f32[4,128]{1,0:T(4,128)S(1)}, u32[]{:S(2)}, u32[]{:S(2)}) collective-permute-start(f32[4,128]{1,0:T(4,128)S(1)} %pad_maximum_fusion), channel_id=1, source_target_pairs={{0,23},{1,22},{2,21},{3,20},{4,19},{5,18},{6,17},{7,16},{16,7},{17... | collective-permute-start | bytes 6152 | tf_op jit(solution)/shard_map/ppermute | solution.py:18
  96.8 34.6 %all-to-all-start.2 = ((bf16[32,16,1792]{2,1,0:T(8,128)(2,1)}), bf16[32,16,1792]{2,1,0:T(8,128)(2,1)}, u32[]{:S(2)}, u32[]{:S(2)}) async-start(bf16[32,16,1792]{2,1,0:T(8,128)(2,1)} %bitcast.87), calls=%async_computation.2 | async-start | bytes 3670016 | tf_op jit(solution)/shard_map/all_to_all | solution.py:53
  133.9 5.7 %collective-permute-start.3 = (f32[2,512,128]{2,1,0:T(8,128)S(1)}, f32[2,512,128]{2,1,0:T(8,128)S(1)}, u32[]{:S(2)}, u32[]{:S(2)}) collective-permute-start(f32[2,512,128]{2,1,0:T(8,128)S(1)} %fusion.9), channel_id=1, source_target_pairs={{0,8},{8,0},{1,9},{9,1},{2,10},{10,2},{3,11},{11,3},{4,12},{12,4},... | collective-permute-start | bytes 1572872 | tf_op jit(solution)/shard_map/ppermute | solution.py:14
  142.6 29.2 %all-to-all-start.3 = ((bf16[32,16,1792]{2,1,0:T(8,128)(2,1)}), bf16[32,16,1792]{2,1,0:T(8,128)(2,1)S(1)}, u32[]{:S(2)}, u32[]{:S(2)}) async-start(bf16[32,16,1792]{2,1,0:T(8,128)(2,1)} %bitcast.86), calls=%async_computation.3 | async-start | bytes 3670016 | tf_op jit(solution)/shard_map/all_to_all | solution.py:53
  146.8 100.2 %reduce-scatter.2.cloned.1.call-start = ((), (), s32[]{:S(2)}) async-start(), calls=%async_computation.7 | async-start | bytes 1949696 | tf_op jit(solution)/shard_map/reduce_scatter | solution.py:131
  177.1 23.5 %all-to-all-start.4 = ((bf16[16,336,128]{2,1,0:T(8,128)(2,1)}), bf16[16,336,128]{2,1,0:T(8,128)(2,1)S(1)}, u32[]{:S(2)}, u32[]{:S(2)}) async-start(bf16[16,336,128]{2,1,0:T(8,128)(2,1)} %bitcast.30), calls=%async_computation.5 | async-start | bytes 2752512 | tf_op jit(solution)/shard_map/all_to_all | solution.py:128
  200.6 19.9 %collective-permute-start.4 = (bf16[336,128]{1,0:T(8,128)(2,1)S(1)}, bf16[336,128]{1,0:T(8,128)(2,1)S(1)}, u32[]{:S(2)}, u32[]{:S(2)}) collective-permute-start(bf16[336,128]{1,0:T(8,128)(2,1)S(1)} %bitcast_select_fusion.1), channel_id=1, source_target_pairs={{0,16},{16,0},{1,17},{17,1},{2,18},{18,2},{3,19},{19,3},{4,20},{20... | collective-permute-start | bytes 258056 | tf_op jit(solution)/shard_map/ppermute | solution.py:14
Sparse Core Ops, SparseCore 0:
  177.2 59.0 reduce-scatter.1

commit v7 on v4

--- a/solution.py
+++ b/solution.py
@@ -1,15 +1,21 @@
 import jax
 import jax.numpy as jnp
 from jax import lax
+from jax.experimental.layout import Layout, with_layout_constraint
 from jax.sharding import Mesh, PartitionSpec as P
 
 PLANE = ("y", "x", "c")
 NEAR = ("mb", "mc")
+RING = ("zh", "ma", "mb", "mc")
 CAP = 16
 
 
 def swap(value, axis):
     return lax.ppermute(value, axis, [(0, 1), (1, 0)])
+
+
+def mirrored(value):
+    return lax.ppermute(value, RING, [(i, 15 - i) for i in range(16)])
 
 
 def place_codes(routes, gate_values, owner):
@@ -73,13 +79,13 @@
     return jnp.transpose(parts, (3, 2, 1, 0, 4)).reshape(near, 2, tok_rows, -1)
 
 
-def near_sum(parts, place):
-    total = lax.dynamic_index_in_dim(parts, place, 0, keepdims=False).astype(jnp.float32)
+def near_sum(parts, place, mine):
     count = parts.shape[0]
+    total = lax.dynamic_index_in_dim(parts, place ^ mine, 0, keepdims=False).astype(jnp.float32)
     for step in range(1, count):
-        block = lax.dynamic_index_in_dim(parts, place ^ step, 0, keepdims=False)
+        block = lax.dynamic_index_in_dim(parts, place ^ step ^ mine, 0, keepdims=False)
         total += lax.ppermute(block, NEAR, [(i, i ^ step) for i in range(count)]).astype(jnp.float32)
-    return total
+    return total.astype(jnp.bfloat16)
 
 
 tied = lax.optimization_barrier
@@ -105,21 +111,22 @@
     tok_rows = tokens.shape[0]
     own = expert_weights[0]
     table = jnp.transpose(tokens.reshape(tok_rows, 2 * near, 2, -1), (2, 0, 1, 3)).reshape(2 * tok_rows, -1)
+    table = with_layout_constraint(table, Layout(major_to_minor=(0, 1)))
     share = 2 * tok_rows // near
-    part = lax.dynamic_slice_in_dim(table, place * share, share, 0)
+    part = lax.dynamic_slice_in_dim(table, (near - 1 - place) * share, share, 0)
     codes = place_codes(routes, gate_values, old_owner)
     rows = placed_rows(codes, zh)
-    part, payload = tied((part, gather_rows(rows, table)))
-    quarter = swap(part, "zh")
+    quarter = mirrored(part)
+    chips = lax.axis_size("y") * lax.axis_size("x")
+    spread = lax.all_to_all(
+        own.reshape(chips, -1, own.shape[-1]), ("y", "x"), split_axis=0, concat_axis=0, tiled=True
+    )
+    payload, spread, quarter, later_codes = tied((gather_rows(rows, table), spread, quarter, codes))
     sent = exchange(payload)
-    chips = lax.axis_size("y") * lax.axis_size("x")
-    pieces, sent, quarter = tied((own.reshape(chips, -1, own.shape[-1]), sent, quarter))
-    spread = lax.all_to_all(pieces, ("y", "x"), split_axis=0, concat_axis=0, tiled=True)
-    quarter, later_codes = tied((quarter, codes))
-    other_codes = swap(later_codes, "zh")
+    other_codes = mirrored(later_codes)
     other_rows = placed_rows(other_codes, zh)
     other_table = lax.all_gather(quarter, NEAR, tiled=True)
-    payload, spread = tied((gather_rows(other_rows, other_table), spread))
+    payload, sent = tied((gather_rows(other_rows, other_table), sent))
     other_sent = exchange(payload)
     payload, other_sent = tied((expert_part(sent, own), other_sent))
     back = exchange(payload)
@@ -127,22 +134,18 @@
     payload, back, chosen = tied((expert_part(other_sent, own), back, chosen))
     other_back = exchange(payload)
 
-    parts = by_columns(weighted(back, codes, rows), near)
-    kept = near_sum(parts, place).astype(jnp.bfloat16)
-    other_back, kept = tied((other_back, kept))
-    other_parts = by_columns(weighted(other_back, other_codes, other_rows), near)
-    near_parts = lax.all_to_all(other_parts, NEAR, split_axis=0, concat_axis=0, tiled=True)
-    near_parts, chosen = tied((near_parts, chosen))
+    kept = near_sum(by_columns(weighted(back, codes, rows), near), place, 0)
+    kept, other_back, chosen = tied((kept, other_back, chosen))
     arrived = lax.all_to_all(chosen, ("y", "x"), split_axis=0, concat_axis=0, tiled=True)
-    other_kept = jnp.sum(near_parts.astype(jnp.float32), axis=0).astype(jnp.bfloat16)
+    other_kept = near_sum(by_columns(weighted(other_back, other_codes, other_rows), near), place, near - 1)
 
     def of(value, index):
         return lax.dynamic_index_in_dim(value, index, 0, keepdims=False)
 
     total = of(kept, far).astype(jnp.float32)
     total += swap(of(kept, 1 - far), "ma").astype(jnp.float32)
-    total += swap(of(other_kept, far), "zh").astype(jnp.float32)
-    total += lax.ppermute(of(other_kept, 1 - far), ("zh", "ma"), [(i, i ^ 3) for i in range(4)]).astype(jnp.float32)
+    total += mirrored(of(other_kept, 1 - far)).astype(jnp.float32)
+    total += lax.ppermute(of(other_kept, far), RING, [(i, i ^ 11) for i in range(16)]).astype(jnp.float32)
     return total.astype(jnp.bfloat16), arrived.reshape(expert_weights.shape)
 
 

time: 290 us -> 263 us (0.907)
  blocking collectives: 69.9 us -> 18 us
  waiting for transfers between devices: 65.7 us -> 79.9 us
  local copies, waits for them, and re-layouts: 12.5 us -> 22.2 us
    ppermute x7 -> x4, starting transfers between devices: 46.9 us -> 15.8 us  [swap(): return lax.ppermute(value, axis, [(0, 1), (1, 0)])]
    all_to_all x1 -> x0, blocking collectives: 30.4 us -> none  [shards(): lax.all_to_all(other_parts, NEAR, split_axis=0, concat_axis=0, tiled=True)]
    ppermute x1 -> x4, waiting for transfers between devices: 4.11 us -> 29.2 us  [the longest x3 18 us: mirrored(): return lax.ppermute(value, RING, [(i, 15 - i) for i in range(16)])]
    ppermute x1 -> x4, starting transfers between devices: 1.92 us -> 26.9 us  [the longest x3 19.4 us: mirrored(): return lax.ppermute(value, RING, [(i, 15 - i) for i in range(16)])]
    ppermute x7 -> x4, waiting for transfers between devices: 32.7 us -> 9.65 us  [swap(): return lax.ppermute(value, axis, [(0, 1), (1, 0)])]
    all_gather x1, blocking collectives: 39.5 us -> 18 us  [shards(): other_table = lax.all_gather(quarter, NEAR, tiled=True)]
    ppermute x3 -> x6, starting transfers between devices: 9.45 us -> 22.3 us  [near_sum(): lax.ppermute(block, NEAR, [(i, i ^ step) for i in range(count)])]
    ppermute x3 -> x6, waiting for transfers between devices: 12.1 us -> 23.6 us  [near_sum(): lax.ppermute(block, NEAR, [(i, i ^ step) for i in range(count)])]
  transfers between devices with their start and end apart: 17 -> 20, of which waited for: 10 -> 11; matrix products, arithmetic and copies ran while one was open for 7% -> 17% of each run, Pallas kernels for 0% -> 0%
where the time goes in v7:
time: 263 us; the launch traced here: 260 us
  starting transfers between devices  110 us (42%)
  waiting for transfers between devices  79.9 us (30%)
  local copies, waits for them, and re-layouts  22.2 us (8%)
  matrix products  19.8 us (8%)
  blocking collectives  18 us (7%)
  other arithmetic  6.48 us (2%)
  between operations  3.77 us (1%)
    all_to_all x4, starting transfers between devices, exchange(): lax.all_to_all(blocks, axes, split_axis=0, concat_axis=0, tiled=True)  30.3 us
    ppermute x6, waiting for transfers between devices, near_sum(): lax.ppermute(block, NEAR, [(i, i ^ step) for i in range(count)])  23.6 us
    ppermute x6, starting transfers between devices, near_sum(): lax.ppermute(block, NEAR, [(i, i ^ step) for i in range(count)])  22.3 us
    ppermute x3, starting transfers between devices, mirrored(): return lax.ppermute(value, RING, [(i, 15 - i) for i in range(16)])  19.4 us
    all_gather x1, blocking collectives, shards(): other_table = lax.all_gather(quarter, NEAR, tiled=True)  18 us
    ppermute x3, waiting for transfers between devices, mirrored(): return lax.ppermute(value, RING, [(i, 15 - i) for i in range(16)])  18 us
    all_to_all x4, waiting for transfers between devices, exchange(): lax.all_to_all(blocks, axes, split_axis=0, concat_axis=0, tiled=True)  17.4 us
    ppermute x4, starting transfers between devices, swap(): return lax.ppermute(value, axis, [(0, 1), (1, 0)])  15.8 us
  transfers between devices with their start and end apart: 20, of which 11 were waited for; matrix products, arithmetic and copies ran while one was open for 17% of the time, Pallas kernels for 0%

profile of v7, /device:TPU:1, one launch (start us, length us, event | category | flops | bytes accessed | tf_op | source)
XLA Modules:
  0.0 259.9 jit_solution(11627503175430718833)
XLA Ops:
  0.6 7.7 %all-to-all-start = ((bf16[16,336,128]{2,1,0:T(8,128)(2,1)}), bf16[16,336,128]{2,1,0:T(8,128)(2,1)S(1)}, u32[]{:S(2)}, u32[]{:S(2)}) async-start(bf16[16,336,128]{2,1,0:T(8,128)(2,1)} %bitcast.114), calls=%async_computation | async-start | bytes 2752512 | tf_op jit(solution)/shard_map/all_to_all | solution.py:121
  10.0 1.3 reshape.280
  11.3 11.1 %collective-permute-start = (bf16[64,1792]{1,0:T(8,128)(2,1)S(1)}, bf16[64,1792]{1,0:T(8,128)(2,1)S(1)}, u32[]{:S(2)}, u32[]{:S(2)}) collective-permute-start(bf16[64,1792]{1,0:T(8,128)(2,1)S(1)} %constant_dynamic-slice_fusion), channel_id=1, source_target_pairs={{0,23},{1,22},{2,21},{3,20},{4,19},{5,18},{6,17},{7,16},{16,7},{17... | collective-permute-start | bytes 688136 | tf_op jit(solution)/shard_map/ppermute | solution.py:18
  23.4 1.9 convolution_convert_fusion.1
  25.3 17.5 %collective-permute-done = bf16[64,1792]{1,0:T(8,128)(2,1)S(1)} collective-permute-done((bf16[64,1792]{1,0:T(8,128)(2,1)S(1)}, bf16[64,1792]{1,0:T(8,128)(2,1)S(1)}, u32[]{:S(2)}, u32[]{:S(2)}) %collective-permute-start) | collective-permute-done | bytes 229408 | tf_op jit(solution)/shard_map/ppermute | solution.py:18
  42.8 7.9 %all-to-all-start.1 = ((bf16[32,16,1792]{2,1,0:T(8,128)(2,1)}), bf16[32,16,1792]{2,1,0:T(8,128)(2,1)S(1)}, u32[]{:S(2)}, u32[]{:S(2)}) async-start(bf16[32,16,1792]{2,1,0:T(8,128)(2,1)} %bitcast.16), calls=%async_computation.1 | async-start | bytes 3670016 | tf_op jit(solution)/shard_map/all_to_all | solution.py:53
  50.7 4.6 %collective-permute-start.1 = (f32[4,128]{1,0:T(4,128)S(1)}, f32[4,128]{1,0:T(4,128)S(1)}, u32[]{:S(2)}, u32[]{:S(2)}) collective-permute-start(f32[4,128]{1,0:T(4,128)S(1)} %pad_maximum_fusion), channel_id=1, source_target_pairs={{0,23},{1,22},{2,21},{3,20},{4,19},{5,18},{6,17},{7,16},{16,7},{17... | collective-permute-start | bytes 6152 | tf_op jit(solution)/shard_map/ppermute | solution.py:18
  55.3 18.0 %all_gather.3 = bf16[256,1792]{1,0:T(8,128)(2,1)S(1)} all-gather(bf16[64,1792]{1,0:T(8,128)(2,1)S(1)} %collective-permute-done), channel_id=1, replica_groups=mesh['y'=4,'x'=4,'zh'=2,'c'=2,'ma'=2,'mb'=2,'mc'=2] {'mb','mc'}, dimensions={0}, use_global_device_ids=true | all-gather | bytes 1146880 | tf_op jit(solution)/shard_map/all_gather | solution.py:128
  73.4 1.9 convolution_convert_fusion
  76.9 8.8 %all-to-all-start.2 = ((bf16[32,16,1792]{2,1,0:T(8,128)(2,1)}), bf16[32,16,1792]{2,1,0:T(8,128)(2,1)}, u32[]{:S(2)}, u32[]{:S(2)}) async-start(bf16[32,16,1792]{2,1,0:T(8,128)(2,1)} %bitcast.23), calls=%async_computation.2 | async-start | bytes 3670016 | tf_op jit(solution)/shard_map/all_to_all | solution.py:53
  85.7 2.1 fusion.6
  87.9 2.2 collective-permute-start.2
  90.1 1.6 collective-permute-done.2
  91.8 1.9 convolution_convert_fusion.3
  93.7 17.0 %all-to-all-done.2 = bf16[32,16,1792]{2,1,0:T(8,128)(2,1)} async-done(((bf16[32,16,1792]{2,1,0:T(8,128)(2,1)}), bf16[32,16,1792]{2,1,0:T(8,128)(2,1)}, u32[]{:S(2)}, u32[]{:S(2)}) %all-to-all-start.2) | async-done | bytes 1835040 | tf_op jit(solution)/shard_map/all_to_all | solution.py:53
  110.7 5.9 %all-to-all-start.3 = ((bf16[32,16,1792]{2,1,0:T(8,128)(2,1)}), bf16[32,16,1792]{2,1,0:T(8,128)(2,1)S(1)}, u32[]{:S(2)}, u32[]{:S(2)}) async-start(bf16[32,16,1792]{2,1,0:T(8,128)(2,1)} %bitcast.112), calls=%async_computation.3 | async-start | bytes 3670016 | tf_op jit(solution)/shard_map/all_to_all | solution.py:53
  119.2 1.3 fusion.75
  120.5 6.9 %collective-permute-start.4 = (bf16[336,128]{1,0:T(8,128)(2,1)S(1)}, bf16[336,128]{1,0:T(8,128)(2,1)S(1)}, u32[]{:S(2)}, u32[]{:S(2)}) collective-permute-start(bf16[336,128]{1,0:T(8,128)(2,1)S(1)} %bitcast_select_fusion.1), channel_id=1, source_target_pairs={{0,16},{16,0},{1,17},{17,1},{2,18},{18,2},{3,19},{19,3},{4,20},{20... | collective-permute-start | bytes 258056 | tf_op jit(solution)/shard_map/ppermute | solution.py:14
  127.4 2.4 fusion.9
  129.8 2.5 collective-permute-start.3
  132.3 8.1 %collective-permute-done.4 = bf16[336,128]{1,0:T(8,128)(2,1)S(1)} collective-permute-done((bf16[336,128]{1,0:T(8,128)(2,1)S(1)}, bf16[336,128]{1,0:T(8,128)(2,1)S(1)}, u32[]{:S(2)}, u32[]{:S(2)}) %collective-permute-start.4) | collective-permute-done | bytes 86048 | tf_op jit(solution)/shard_map/ppermute | solution.py:14
  140.4 1.3 select_select_fusion
  141.8 2.9 %convolution_convert_fusion.2 = bf16[512,1792]{1,0:T(8,128)(2,1)} fusion(bf16[1,3,1792,128]{3,2,1,0:T(8,128)(2,1)} %param.9, f32[2,512,128]{2,1,0:T(8,128)S(1)} %add.233), kind=kOutput, calls=%fused_computation.2 | convolution fusion | flops 236191744 | bytes 2818048 | tf_op jit(solution)/shard_map/dot_general | solution.py:60
  146.0 7.7 %all-to-all-start.4 = ((bf16[32,16,1792]{2,1,0:T(8,128)(2,1)}), bf16[32,16,1792]{2,1,0:T(8,128)(2,1)S(1)}, u32[]{:S(2)}, u32[]{:S(2)}) async-start(bf16[32,16,1792]{2,1,0:T(8,128)(2,1)} %bitcast.111), calls=%async_computation.4 | async-start | bytes 3670016 | tf_op jit(solution)/shard_map/all_to_all | solution.py:53
  153.7 2.4 fusion.51
  156.1 1.7 fusion
  157.8 3.5 %reshape.281 = bf16[2,128,2,4,224]{4,3,2,1,0:T(4,128)(2,1)S(1)} reshape(bf16[256,1792]{1,0:T(8,128)(2,1)} %fusion) | data formatting | bytes 1835008 | tf_op jit(solution)/shard_map/reshape | solution.py:78
  161.3 2.3 copy.25
  163.6 1.3 copy.20
  165.7 1.9 collective-permute-start.5
  167.6 2.9 %collective-permute-start.6 = (bf16[2,128,448]{1,2,0:T(8,128)(2,1)S(1)}, bf16[2,128,448]{1,2,0:T(8,128)(2,1)}, u32[]{:S(2)}, u32[]{:S(2)}) collective-permute-start(bf16[2,128,448]{1,2,0:T(8,128)(2,1)S(1)} %get-tuple-element.43), channel_id=1, source_target_pairs={{0,2},{1,3},{2,0},{3,1},{4,6},{5,7},{6,4},{7,5},{8,10},{9,11},{10,... | collective-permute-start | bytes 688136 | tf_op jit(solution)/shard_map/ppermute | solution.py:87
  170.5 4.4 %collective-permute-start.7 = (bf16[2,128,448]{1,2,0:T(8,128)(2,1)S(1)}, bf16[2,128,448]{1,2,0:T(8,128)(2,1)}, u32[]{:S(2)}, u32[]{:S(2)}) collective-permute-start(bf16[2,128,448]{1,2,0:T(8,128)(2,1)S(1)} %get-tuple-element.42), channel_id=1, source_target_pairs={{0,3},{1,2},{2,1},{3,0},{4,7},{5,6},{6,5},{7,4},{8,11},{9,10},{10,... | collective-permute-start | bytes 688136 | tf_op jit(solution)/shard_map/ppermute | solution.py:87
  175.0 1.3 collective-permute-done.5
  176.3 10.9 %collective-permute-done.6 = bf16[2,128,448]{1,2,0:T(8,128)(2,1)} collective-permute-done((bf16[2,128,448]{1,2,0:T(8,128)(2,1)S(1)}, bf16[2,128,448]{1,2,0:T(8,128)(2,1)}, u32[]{:S(2)}, u32[]{:S(2)}) %collective-permute-start.6) | collective-permute-done | bytes 229408 | tf_op jit(solution)/shard_map/ppermute | solution.py:87
  188.3 6.8 %all-to-all-start.5 = ((bf16[16,336,128]{2,1,0:T(8,128)(2,1)}), bf16[16,336,128]{2,1,0:T(8,128)(2,1)S(1)}, u32[]{:S(2)}, u32[]{:S(2)}) async-start(bf16[16,336,128]{2,1,0:T(8,128)(2,1)} %select_select_fusion), calls=%async_computation.5 | async-start | bytes 2752512 | tf_op jit(solution)/shard_map/all_to_all | solution.py:139
  195.8 1.7 fusion.1
  197.5 3.5 %reshape.282 = bf16[2,128,2,4,224]{4,3,2,1,0:T(4,128)(2,1)S(1)} reshape(bf16[256,1792]{1,0:T(8,128)(2,1)} %fusion.1) | data formatting | bytes 1835008 | tf_op jit(solution)/shard_map/reshape | solution.py:78
  201.1 2.3 copy.26
  203.3 1.3 copy.22
  205.4 7.1 %collective-permute-start.10 = (bf16[2,128,448]{1,2,0:T(8,128)(2,1)}, bf16[2,128,448]{1,2,0:T(8,128)(2,1)S(1)}, u32[]{:S(2)}, u32[]{:S(2)}) collective-permute-start(bf16[2,128,448]{1,2,0:T(8,128)(2,1)} %get-tuple-element.40), channel_id=1, source_target_pairs={{0,2},{1,3},{2,0},{3,1},{4,6},{5,7},{6,4},{7,5},{8,10},{9,11},{10,... | collective-permute-start | bytes 688136 | tf_op jit(solution)/shard_map/ppermute | solution.py:87
  212.5 4.0 %collective-permute-start.11 = (bf16[2,128,448]{1,2,0:T(8,128)(2,1)S(1)}, bf16[2,128,448]{1,2,0:T(8,128)(2,1)S(1)}, u32[]{:S(2)}, u32[]{:S(2)}) collective-permute-start(bf16[2,128,448]{1,2,0:T(8,128)(2,1)S(1)} %get-tuple-element.39), channel_id=1, source_target_pairs={{0,3},{1,2},{2,1},{3,0},{4,7},{5,6},{6,5},{7,4},{8,11},{9,10},{10,... | collective-permute-start | bytes 688136 | tf_op jit(solution)/shard_map/ppermute | solution.py:87
  216.5 1.9 collective-permute-start.9
  218.4 4.2 %collective-permute-start.8 = (bf16[128,448]{0,1:T(8,128)(2,1)S(1)}, bf16[128,448]{0,1:T(8,128)(2,1)S(1)}, u32[]{:S(2)}, u32[]{:S(2)}) collective-permute-start(bf16[128,448]{0,1:T(8,128)(2,1)S(1)} %dynamic-slice_bitcast_fusion.8), channel_id=1, source_target_pairs={{0,4},{4,0},{1,5},{5,1},{2,6},{6,2},{3,7},{7,3},{8,12},{12,8},{9,1... | collective-permute-start | bytes 344072 | tf_op jit(solution)/shard_map/ppermute | solution.py:14
  222.6 3.6 %collective-permute-done.10 = bf16[2,128,448]{1,2,0:T(8,128)(2,1)S(1)} collective-permute-done((bf16[2,128,448]{1,2,0:T(8,128)(2,1)}, bf16[2,128,448]{1,2,0:T(8,128)(2,1)S(1)}, u32[]{:S(2)}, u32[]{:S(2)}) %collective-permute-start.10) | collective-permute-done | bytes 229408 | tf_op jit(solution)/shard_map/ppermute | solution.py:87
  226.2 7.9 %collective-permute-done.9 = bf16[2,128,448]{1,2,0:T(8,128)(2,1)} collective-permute-done((bf16[2,128,448]{1,2,0:T(8,128)(2,1)S(1)}, bf16[2,128,448]{1,2,0:T(8,128)(2,1)}, u32[]{:S(2)}, u32[]{:S(2)}) %collective-permute-start.9) | collective-permute-done | bytes 229408 | tf_op jit(solution)/shard_map/ppermute | solution.py:87
  235.2 3.7 %collective-permute-start.12 = (bf16[128,448]{0,1:T(8,128)(2,1)S(1)}, bf16[128,448]{0,1:T(8,128)(2,1)S(1)}, u32[]{:S(2)}, u32[]{:S(2)}) collective-permute-start(bf16[128,448]{0,1:T(8,128)(2,1)S(1)} %get-tuple-element.44), channel_id=1, source_target_pairs={{0,23},{1,22},{2,21},{3,20},{4,19},{5,18},{6,17},{7,16},{16,7},{17... | collective-permute-start | bytes 344072 | tf_op jit(solution)/shard_map/ppermute | solution.py:18
  238.9 7.5 %collective-permute-start.13 = (bf16[128,448]{0,1:T(8,128)(2,1)S(1)}, bf16[128,448]{0,1:T(8,128)(2,1)S(1)}, u32[]{:S(2)}, u32[]{:S(2)}) collective-permute-start(bf16[128,448]{0,1:T(8,128)(2,1)S(1)} %get-tuple-element.45), channel_id=1, source_target_pairs={{0,19},{1,18},{2,17},{3,16},{4,23},{5,22},{6,21},{7,20},{16,3},{17... | collective-permute-start | bytes 344072 | tf_op jit(solution)/shard_map/ppermute | solution.py:148
  247.0 11.2 %collective-permute-done.13 = bf16[128,448]{0,1:T(8,128)(2,1)S(1)} collective-permute-done((bf16[128,448]{0,1:T(8,128)(2,1)S(1)}, bf16[128,448]{0,1:T(8,128)(2,1)S(1)}, u32[]{:S(2)}, u32[]{:S(2)}) %collective-permute-start.13) | collective-permute-done | bytes 114720 | tf_op jit(solution)/shard_map/ppermute | solution.py:148
  (56 shorter events, 12.4 us)
Async XLA Ops:
  0.6 7.8 %copy-start.4 = (bf16[128,3584]{1,0:T(8,128)(2,1)S(1)}, bf16[128,3584]{1,0:T(8,128)(2,1)}, u32[]{:S(2)}) copy-start(bf16[128,3584]{1,0:T(8,128)(2,1)} %param.6) | copy-start | bytes 2752516
  0.6 42.1 %all-to-all-start = ((bf16[16,336,128]{2,1,0:T(8,128)(2,1)}), bf16[16,336,128]{2,1,0:T(8,128)(2,1)S(1)}, u32[]{:S(2)}, u32[]{:S(2)}) async-start(bf16[16,336,128]{2,1,0:T(8,128)(2,1)} %bitcast.114), calls=%async_computation | async-start | bytes 2752512 | tf_op jit(solution)/shard_map/all_to_all | solution.py:121
  9.0 13.4 %copy-start.6 = (s32[32]{0:T(128)S(1)}, s32[32]{0:T(128)}, u32[]{:S(2)}) copy-start(s32[32]{0:T(128)} %param.10) | copy-start | bytes 388
  9.0 13.4 %copy-start.7 = (s32[32]{0:T(128)S(1)}, s32[32]{0:T(128)}, u32[]{:S(2)}) copy-start(s32[32]{0:T(128)} %param.11) | copy-start | bytes 388
  9.0 14.1 %copy-start.8 = (s32[128,2]{0,1:T(2,128)S(1)}, s32[128,2]{0,1:T(2,128)}, u32[]{:S(2)}) copy-start(s32[128,2]{0,1:T(2,128)} %param.7) | copy-start | bytes 3076
  9.0 14.3 %copy-start.5 = (f32[128,2]{0,1:T(2,128)S(1)}, f32[128,2]{0,1:T(2,128)}, u32[]{:S(2)}) copy-start(f32[128,2]{0,1:T(2,128)} %param.8) | copy-start | bytes 3076
  11.3 31.5 %collective-permute-start = (bf16[64,1792]{1,0:T(8,128)(2,1)S(1)}, bf16[64,1792]{1,0:T(8,128)(2,1)S(1)}, u32[]{:S(2)}, u32[]{:S(2)}) collective-permute-start(bf16[64,1792]{1,0:T(8,128)(2,1)S(1)} %constant_dynamic-slice_fusion), channel_id=1, source_target_pairs={{0,23},{1,22},{2,21},{3,20},{4,19},{5,18},{6,17},{7,16},{16,7},{17... | collective-permute-start | bytes 688136 | tf_op jit(solution)/shard_map/ppermute | solution.py:18
  42.8 32.8 %all-to-all-start.1 = ((bf16[32,16,1792]{2,1,0:T(8,128)(2,1)}), bf16[32,16,1792]{2,1,0:T(8,128)(2,1)S(1)}, u32[]{:S(2)}, u32[]{:S(2)}) async-start(bf16[32,16,1792]{2,1,0:T(8,128)(2,1)} %bitcast.16), calls=%async_computation.1 | async-start | bytes 3670016 | tf_op jit(solution)/shard_map/all_to_all | solution.py:53
  50.7 22.6 %collective-permute-start.1 = (f32[4,128]{1,0:T(4,128)S(1)}, f32[4,128]{1,0:T(4,128)S(1)}, u32[]{:S(2)}, u32[]{:S(2)}) collective-permute-start(f32[4,128]{1,0:T(4,128)S(1)} %pad_maximum_fusion), channel_id=1, source_target_pairs={{0,23},{1,22},{2,21},{3,20},{4,19},{5,18},{6,17},{7,16},{16,7},{17... | collective-permute-start | bytes 6152 | tf_op jit(solution)/shard_map/ppermute | solution.py:18
  75.6 1.3 copy-start.3
  76.9 8.8 %copy-start.2 = (bf16[1,3,1792,128]{3,2,1,0:T(8,128)(2,1)S(1)}, bf16[1,3,1792,128]{3,2,1,0:T(8,128)(2,1)}, u32[]{:S(2)}) copy-start(bf16[1,3,1792,128]{3,2,1,0:T(8,128)(2,1)} %param.9) | copy-start | bytes 4128772
  76.9 33.8 %all-to-all-start.2 = ((bf16[32,16,1792]{2,1,0:T(8,128)(2,1)}), bf16[32,16,1792]{2,1,0:T(8,128)(2,1)}, u32[]{:S(2)}, u32[]{:S(2)}) async-start(bf16[32,16,1792]{2,1,0:T(8,128)(2,1)} %bitcast.23), calls=%async_computation.2 | async-start | bytes 3670016 | tf_op jit(solution)/shard_map/all_to_all | solution.py:53
  87.9 3.8 %collective-permute-start.2 = (f32[2,512,128]{2,1,0:T(8,128)S(1)}, f32[2,512,128]{2,1,0:T(8,128)S(1)}, u32[]{:S(2)}, u32[]{:S(2)}) collective-permute-start(f32[2,512,128]{2,1,0:T(8,128)S(1)} %fusion.6), channel_id=1, source_target_pairs={{0,8},{8,0},{1,9},{9,1},{2,10},{10,2},{3,11},{11,3},{4,12},{12,4},... | collective-permute-start | bytes 1572872 | tf_op jit(solution)/shard_map/ppermute | solution.py:14
  110.7 34.1 %all-to-all-start.3 = ((bf16[32,16,1792]{2,1,0:T(8,128)(2,1)}), bf16[32,16,1792]{2,1,0:T(8,128)(2,1)S(1)}, u32[]{:S(2)}, u32[]{:S(2)}) async-start(bf16[32,16,1792]{2,1,0:T(8,128)(2,1)} %bitcast.112), calls=%async_computation.3 | async-start | bytes 3670016 | tf_op jit(solution)/shard_map/all_to_all | solution.py:53
  120.5 19.9 %collective-permute-start.4 = (bf16[336,128]{1,0:T(8,128)(2,1)S(1)}, bf16[336,128]{1,0:T(8,128)(2,1)S(1)}, u32[]{:S(2)}, u32[]{:S(2)}) collective-permute-start(bf16[336,128]{1,0:T(8,128)(2,1)S(1)} %bitcast_select_fusion.1), channel_id=1, source_target_pairs={{0,16},{16,0},{1,17},{17,1},{2,18},{18,2},{3,19},{19,3},{4,20},{20... | collective-permute-start | bytes 258056 | tf_op jit(solution)/shard_map/ppermute | solution.py:14
  129.8 12.0 %collective-permute-start.3 = (f32[2,512,128]{2,1,0:T(8,128)S(1)}, f32[2,512,128]{2,1,0:T(8,128)S(1)}, u32[]{:S(2)}, u32[]{:S(2)}) collective-permute-start(f32[2,512,128]{2,1,0:T(8,128)S(1)} %fusion.9), channel_id=1, source_target_pairs={{0,8},{8,0},{1,9},{9,1},{2,10},{10,2},{3,11},{11,3},{4,12},{12,4},... | collective-permute-start | bytes 1572872 | tf_op jit(solution)/shard_map/ppermute | solution.py:14
  144.8 1.2 copy-start
  146.0 42.3 %all-to-all-start.4 = ((bf16[32,16,1792]{2,1,0:T(8,128)(2,1)}), bf16[32,16,1792]{2,1,0:T(8,128)(2,1)S(1)}, u32[]{:S(2)}, u32[]{:S(2)}) async-start(bf16[32,16,1792]{2,1,0:T(8,128)(2,1)} %bitcast.111), calls=%async_computation.4 | async-start | bytes 3670016 | tf_op jit(solution)/shard_map/all_to_all | solution.py:53
  153.7 2.4 copy-start.1
  165.7 10.6 %collective-permute-start.5 = (bf16[2,128,448]{1,2,0:T(8,128)(2,1)}, bf16[2,128,448]{1,2,0:T(8,128)(2,1)S(1)}, u32[]{:S(2)}, u32[]{:S(2)}) collective-permute-start(bf16[2,128,448]{1,2,0:T(8,128)(2,1)} %get-tuple-element.41), channel_id=1, source_target_pairs={{0,1},{1,0},{2,3},{3,2},{4,5},{5,4},{6,7},{7,6},{8,9},{9,8},{10,11... | collective-permute-start | bytes 688136 | tf_op jit(solution)/shard_map/ppermute | solution.py:87
  167.6 19.6 %collective-permute-start.6 = (bf16[2,128,448]{1,2,0:T(8,128)(2,1)S(1)}, bf16[2,128,448]{1,2,0:T(8,128)(2,1)}, u32[]{:S(2)}, u32[]{:S(2)}) collective-permute-start(bf16[2,128,448]{1,2,0:T(8,128)(2,1)S(1)} %get-tuple-element.43), channel_id=1, source_target_pairs={{0,2},{1,3},{2,0},{3,1},{4,6},{5,7},{6,4},{7,5},{8,10},{9,11},{10,... | collective-permute-start | bytes 688136 | tf_op jit(solution)/shard_map/ppermute | solution.py:87
  170.5 16.6 %collective-permute-start.7 = (bf16[2,128,448]{1,2,0:T(8,128)(2,1)S(1)}, bf16[2,128,448]{1,2,0:T(8,128)(2,1)}, u32[]{:S(2)}, u32[]{:S(2)}) collective-permute-start(bf16[2,128,448]{1,2,0:T(8,128)(2,1)S(1)} %get-tuple-element.42), channel_id=1, source_target_pairs={{0,3},{1,2},{2,1},{3,0},{4,7},{5,6},{6,5},{7,4},{8,11},{9,10},{10,... | collective-permute-start | bytes 688136 | tf_op jit(solution)/shard_map/ppermute | solution.py:87
  188.3 70.5 %all-to-all-start.5 = ((bf16[16,336,128]{2,1,0:T(8,128)(2,1)}), bf16[16,336,128]{2,1,0:T(8,128)(2,1)S(1)}, u32[]{:S(2)}, u32[]{:S(2)}) async-start(bf16[16,336,128]{2,1,0:T(8,128)(2,1)} %select_select_fusion), calls=%async_computation.5 | async-start | bytes 2752512 | tf_op jit(solution)/shard_map/all_to_all | solution.py:139
  205.4 20.8 %collective-permute-start.10 = (bf16[2,128,448]{1,2,0:T(8,128)(2,1)}, bf16[2,128,448]{1,2,0:T(8,128)(2,1)S(1)}, u32[]{:S(2)}, u32[]{:S(2)}) collective-permute-start(bf16[2,128,448]{1,2,0:T(8,128)(2,1)} %get-tuple-element.40), channel_id=1, source_target_pairs={{0,2},{1,3},{2,0},{3,1},{4,6},{5,7},{6,4},{7,5},{8,10},{9,11},{10,... | collective-permute-start | bytes 688136 | tf_op jit(solution)/shard_map/ppermute | solution.py:87
  212.5 13.7 %collective-permute-start.11 = (bf16[2,128,448]{1,2,0:T(8,128)(2,1)S(1)}, bf16[2,128,448]{1,2,0:T(8,128)(2,1)S(1)}, u32[]{:S(2)}, u32[]{:S(2)}) collective-permute-start(bf16[2,128,448]{1,2,0:T(8,128)(2,1)S(1)} %get-tuple-element.39), channel_id=1, source_target_pairs={{0,3},{1,2},{2,1},{3,0},{4,7},{5,6},{6,5},{7,4},{8,11},{9,10},{10,... | collective-permute-start | bytes 688136 | tf_op jit(solution)/shard_map/ppermute | solution.py:87
  216.5 17.6 %collective-permute-start.9 = (bf16[2,128,448]{1,2,0:T(8,128)(2,1)S(1)}, bf16[2,128,448]{1,2,0:T(8,128)(2,1)}, u32[]{:S(2)}, u32[]{:S(2)}) collective-permute-start(bf16[2,128,448]{1,2,0:T(8,128)(2,1)S(1)} %get-tuple-element.38), channel_id=1, source_target_pairs={{0,1},{1,0},{2,3},{3,2},{4,5},{5,4},{6,7},{7,6},{8,9},{9,8},{10,11... | collective-permute-start | bytes 688136 | tf_op jit(solution)/shard_map/ppermute | solution.py:87
  218.4 28.0 %collective-permute-start.8 = (bf16[128,448]{0,1:T(8,128)(2,1)S(1)}, bf16[128,448]{0,1:T(8,128)(2,1)S(1)}, u32[]{:S(2)}, u32[]{:S(2)}) collective-permute-start(bf16[128,448]{0,1:T(8,128)(2,1)S(1)} %dynamic-slice_bitcast_fusion.8), channel_id=1, source_target_pairs={{0,4},{4,0},{1,5},{5,1},{2,6},{6,2},{3,7},{7,3},{8,12},{12,8},{9,1... | collective-permute-start | bytes 344072 | tf_op jit(solution)/shard_map/ppermute | solution.py:14
  235.2 11.8 %collective-permute-start.12 = (bf16[128,448]{0,1:T(8,128)(2,1)S(1)}, bf16[128,448]{0,1:T(8,128)(2,1)S(1)}, u32[]{:S(2)}, u32[]{:S(2)}) collective-permute-start(bf16[128,448]{0,1:T(8,128)(2,1)S(1)} %get-tuple-element.44), channel_id=1, source_target_pairs={{0,23},{1,22},{2,21},{3,20},{4,19},{5,18},{6,17},{7,16},{16,7},{17... | collective-permute-start | bytes 344072 | tf_op jit(solution)/shard_map/ppermute | solution.py:18
  238.9 19.2 %collective-permute-start.13 = (bf16[128,448]{0,1:T(8,128)(2,1)S(1)}, bf16[128,448]{0,1:T(8,128)(2,1)S(1)}, u32[]{:S(2)}, u32[]{:S(2)}) collective-permute-start(bf16[128,448]{0,1:T(8,128)(2,1)S(1)} %get-tuple-element.45), channel_id=1, source_target_pairs={{0,19},{1,18},{2,17},{3,16},{4,23},{5,22},{6,21},{7,20},{16,3},{17... | collective-permute-start | bytes 344072 | tf_op jit(solution)/shard_map/ppermute | solution.py:148

commit v8 on v7

--- a/solution.py
+++ b/solution.py
@@ -79,13 +79,15 @@
     return jnp.transpose(parts, (3, 2, 1, 0, 4)).reshape(near, 2, tok_rows, -1)
 
 
-def near_sum(parts, place, mine):
+def near_sum(parts, place, mine, beside):
     count = parts.shape[0]
-    total = lax.dynamic_index_in_dim(parts, place ^ mine, 0, keepdims=False).astype(jnp.float32)
+    own = lax.dynamic_index_in_dim(parts, place ^ mine, 0, keepdims=False)
+    own, beside = tied((own, beside))
+    total = own.astype(jnp.float32)
     for step in range(1, count):
         block = lax.dynamic_index_in_dim(parts, place ^ step ^ mine, 0, keepdims=False)
         total += lax.ppermute(block, NEAR, [(i, i ^ step) for i in range(count)]).astype(jnp.float32)
-    return total.astype(jnp.bfloat16)
+    return total.astype(jnp.bfloat16), beside
 
 
 tied = lax.optimization_barrier
@@ -128,16 +130,17 @@
     other_table = lax.all_gather(quarter, NEAR, tiled=True)
     payload, sent = tied((gather_rows(other_rows, other_table), sent))
     other_sent = exchange(payload)
-    payload, other_sent = tied((expert_part(sent, own), other_sent))
+    chosen = pick_pieces(spread, old_owner, new_owner, zh)
+    payload, other_sent, chosen = tied((expert_part(sent, own), other_sent, chosen))
     back = exchange(payload)
-    chosen = pick_pieces(spread, old_owner, new_owner, zh)
-    payload, back, chosen = tied((expert_part(other_sent, own), back, chosen))
+    payload, back = tied((expert_part(other_sent, own), back))
     other_back = exchange(payload)
 
-    kept = near_sum(by_columns(weighted(back, codes, rows), near), place, 0)
-    kept, other_back, chosen = tied((kept, other_back, chosen))
+    parts = by_columns(weighted(back, codes, rows), near)
+    kept, other_back = near_sum(parts, place, 0, other_back)
+    other_parts = by_columns(weighted(other_back, other_codes, other_rows), near)
+    other_kept, chosen = near_sum(other_parts, place, near - 1, chosen)
     arrived = lax.all_to_all(chosen, ("y", "x"), split_axis=0, concat_axis=0, tiled=True)
-    other_kept = near_sum(by_columns(weighted(other_back, other_codes, other_rows), near), place, near - 1)
 
     def of(value, index):
         return lax.dynamic_index_in_dim(value, index, 0, keepdims=False)

time: 263 us -> 239 us (0.909)
  waiting for transfers between devices: 79.9 us -> 71.7 us
  starting transfers between devices: 110 us -> 102 us
  local copies, waits for them, and re-layouts: 22.2 us -> 17.5 us
    ppermute x6, waiting for transfers between devices: 23.6 us -> 12.1 us  [near_sum(): lax.ppermute(block, NEAR, [(i, i ^ step) for i in range(count)])]
    ppermute x6, starting transfers between devices: 22.3 us -> 17.6 us  [near_sum(): lax.ppermute(block, NEAR, [(i, i ^ step) for i in range(count)])]
    all_to_all x4, waiting for transfers between devices: 17.4 us -> 21 us  [exchange(): lax.all_to_all(blocks, axes, split_axis=0, concat_axis=0, tiled=True)]
    reshape x4, local copies, waits for them, and re-layouts: 11.6 us -> 8.71 us  [by_columns(): parts = mixed.astype(jnp.bfloat16).reshape(2, tok_rows, 2, near, -1)]
  transfers between devices with their start and end apart: 20 -> 20, of which waited for: 11 -> 9; matrix products, arithmetic and copies ran while one was open for 17% -> 16% of each run, Pallas kernels for 0% -> 0%
where the time goes in v8:
time: 239 us; the launch traced here: 237 us
  starting transfers between devices  102 us (43%)
  waiting for transfers between devices  71.7 us (30%)
  blocking collectives  18 us (8%)
  matrix products  17.6 us (7%)
  local copies, waits for them, and re-layouts  17.5 us (7%)
  other arithmetic  5.65 us (2%)
  between operations  3.81 us (2%)
    all_to_all x4, starting transfers between devices, exchange(): lax.all_to_all(blocks, axes, split_axis=0, concat_axis=0, tiled=True)  30.3 us
    all_to_all x4, waiting for transfers between devices, exchange(): lax.all_to_all(blocks, axes, split_axis=0, concat_axis=0, tiled=True)  21 us
    all_gather x1, blocking collectives, shards(): other_table = lax.all_gather(quarter, NEAR, tiled=True)  18 us
    ppermute x6, starting transfers between devices, near_sum(): lax.ppermute(block, NEAR, [(i, i ^ step) for i in range(count)])  17.6 us
    ppermute x3, starting transfers between devices, mirrored(): return lax.ppermute(value, RING, [(i, 15 - i) for i in range(16)])  17.6 us
    ppermute x3, waiting for transfers between devices, mirrored(): return lax.ppermute(value, RING, [(i, 15 - i) for i in range(16)])  17.5 us
    ppermute x4, starting transfers between devices, swap(): return lax.ppermute(value, axis, [(0, 1), (1, 0)])  15.7 us
    ppermute x6, waiting for transfers between devices, near_sum(): lax.ppermute(block, NEAR, [(i, i ^ step) for i in range(count)])  12.1 us
  transfers between devices with their start and end apart: 20, of which 9 were waited for; matrix products, arithmetic and copies ran while one was open for 16% of the time, Pallas kernels for 0%

profile of v8, /device:TPU:1, one launch (start us, length us, event | category | flops | bytes accessed | tf_op | source)
XLA Modules:
  0.0 236.8 jit_solution(13907131946793928905)
XLA Ops:
  0.6 7.7 %all-to-all-start = ((bf16[16,336,128]{2,1,0:T(8,128)(2,1)}), bf16[16,336,128]{2,1,0:T(8,128)(2,1)S(1)}, u32[]{:S(2)}, u32[]{:S(2)}) async-start(bf16[16,336,128]{2,1,0:T(8,128)(2,1)} %bitcast.112), calls=%async_computation | async-start | bytes 2752512 | tf_op jit(solution)/shard_map/all_to_all | solution.py:123
  10.0 1.3 reshape.274
  11.3 11.1 %collective-permute-start = (bf16[64,1792]{1,0:T(8,128)(2,1)S(1)}, bf16[64,1792]{1,0:T(8,128)(2,1)S(1)}, u32[]{:S(2)}, u32[]{:S(2)}) collective-permute-start(bf16[64,1792]{1,0:T(8,128)(2,1)S(1)} %constant_dynamic-slice_fusion), channel_id=1, source_target_pairs={{0,23},{1,22},{2,21},{3,20},{4,19},{5,18},{6,17},{7,16},{16,7},{17... | collective-permute-start | bytes 688136 | tf_op jit(solution)/shard_map/ppermute | solution.py:18
  23.4 1.9 convolution_convert_fusion.1
  25.3 17.5 %collective-permute-done = bf16[64,1792]{1,0:T(8,128)(2,1)S(1)} collective-permute-done((bf16[64,1792]{1,0:T(8,128)(2,1)S(1)}, bf16[64,1792]{1,0:T(8,128)(2,1)S(1)}, u32[]{:S(2)}, u32[]{:S(2)}) %collective-permute-start) | collective-permute-done | bytes 229408 | tf_op jit(solution)/shard_map/ppermute | solution.py:18
  42.8 7.9 %all-to-all-start.1 = ((bf16[32,16,1792]{2,1,0:T(8,128)(2,1)}), bf16[32,16,1792]{2,1,0:T(8,128)(2,1)S(1)}, u32[]{:S(2)}, u32[]{:S(2)}) async-start(bf16[32,16,1792]{2,1,0:T(8,128)(2,1)} %bitcast.16), calls=%async_computation.1 | async-start | bytes 3670016 | tf_op jit(solution)/shard_map/all_to_all | solution.py:53
  50.7 4.6 %collective-permute-start.1 = (f32[4,128]{1,0:T(4,128)S(1)}, f32[4,128]{1,0:T(4,128)S(1)}, u32[]{:S(2)}, u32[]{:S(2)}) collective-permute-start(f32[4,128]{1,0:T(4,128)S(1)} %pad_maximum_fusion), channel_id=1, source_target_pairs={{0,23},{1,22},{2,21},{3,20},{4,19},{5,18},{6,17},{7,16},{16,7},{17... | collective-permute-start | bytes 6152 | tf_op jit(solution)/shard_map/ppermute | solution.py:18
  55.3 18.0 %all_gather.3 = bf16[256,1792]{1,0:T(8,128)(2,1)S(1)} all-gather(bf16[64,1792]{1,0:T(8,128)(2,1)S(1)} %collective-permute-done), channel_id=1, replica_groups=mesh['y'=4,'x'=4,'zh'=2,'c'=2,'ma'=2,'mb'=2,'mc'=2] {'mb','mc'}, dimensions={0}, use_global_device_ids=true | all-gather | bytes 1146880 | tf_op jit(solution)/shard_map/all_gather | solution.py:130
  73.4 1.9 convolution_convert_fusion
  75.6 1.3 copy-done.3
  76.9 8.8 %all-to-all-start.2 = ((bf16[32,16,1792]{2,1,0:T(8,128)(2,1)}), bf16[32,16,1792]{2,1,0:T(8,128)(2,1)}, u32[]{:S(2)}, u32[]{:S(2)}) async-start(bf16[32,16,1792]{2,1,0:T(8,128)(2,1)} %bitcast.23), calls=%async_computation.2 | async-start | bytes 3670016 | tf_op jit(solution)/shard_map/all_to_all | solution.py:53
  88.3 1.3 fusion.69
  89.6 6.8 %collective-permute-start.3 = (bf16[336,128]{1,0:T(8,128)(2,1)S(1)}, bf16[336,128]{1,0:T(8,128)(2,1)S(1)}, u32[]{:S(2)}, u32[]{:S(2)}) collective-permute-start(bf16[336,128]{1,0:T(8,128)(2,1)S(1)} %bitcast_select_fusion.1), channel_id=1, source_target_pairs={{0,16},{16,0},{1,17},{17,1},{2,18},{18,2},{3,19},{19,3},{4,20},{20... | collective-permute-start | bytes 258056 | tf_op jit(solution)/shard_map/ppermute | solution.py:14
  96.4 2.1 fusion.6
  98.6 2.6 %collective-permute-start.2 = (f32[2,512,128]{2,1,0:T(8,128)S(1)}, f32[2,512,128]{2,1,0:T(8,128)S(1)}, u32[]{:S(2)}, u32[]{:S(2)}) collective-permute-start(f32[2,512,128]{2,1,0:T(8,128)S(1)} %fusion.6), channel_id=1, source_target_pairs={{0,8},{8,0},{1,9},{9,1},{2,10},{10,2},{3,11},{11,3},{4,12},{12,4},... | collective-permute-start | bytes 1572872 | tf_op jit(solution)/shard_map/ppermute | solution.py:14
  101.2 8.2 %collective-permute-done.3 = bf16[336,128]{1,0:T(8,128)(2,1)S(1)} collective-permute-done((bf16[336,128]{1,0:T(8,128)(2,1)S(1)}, bf16[336,128]{1,0:T(8,128)(2,1)S(1)}, u32[]{:S(2)}, u32[]{:S(2)}) %collective-permute-start.3) | collective-permute-done | bytes 86048 | tf_op jit(solution)/shard_map/ppermute | solution.py:14
  109.5 1.3 select_select_fusion
  110.9 1.9 convolution_convert_fusion.3
  112.8 7.6 %all-to-all-start.3 = ((bf16[32,16,1792]{2,1,0:T(8,128)(2,1)}), bf16[32,16,1792]{2,1,0:T(8,128)(2,1)S(1)}, u32[]{:S(2)}, u32[]{:S(2)}) async-start(bf16[32,16,1792]{2,1,0:T(8,128)(2,1)} %bitcast.110), calls=%async_computation.3 | async-start | bytes 3670016 | tf_op jit(solution)/shard_map/all_to_all | solution.py:53
  120.4 2.1 fusion.9
  122.6 2.1 collective-permute-start.4
  124.7 1.7 collective-permute-done.4
  126.5 1.9 convolution_convert_fusion.2
  128.3 17.0 %all-to-all-done.3 = bf16[32,16,1792]{2,1,0:T(8,128)(2,1)S(1)} async-done(((bf16[32,16,1792]{2,1,0:T(8,128)(2,1)}), bf16[32,16,1792]{2,1,0:T(8,128)(2,1)S(1)}, u32[]{:S(2)}, u32[]{:S(2)}) %all-to-all-start.3) | async-done | bytes 1835040 | tf_op jit(solution)/shard_map/all_to_all | solution.py:53
  145.3 1.2 copy-done
  146.6 5.9 %all-to-all-start.4 = ((bf16[32,16,1792]{2,1,0:T(8,128)(2,1)}), bf16[32,16,1792]{2,1,0:T(8,128)(2,1)S(1)}, u32[]{:S(2)}, u32[]{:S(2)}) async-start(bf16[32,16,1792]{2,1,0:T(8,128)(2,1)} %bitcast.109), calls=%async_computation.4 | async-start | bytes 3670016 | tf_op jit(solution)/shard_map/all_to_all | solution.py:53
  152.6 2.4 %fusion.45 = f32[256,1792]{1,0:T(8,128)S(1)} fusion(bf16[512,1792]{1,0:T(8,128)(2,1)} %bitcast.107, f32[256]{0:T(256)S(1)} %bitcast.131, s32[256]{0:T(256)S(1)} %get-tuple-element.53, f32[256]{0:T(256)S(1)} %bitcast.129, s32[256]{0:T(256)S(1)} %get-tuple-element.52), kind=kOutput, calls=%fused_computation.63 | convolution fusion | flops 470548480 | bytes 3674112 | tf_op jit(solution)/shard_map/dot_general | solution.py:71
  155.0 1.7 fusion
  156.7 3.5 %reshape.275 = bf16[2,128,2,4,224]{4,3,2,1,0:T(4,128)(2,1)S(1)} reshape(bf16[256,1792]{1,0:T(8,128)(2,1)} %fusion) | data formatting | bytes 1835008 | tf_op jit(solution)/shard_map/reshape | solution.py:78
  160.2 2.3 copy.18
  162.5 1.3 copy.13
  164.5 1.9 collective-permute-start.5
  166.5 2.9 %collective-permute-start.6 = (bf16[2,128,448]{1,2,0:T(8,128)(2,1)S(1)}, bf16[2,128,448]{1,2,0:T(8,128)(2,1)}, u32[]{:S(2)}, u32[]{:S(2)}) collective-permute-start(bf16[2,128,448]{1,2,0:T(8,128)(2,1)S(1)} %get-tuple-element.42), channel_id=1, source_target_pairs={{0,2},{1,3},{2,0},{3,1},{4,6},{5,7},{6,4},{7,5},{8,10},{9,11},{10,... | collective-permute-start | bytes 688136 | tf_op jit(solution)/shard_map/ppermute | solution.py:89
  169.4 4.5 %collective-permute-start.7 = (bf16[2,128,448]{1,2,0:T(8,128)(2,1)S(1)}, bf16[2,128,448]{1,2,0:T(8,128)(2,1)}, u32[]{:S(2)}, u32[]{:S(2)}) collective-permute-start(bf16[2,128,448]{1,2,0:T(8,128)(2,1)S(1)} %get-tuple-element.41), channel_id=1, source_target_pairs={{0,3},{1,2},{2,1},{3,0},{4,7},{5,6},{6,5},{7,4},{8,11},{9,10},{10,... | collective-permute-start | bytes 688136 | tf_op jit(solution)/shard_map/ppermute | solution.py:89
  173.8 3.6 %all-to-all-done.4 = bf16[32,16,1792]{2,1,0:T(8,128)(2,1)S(1)} async-done(((bf16[32,16,1792]{2,1,0:T(8,128)(2,1)}), bf16[32,16,1792]{2,1,0:T(8,128)(2,1)S(1)}, u32[]{:S(2)}, u32[]{:S(2)}) %all-to-all-start.4) | async-done | bytes 1835040 | tf_op jit(solution)/shard_map/all_to_all | solution.py:53
  179.0 1.5 reshape.276
  180.4 1.4 copy.19
  182.1 4.5 %all-to-all-start.5 = ((bf16[16,336,128]{2,1,0:T(8,128)(2,1)}), bf16[16,336,128]{2,1,0:T(8,128)(2,1)S(1)}, u32[]{:S(2)}, u32[]{:S(2)}) async-start(bf16[16,336,128]{2,1,0:T(8,128)(2,1)} %select_select_fusion), calls=%async_computation.5 | async-start | bytes 2752512 | tf_op jit(solution)/shard_map/all_to_all | solution.py:143
  186.6 1.9 collective-permute-start.10
  188.5 2.6 %collective-permute-start.11 = (bf16[2,128,448]{1,2,0:T(8,128)(2,1)S(1)}, bf16[2,128,448]{1,2,0:T(8,128)(2,1)S(1)}, u32[]{:S(2)}, u32[]{:S(2)}) collective-permute-start(bf16[2,128,448]{1,2,0:T(8,128)(2,1)S(1)} %get-tuple-element.45), channel_id=1, source_target_pairs={{0,3},{1,2},{2,1},{3,0},{4,7},{5,6},{6,5},{7,4},{8,11},{9,10},{10,... | collective-permute-start | bytes 688136 | tf_op jit(solution)/shard_map/ppermute | solution.py:89
  191.2 3.8 %collective-permute-start.9 = (bf16[2,128,448]{1,2,0:T(8,128)(2,1)S(1)}, bf16[2,128,448]{1,2,0:T(8,128)(2,1)S(1)}, u32[]{:S(2)}, u32[]{:S(2)}) collective-permute-start(bf16[2,128,448]{1,2,0:T(8,128)(2,1)S(1)} %get-tuple-element.47), channel_id=1, source_target_pairs={{0,1},{1,0},{2,3},{3,2},{4,5},{5,4},{6,7},{7,6},{8,9},{9,8},{10,11... | collective-permute-start | bytes 688136 | tf_op jit(solution)/shard_map/ppermute | solution.py:89
  195.0 1.3 add_convert_fusion.1
  196.3 4.2 %collective-permute-start.8 = (bf16[128,448]{0,1:T(8,128)(2,1)S(1)}, bf16[128,448]{0,1:T(8,128)(2,1)S(1)}, u32[]{:S(2)}, u32[]{:S(2)}) collective-permute-start(bf16[128,448]{0,1:T(8,128)(2,1)S(1)} %dynamic-slice_bitcast_fusion.10), channel_id=1, source_target_pairs={{0,4},{4,0},{1,5},{5,1},{2,6},{6,2},{3,7},{7,3},{8,12},{12,8},{9,1... | collective-permute-start | bytes 344072 | tf_op jit(solution)/shard_map/ppermute | solution.py:14
  200.5 6.2 %collective-permute-done.10 = bf16[2,128,448]{1,2,0:T(8,128)(2,1)S(1)} collective-permute-done((bf16[2,128,448]{1,2,0:T(8,128)(2,1)S(1)}, bf16[2,128,448]{1,2,0:T(8,128)(2,1)S(1)}, u32[]{:S(2)}, u32[]{:S(2)}) %collective-permute-start.10) | collective-permute-done | bytes 229408 | tf_op jit(solution)/shard_map/ppermute | solution.py:89
  206.7 5.9 %collective-permute-done.9 = bf16[2,128,448]{1,2,0:T(8,128)(2,1)S(1)} collective-permute-done((bf16[2,128,448]{1,2,0:T(8,128)(2,1)S(1)}, bf16[2,128,448]{1,2,0:T(8,128)(2,1)S(1)}, u32[]{:S(2)}, u32[]{:S(2)}) %collective-permute-start.9) | collective-permute-done | bytes 229408 | tf_op jit(solution)/shard_map/ppermute | solution.py:89
  212.8 1.9 collective-permute-start.12
  214.7 9.0 %collective-permute-start.13 = (bf16[128,448]{0,1:T(8,128)(2,1)S(1)}, bf16[128,448]{0,1:T(8,128)(2,1)S(1)}, u32[]{:S(2)}, u32[]{:S(2)}) collective-permute-start(bf16[128,448]{0,1:T(8,128)(2,1)S(1)} %get-tuple-element.49), channel_id=1, source_target_pairs={{0,19},{1,18},{2,17},{3,16},{4,23},{5,22},{6,21},{7,20},{16,3},{17... | collective-permute-start | bytes 344072 | tf_op jit(solution)/shard_map/ppermute | solution.py:151
  223.7 11.2 %collective-permute-done.13 = bf16[128,448]{0,1:T(8,128)(2,1)S(1)} collective-permute-done((bf16[128,448]{0,1:T(8,128)(2,1)S(1)}, bf16[128,448]{0,1:T(8,128)(2,1)S(1)}, u32[]{:S(2)}, u32[]{:S(2)}) %collective-permute-start.13) | collective-permute-done | bytes 114720 | tf_op jit(solution)/shard_map/ppermute | solution.py:151
  (56 shorter events, 7.5 us)
Async XLA Ops:
  0.6 7.8 %copy-start.4 = (bf16[128,3584]{1,0:T(8,128)(2,1)S(1)}, bf16[128,3584]{1,0:T(8,128)(2,1)}, u32[]{:S(2)}) copy-start(bf16[128,3584]{1,0:T(8,128)(2,1)} %param.6) | copy-start | bytes 2752516
  0.6 42.1 %all-to-all-start = ((bf16[16,336,128]{2,1,0:T(8,128)(2,1)}), bf16[16,336,128]{2,1,0:T(8,128)(2,1)S(1)}, u32[]{:S(2)}, u32[]{:S(2)}) async-start(bf16[16,336,128]{2,1,0:T(8,128)(2,1)} %bitcast.112), calls=%async_computation | async-start | bytes 2752512 | tf_op jit(solution)/shard_map/all_to_all | solution.py:123
  9.0 13.4 %copy-start.6 = (s32[32]{0:T(128)S(1)}, s32[32]{0:T(128)}, u32[]{:S(2)}) copy-start(s32[32]{0:T(128)} %param.10) | copy-start | bytes 388
  9.0 13.4 %copy-start.7 = (s32[32]{0:T(128)S(1)}, s32[32]{0:T(128)}, u32[]{:S(2)}) copy-start(s32[32]{0:T(128)} %param.11) | copy-start | bytes 388
  9.0 14.1 %copy-start.8 = (s32[128,2]{0,1:T(2,128)S(1)}, s32[128,2]{0,1:T(2,128)}, u32[]{:S(2)}) copy-start(s32[128,2]{0,1:T(2,128)} %param.7) | copy-start | bytes 3076
  9.0 14.3 %copy-start.5 = (f32[128,2]{0,1:T(2,128)S(1)}, f32[128,2]{0,1:T(2,128)}, u32[]{:S(2)}) copy-start(f32[128,2]{0,1:T(2,128)} %param.8) | copy-start | bytes 3076
  11.3 31.5 %collective-permute-start = (bf16[64,1792]{1,0:T(8,128)(2,1)S(1)}, bf16[64,1792]{1,0:T(8,128)(2,1)S(1)}, u32[]{:S(2)}, u32[]{:S(2)}) collective-permute-start(bf16[64,1792]{1,0:T(8,128)(2,1)S(1)} %constant_dynamic-slice_fusion), channel_id=1, source_target_pairs={{0,23},{1,22},{2,21},{3,20},{4,19},{5,18},{6,17},{7,16},{16,7},{17... | collective-permute-start | bytes 688136 | tf_op jit(solution)/shard_map/ppermute | solution.py:18
  42.8 32.8 %all-to-all-start.1 = ((bf16[32,16,1792]{2,1,0:T(8,128)(2,1)}), bf16[32,16,1792]{2,1,0:T(8,128)(2,1)S(1)}, u32[]{:S(2)}, u32[]{:S(2)}) async-start(bf16[32,16,1792]{2,1,0:T(8,128)(2,1)} %bitcast.16), calls=%async_computation.1 | async-start | bytes 3670016 | tf_op jit(solution)/shard_map/all_to_all | solution.py:53
  50.7 22.6 %collective-permute-start.1 = (f32[4,128]{1,0:T(4,128)S(1)}, f32[4,128]{1,0:T(4,128)S(1)}, u32[]{:S(2)}, u32[]{:S(2)}) collective-permute-start(f32[4,128]{1,0:T(4,128)S(1)} %pad_maximum_fusion), channel_id=1, source_target_pairs={{0,23},{1,22},{2,21},{3,20},{4,19},{5,18},{6,17},{7,16},{16,7},{17... | collective-permute-start | bytes 6152 | tf_op jit(solution)/shard_map/ppermute | solution.py:18
  75.6 1.3 copy-start.3
  76.9 19.5 %copy-start.2 = (bf16[1,3,1792,128]{3,2,1,0:T(8,128)(2,1)S(1)}, bf16[1,3,1792,128]{3,2,1,0:T(8,128)(2,1)}, u32[]{:S(2)}) copy-start(bf16[1,3,1792,128]{3,2,1,0:T(8,128)(2,1)} %param.9) | copy-start | bytes 4128772
  76.9 35.9 %all-to-all-start.2 = ((bf16[32,16,1792]{2,1,0:T(8,128)(2,1)}), bf16[32,16,1792]{2,1,0:T(8,128)(2,1)}, u32[]{:S(2)}, u32[]{:S(2)}) async-start(bf16[32,16,1792]{2,1,0:T(8,128)(2,1)} %bitcast.23), calls=%async_computation.2 | async-start | bytes 3670016 | tf_op jit(solution)/shard_map/all_to_all | solution.py:53
  89.6 19.8 %collective-permute-start.3 = (bf16[336,128]{1,0:T(8,128)(2,1)S(1)}, bf16[336,128]{1,0:T(8,128)(2,1)S(1)}, u32[]{:S(2)}, u32[]{:S(2)}) collective-permute-start(bf16[336,128]{1,0:T(8,128)(2,1)S(1)} %bitcast_select_fusion.1), channel_id=1, source_target_pairs={{0,16},{16,0},{1,17},{17,1},{2,18},{18,2},{3,19},{19,3},{4,20},{20... | collective-permute-start | bytes 258056 | tf_op jit(solution)/shard_map/ppermute | solution.py:14
  98.6 12.2 %collective-permute-start.2 = (f32[2,512,128]{2,1,0:T(8,128)S(1)}, f32[2,512,128]{2,1,0:T(8,128)S(1)}, u32[]{:S(2)}, u32[]{:S(2)}) collective-permute-start(f32[2,512,128]{2,1,0:T(8,128)S(1)} %fusion.6), channel_id=1, source_target_pairs={{0,8},{8,0},{1,9},{9,1},{2,10},{10,2},{3,11},{11,3},{4,12},{12,4},... | collective-permute-start | bytes 1572872 | tf_op jit(solution)/shard_map/ppermute | solution.py:14
  112.8 32.6 %all-to-all-start.3 = ((bf16[32,16,1792]{2,1,0:T(8,128)(2,1)}), bf16[32,16,1792]{2,1,0:T(8,128)(2,1)S(1)}, u32[]{:S(2)}, u32[]{:S(2)}) async-start(bf16[32,16,1792]{2,1,0:T(8,128)(2,1)} %bitcast.110), calls=%async_computation.3 | async-start | bytes 3670016 | tf_op jit(solution)/shard_map/all_to_all | solution.py:53
  122.6 3.8 %collective-permute-start.4 = (f32[2,512,128]{2,1,0:T(8,128)S(1)}, f32[2,512,128]{2,1,0:T(8,128)S(1)}, u32[]{:S(2)}, u32[]{:S(2)}) collective-permute-start(f32[2,512,128]{2,1,0:T(8,128)S(1)} %fusion.9), channel_id=1, source_target_pairs={{0,8},{8,0},{1,9},{9,1},{2,10},{10,2},{3,11},{11,3},{4,12},{12,4},... | collective-permute-start | bytes 1572872 | tf_op jit(solution)/shard_map/ppermute | solution.py:14
  145.3 1.2 copy-start
  146.6 30.9 %all-to-all-start.4 = ((bf16[32,16,1792]{2,1,0:T(8,128)(2,1)}), bf16[32,16,1792]{2,1,0:T(8,128)(2,1)S(1)}, u32[]{:S(2)}, u32[]{:S(2)}) async-start(bf16[32,16,1792]{2,1,0:T(8,128)(2,1)} %bitcast.109), calls=%async_computation.4 | async-start | bytes 3670016 | tf_op jit(solution)/shard_map/all_to_all | solution.py:53
  152.6 2.4 %copy-start.1 = (bf16[32,16,1792]{2,1,0:T(8,128)(2,1)S(1)}, bf16[32,16,1792]{2,1,0:T(8,128)(2,1)}, u32[]{:S(2)}) copy-start(bf16[32,16,1792]{2,1,0:T(8,128)(2,1)} %copy-done) | copy-start | bytes 5505028
  164.5 26.6 %collective-permute-start.5 = (bf16[2,128,448]{1,2,0:T(8,128)(2,1)}, bf16[2,128,448]{1,2,0:T(8,128)(2,1)}, u32[]{:S(2)}, u32[]{:S(2)}) collective-permute-start(bf16[2,128,448]{1,2,0:T(8,128)(2,1)} %get-tuple-element.40), channel_id=1, source_target_pairs={{0,1},{1,0},{2,3},{3,2},{4,5},{5,4},{6,7},{7,6},{8,9},{9,8},{10,11... | collective-permute-start | bytes 688136 | tf_op jit(solution)/shard_map/ppermute | solution.py:89
  166.5 28.6 %collective-permute-start.6 = (bf16[2,128,448]{1,2,0:T(8,128)(2,1)S(1)}, bf16[2,128,448]{1,2,0:T(8,128)(2,1)}, u32[]{:S(2)}, u32[]{:S(2)}) collective-permute-start(bf16[2,128,448]{1,2,0:T(8,128)(2,1)S(1)} %get-tuple-element.42), channel_id=1, source_target_pairs={{0,2},{1,3},{2,0},{3,1},{4,6},{5,7},{6,4},{7,5},{8,10},{9,11},{10,... | collective-permute-start | bytes 688136 | tf_op jit(solution)/shard_map/ppermute | solution.py:89
  169.4 25.7 %collective-permute-start.7 = (bf16[2,128,448]{1,2,0:T(8,128)(2,1)S(1)}, bf16[2,128,448]{1,2,0:T(8,128)(2,1)}, u32[]{:S(2)}, u32[]{:S(2)}) collective-permute-start(bf16[2,128,448]{1,2,0:T(8,128)(2,1)S(1)} %get-tuple-element.41), channel_id=1, source_target_pairs={{0,3},{1,2},{2,1},{3,0},{4,7},{5,6},{6,5},{7,4},{8,11},{9,10},{10,... | collective-permute-start | bytes 688136 | tf_op jit(solution)/shard_map/ppermute | solution.py:89
  182.1 53.6 %all-to-all-start.5 = ((bf16[16,336,128]{2,1,0:T(8,128)(2,1)}), bf16[16,336,128]{2,1,0:T(8,128)(2,1)S(1)}, u32[]{:S(2)}, u32[]{:S(2)}) async-start(bf16[16,336,128]{2,1,0:T(8,128)(2,1)} %select_select_fusion), calls=%async_computation.5 | async-start | bytes 2752512 | tf_op jit(solution)/shard_map/all_to_all | solution.py:143
  186.6 20.1 %collective-permute-start.10 = (bf16[2,128,448]{1,2,0:T(8,128)(2,1)S(1)}, bf16[2,128,448]{1,2,0:T(8,128)(2,1)S(1)}, u32[]{:S(2)}, u32[]{:S(2)}) collective-permute-start(bf16[2,128,448]{1,2,0:T(8,128)(2,1)S(1)} %get-tuple-element.46), channel_id=1, source_target_pairs={{0,2},{1,3},{2,0},{3,1},{4,6},{5,7},{6,4},{7,5},{8,10},{9,11},{10,... | collective-permute-start | bytes 688136 | tf_op jit(solution)/shard_map/ppermute | solution.py:89
  188.5 18.2 %collective-permute-start.11 = (bf16[2,128,448]{1,2,0:T(8,128)(2,1)S(1)}, bf16[2,128,448]{1,2,0:T(8,128)(2,1)S(1)}, u32[]{:S(2)}, u32[]{:S(2)}) collective-permute-start(bf16[2,128,448]{1,2,0:T(8,128)(2,1)S(1)} %get-tuple-element.45), channel_id=1, source_target_pairs={{0,3},{1,2},{2,1},{3,0},{4,7},{5,6},{6,5},{7,4},{8,11},{9,10},{10,... | collective-permute-start | bytes 688136 | tf_op jit(solution)/shard_map/ppermute | solution.py:89
  191.2 21.4 %collective-permute-start.9 = (bf16[2,128,448]{1,2,0:T(8,128)(2,1)S(1)}, bf16[2,128,448]{1,2,0:T(8,128)(2,1)S(1)}, u32[]{:S(2)}, u32[]{:S(2)}) collective-permute-start(bf16[2,128,448]{1,2,0:T(8,128)(2,1)S(1)} %get-tuple-element.47), channel_id=1, source_target_pairs={{0,1},{1,0},{2,3},{3,2},{4,5},{5,4},{6,7},{7,6},{8,9},{9,8},{10,11... | collective-permute-start | bytes 688136 | tf_op jit(solution)/shard_map/ppermute | solution.py:89
  196.3 27.4 %collective-permute-start.8 = (bf16[128,448]{0,1:T(8,128)(2,1)S(1)}, bf16[128,448]{0,1:T(8,128)(2,1)S(1)}, u32[]{:S(2)}, u32[]{:S(2)}) collective-permute-start(bf16[128,448]{0,1:T(8,128)(2,1)S(1)} %dynamic-slice_bitcast_fusion.10), channel_id=1, source_target_pairs={{0,4},{4,0},{1,5},{5,1},{2,6},{6,2},{3,7},{7,3},{8,12},{12,8},{9,1... | collective-permute-start | bytes 344072 | tf_op jit(solution)/shard_map/ppermute | solution.py:14
  212.8 11.0 %collective-permute-start.12 = (bf16[128,448]{0,1:T(8,128)(2,1)S(1)}, bf16[128,448]{0,1:T(8,128)(2,1)S(1)}, u32[]{:S(2)}, u32[]{:S(2)}) collective-permute-start(bf16[128,448]{0,1:T(8,128)(2,1)S(1)} %get-tuple-element.48), channel_id=1, source_target_pairs={{0,23},{1,22},{2,21},{3,20},{4,19},{5,18},{6,17},{7,16},{16,7},{17... | collective-permute-start | bytes 344072 | tf_op jit(solution)/shard_map/ppermute | solution.py:18
  214.7 20.3 %collective-permute-start.13 = (bf16[128,448]{0,1:T(8,128)(2,1)S(1)}, bf16[128,448]{0,1:T(8,128)(2,1)S(1)}, u32[]{:S(2)}, u32[]{:S(2)}) collective-permute-start(bf16[128,448]{0,1:T(8,128)(2,1)S(1)} %get-tuple-element.49), channel_id=1, source_target_pairs={{0,19},{1,18},{2,17},{3,16},{4,23},{5,22},{6,21},{7,20},{16,3},{17... | collective-permute-start | bytes 344072 | tf_op jit(solution)/shard_map/ppermute | solution.py:151

commit v9 on v8

--- a/solution.py
+++ b/solution.py
@@ -123,9 +123,9 @@
     spread = lax.all_to_all(
         own.reshape(chips, -1, own.shape[-1]), ("y", "x"), split_axis=0, concat_axis=0, tiled=True
     )
-    payload, spread, quarter, later_codes = tied((gather_rows(rows, table), spread, quarter, codes))
+    other_codes = mirrored(codes)
+    payload, spread, quarter, other_codes = tied((gather_rows(rows, table), spread, quarter, other_codes))
     sent = exchange(payload)
-    other_codes = mirrored(later_codes)
     other_rows = placed_rows(other_codes, zh)
     other_table = lax.all_gather(quarter, NEAR, tiled=True)
     payload, sent = tied((gather_rows(other_rows, other_table), sent))

time: 239 us -> 238 us (level)
    all_to_all x4, waiting for transfers between devices: 21 us -> 24.9 us  [exchange(): lax.all_to_all(blocks, axes, split_axis=0, concat_axis=0, tiled=True)]
    ppermute x3, starting transfers between devices: 17.6 us -> 15 us  [mirrored(): return lax.ppermute(value, RING, [(i, 15 - i) for i in range(16)])]
    ppermute x4, starting transfers between devices: 15.7 us -> 18.1 us  [swap(): return lax.ppermute(value, axis, [(0, 1), (1, 0)])]
where the time goes in v9:
time: 238 us; the launch traced here: 234 us
  starting transfers between devices  101 us (42%)
  waiting for transfers between devices  70.2 us (29%)
  blocking collectives  18.6 us (8%)
  matrix products  17.7 us (7%)
  local copies, waits for them, and re-layouts  17.5 us (7%)
  other arithmetic  5.65 us (2%)
  between operations  3.81 us (2%)
    all_to_all x4, starting transfers between devices, exchange(): lax.all_to_all(blocks, axes, split_axis=0, concat_axis=0, tiled=True)  28.2 us
    all_to_all x4, waiting for transfers between devices, exchange(): lax.all_to_all(blocks, axes, split_axis=0, concat_axis=0, tiled=True)  24.9 us
    all_gather x1, blocking collectives, shards(): other_table = lax.all_gather(quarter, NEAR, tiled=True)  18.6 us
    ppermute x4, starting transfers between devices, swap(): return lax.ppermute(value, axis, [(0, 1), (1, 0)])  18.1 us
    ppermute x6, starting transfers between devices, near_sum(): lax.ppermute(block, NEAR, [(i, i ^ step) for i in range(count)])  17.6 us
    ppermute x3, waiting for transfers between devices, mirrored(): return lax.ppermute(value, RING, [(i, 15 - i) for i in range(16)])  15.8 us
    ppermute x3, starting transfers between devices, mirrored(): return lax.ppermute(value, RING, [(i, 15 - i) for i in range(16)])  15 us
    ppermute x6, waiting for transfers between devices, near_sum(): lax.ppermute(block, NEAR, [(i, i ^ step) for i in range(count)])  11.1 us
  transfers between devices with their start and end apart: 20, of which 9 were waited for; matrix products, arithmetic and copies ran while one was open for 16% of the time, Pallas kernels for 0%

profile of v9, /device:TPU:1, one launch (start us, length us, event | category | flops | bytes accessed | tf_op | source)
XLA Modules:
  0.0 234.2 jit_solution(9027821609001539932)
XLA Ops:
  0.6 7.7 %all-to-all-start = ((bf16[16,336,128]{2,1,0:T(8,128)(2,1)}), bf16[16,336,128]{2,1,0:T(8,128)(2,1)S(1)}, u32[]{:S(2)}, u32[]{:S(2)}) async-start(bf16[16,336,128]{2,1,0:T(8,128)(2,1)} %bitcast.112), calls=%async_computation | async-start | bytes 2752512 | tf_op jit(solution)/shard_map/all_to_all | solution.py:123
  10.0 1.3 reshape.274
  11.3 11.1 %collective-permute-start = (bf16[64,1792]{1,0:T(8,128)(2,1)S(1)}, bf16[64,1792]{1,0:T(8,128)(2,1)S(1)}, u32[]{:S(2)}, u32[]{:S(2)}) collective-permute-start(bf16[64,1792]{1,0:T(8,128)(2,1)S(1)} %constant_dynamic-slice_fusion), channel_id=1, source_target_pairs={{0,23},{1,22},{2,21},{3,20},{4,19},{5,18},{6,17},{7,16},{16,7},{17... | collective-permute-start | bytes 688136 | tf_op jit(solution)/shard_map/ppermute | solution.py:18
  23.3 1.9 collective-permute-start.1
  25.3 1.9 convolution_convert_fusion.1
  27.2 15.7 %collective-permute-done.1 = f32[4,128]{1,0:T(4,128)S(1)} collective-permute-done((f32[4,128]{1,0:T(4,128)S(1)}, f32[4,128]{1,0:T(4,128)S(1)}, u32[]{:S(2)}, u32[]{:S(2)}) %collective-permute-start.1) | collective-permute-done | bytes 2080 | tf_op jit(solution)/shard_map/ppermute | solution.py:18
  43.0 7.9 %all-to-all-start.1 = ((bf16[32,16,1792]{2,1,0:T(8,128)(2,1)}), bf16[32,16,1792]{2,1,0:T(8,128)(2,1)S(1)}, u32[]{:S(2)}, u32[]{:S(2)}) async-start(bf16[32,16,1792]{2,1,0:T(8,128)(2,1)} %bitcast.16), calls=%async_computation.1 | async-start | bytes 3670016 | tf_op jit(solution)/shard_map/all_to_all | solution.py:53
  50.9 18.6 %all_gather.3 = bf16[256,1792]{1,0:T(8,128)(2,1)S(1)} all-gather(bf16[64,1792]{1,0:T(8,128)(2,1)S(1)} %collective-permute-done), channel_id=1, replica_groups=mesh['y'=4,'x'=4,'zh'=2,'c'=2,'ma'=2,'mb'=2,'mc'=2] {'mb','mc'}, dimensions={0}, use_global_device_ids=true | all-gather | bytes 1146880 | tf_op jit(solution)/shard_map/all_gather | solution.py:130
  69.6 1.9 convolution_convert_fusion
  71.5 4.3 %all-to-all-done.1 = bf16[32,16,1792]{2,1,0:T(8,128)(2,1)S(1)} async-done(((bf16[32,16,1792]{2,1,0:T(8,128)(2,1)}), bf16[32,16,1792]{2,1,0:T(8,128)(2,1)S(1)}, u32[]{:S(2)}, u32[]{:S(2)}) %all-to-all-start.1) | async-done | bytes 1835040 | tf_op jit(solution)/shard_map/all_to_all | solution.py:53
  75.8 1.3 copy-done.3
  77.1 6.7 %all-to-all-start.2 = ((bf16[32,16,1792]{2,1,0:T(8,128)(2,1)}), bf16[32,16,1792]{2,1,0:T(8,128)(2,1)}, u32[]{:S(2)}, u32[]{:S(2)}) async-start(bf16[32,16,1792]{2,1,0:T(8,128)(2,1)} %bitcast.23), calls=%async_computation.2 | async-start | bytes 3670016 | tf_op jit(solution)/shard_map/all_to_all | solution.py:53
  86.4 1.3 fusion.69
  87.7 8.9 %collective-permute-start.3 = (bf16[336,128]{1,0:T(8,128)(2,1)S(1)}, bf16[336,128]{1,0:T(8,128)(2,1)S(1)}, u32[]{:S(2)}, u32[]{:S(2)}) collective-permute-start(bf16[336,128]{1,0:T(8,128)(2,1)S(1)} %bitcast_select_fusion.1), channel_id=1, source_target_pairs={{0,16},{16,0},{1,17},{17,1},{2,18},{18,2},{3,19},{19,3},{4,20},{20... | collective-permute-start | bytes 258056 | tf_op jit(solution)/shard_map/ppermute | solution.py:14
  96.6 2.1 fusion.6
  98.8 2.6 %collective-permute-start.2 = (f32[2,512,128]{2,1,0:T(8,128)S(1)}, f32[2,512,128]{2,1,0:T(8,128)S(1)}, u32[]{:S(2)}, u32[]{:S(2)}) collective-permute-start(f32[2,512,128]{2,1,0:T(8,128)S(1)} %fusion.6), channel_id=1, source_target_pairs={{0,8},{8,0},{1,9},{9,1},{2,10},{10,2},{3,11},{11,3},{4,12},{12,4},... | collective-permute-start | bytes 1572872 | tf_op jit(solution)/shard_map/ppermute | solution.py:14
  101.4 6.7 %collective-permute-done.3 = bf16[336,128]{1,0:T(8,128)(2,1)S(1)} collective-permute-done((bf16[336,128]{1,0:T(8,128)(2,1)S(1)}, bf16[336,128]{1,0:T(8,128)(2,1)S(1)}, u32[]{:S(2)}, u32[]{:S(2)}) %collective-permute-start.3) | collective-permute-done | bytes 86048 | tf_op jit(solution)/shard_map/ppermute | solution.py:14
  108.1 1.3 select_select_fusion
  109.5 1.9 convolution_convert_fusion.3
  111.4 7.6 %all-to-all-start.3 = ((bf16[32,16,1792]{2,1,0:T(8,128)(2,1)}), bf16[32,16,1792]{2,1,0:T(8,128)(2,1)S(1)}, u32[]{:S(2)}, u32[]{:S(2)}) async-start(bf16[32,16,1792]{2,1,0:T(8,128)(2,1)} %bitcast.110), calls=%async_computation.3 | async-start | bytes 3670016 | tf_op jit(solution)/shard_map/all_to_all | solution.py:53
  119.1 2.1 fusion.9
  121.2 2.1 collective-permute-start.4
  123.4 1.7 collective-permute-done.4
  125.1 1.9 convolution_convert_fusion.2
  127.0 17.0 %all-to-all-done.3 = bf16[32,16,1792]{2,1,0:T(8,128)(2,1)S(1)} async-done(((bf16[32,16,1792]{2,1,0:T(8,128)(2,1)}), bf16[32,16,1792]{2,1,0:T(8,128)(2,1)S(1)}, u32[]{:S(2)}, u32[]{:S(2)}) %all-to-all-start.3) | async-done | bytes 1835040 | tf_op jit(solution)/shard_map/all_to_all | solution.py:53
  145.2 5.9 %all-to-all-start.4 = ((bf16[32,16,1792]{2,1,0:T(8,128)(2,1)}), bf16[32,16,1792]{2,1,0:T(8,128)(2,1)S(1)}, u32[]{:S(2)}, u32[]{:S(2)}) async-start(bf16[32,16,1792]{2,1,0:T(8,128)(2,1)} %bitcast.109), calls=%async_computation.4 | async-start | bytes 3670016 | tf_op jit(solution)/shard_map/all_to_all | solution.py:53
  151.2 2.4 %fusion.45 = f32[256,1792]{1,0:T(8,128)S(1)} fusion(bf16[512,1792]{1,0:T(8,128)(2,1)} %bitcast.107, f32[256]{0:T(256)S(1)} %bitcast.131, s32[256]{0:T(256)S(1)} %get-tuple-element.53, f32[256]{0:T(256)S(1)} %bitcast.129, s32[256]{0:T(256)S(1)} %get-tuple-element.52), kind=kOutput, calls=%fused_computation.63 | convolution fusion | flops 470548480 | bytes 3674112 | tf_op jit(solution)/shard_map/dot_general | solution.py:71
  153.6 1.7 fusion
  155.3 3.5 %reshape.275 = bf16[2,128,2,4,224]{4,3,2,1,0:T(4,128)(2,1)S(1)} reshape(bf16[256,1792]{1,0:T(8,128)(2,1)} %fusion) | data formatting | bytes 1835008 | tf_op jit(solution)/shard_map/reshape | solution.py:78
  158.8 2.3 copy.18
  161.1 1.3 copy.13
  163.2 1.9 collective-permute-start.5
  165.1 1.9 collective-permute-start.6
  167.0 5.4 %collective-permute-start.7 = (bf16[2,128,448]{1,2,0:T(8,128)(2,1)S(1)}, bf16[2,128,448]{1,2,0:T(8,128)(2,1)}, u32[]{:S(2)}, u32[]{:S(2)}) collective-permute-start(bf16[2,128,448]{1,2,0:T(8,128)(2,1)S(1)} %get-tuple-element.41), channel_id=1, source_target_pairs={{0,3},{1,2},{2,1},{3,0},{4,7},{5,6},{6,5},{7,4},{8,11},{9,10},{10,... | collective-permute-start | bytes 688136 | tf_op jit(solution)/shard_map/ppermute | solution.py:89
  172.5 3.6 %all-to-all-done.4 = bf16[32,16,1792]{2,1,0:T(8,128)(2,1)S(1)} async-done(((bf16[32,16,1792]{2,1,0:T(8,128)(2,1)}), bf16[32,16,1792]{2,1,0:T(8,128)(2,1)S(1)}, u32[]{:S(2)}, u32[]{:S(2)}) %all-to-all-start.4) | async-done | bytes 1835040 | tf_op jit(solution)/shard_map/all_to_all | solution.py:53
  177.6 1.5 reshape.276
  179.1 1.4 copy.19
  180.7 4.5 %all-to-all-start.5 = ((bf16[16,336,128]{2,1,0:T(8,128)(2,1)}), bf16[16,336,128]{2,1,0:T(8,128)(2,1)S(1)}, u32[]{:S(2)}, u32[]{:S(2)}) async-start(bf16[16,336,128]{2,1,0:T(8,128)(2,1)} %select_select_fusion), calls=%async_computation.5 | async-start | bytes 2752512 | tf_op jit(solution)/shard_map/all_to_all | solution.py:143
  185.2 1.9 collective-permute-start.10
  187.2 1.9 collective-permute-start.11
  189.1 4.5 %collective-permute-start.9 = (bf16[2,128,448]{1,2,0:T(8,128)(2,1)S(1)}, bf16[2,128,448]{1,2,0:T(8,128)(2,1)S(1)}, u32[]{:S(2)}, u32[]{:S(2)}) collective-permute-start(bf16[2,128,448]{1,2,0:T(8,128)(2,1)S(1)} %get-tuple-element.47), channel_id=1, source_target_pairs={{0,1},{1,0},{2,3},{3,2},{4,5},{5,4},{6,7},{7,6},{8,9},{9,8},{10,11... | collective-permute-start | bytes 688136 | tf_op jit(solution)/shard_map/ppermute | solution.py:89
  193.7 1.3 add_convert_fusion.1
  195.0 4.5 %collective-permute-start.8 = (bf16[128,448]{0,1:T(8,128)(2,1)S(1)}, bf16[128,448]{0,1:T(8,128)(2,1)S(1)}, u32[]{:S(2)}, u32[]{:S(2)}) collective-permute-start(bf16[128,448]{0,1:T(8,128)(2,1)S(1)} %dynamic-slice_bitcast_fusion.10), channel_id=1, source_target_pairs={{0,4},{4,0},{1,5},{5,1},{2,6},{6,2},{3,7},{7,3},{8,12},{12,8},{9,1... | collective-permute-start | bytes 344072 | tf_op jit(solution)/shard_map/ppermute | solution.py:14
  199.4 5.9 %collective-permute-done.10 = bf16[2,128,448]{1,2,0:T(8,128)(2,1)S(1)} collective-permute-done((bf16[2,128,448]{1,2,0:T(8,128)(2,1)S(1)}, bf16[2,128,448]{1,2,0:T(8,128)(2,1)S(1)}, u32[]{:S(2)}, u32[]{:S(2)}) %collective-permute-start.10) | collective-permute-done | bytes 229408 | tf_op jit(solution)/shard_map/ppermute | solution.py:89
  205.3 5.2 %collective-permute-done.9 = bf16[2,128,448]{1,2,0:T(8,128)(2,1)S(1)} collective-permute-done((bf16[2,128,448]{1,2,0:T(8,128)(2,1)S(1)}, bf16[2,128,448]{1,2,0:T(8,128)(2,1)S(1)}, u32[]{:S(2)}, u32[]{:S(2)}) %collective-permute-start.9) | collective-permute-done | bytes 229408 | tf_op jit(solution)/shard_map/ppermute | solution.py:89
  210.7 1.9 collective-permute-start.12
  212.6 9.7 %collective-permute-start.13 = (bf16[128,448]{0,1:T(8,128)(2,1)S(1)}, bf16[128,448]{0,1:T(8,128)(2,1)S(1)}, u32[]{:S(2)}, u32[]{:S(2)}) collective-permute-start(bf16[128,448]{0,1:T(8,128)(2,1)S(1)} %get-tuple-element.49), channel_id=1, source_target_pairs={{0,19},{1,18},{2,17},{3,16},{4,23},{5,22},{6,21},{7,20},{16,3},{17... | collective-permute-start | bytes 344072 | tf_op jit(solution)/shard_map/ppermute | solution.py:151
  222.4 10.0 %collective-permute-done.13 = bf16[128,448]{0,1:T(8,128)(2,1)S(1)} collective-permute-done((bf16[128,448]{0,1:T(8,128)(2,1)S(1)}, bf16[128,448]{0,1:T(8,128)(2,1)S(1)}, u32[]{:S(2)}, u32[]{:S(2)}) %collective-permute-start.13) | collective-permute-done | bytes 114720 | tf_op jit(solution)/shard_map/ppermute | solution.py:151
  (56 shorter events, 8.4 us)
Async XLA Ops:
  0.6 7.8 %copy-start.4 = (bf16[128,3584]{1,0:T(8,128)(2,1)S(1)}, bf16[128,3584]{1,0:T(8,128)(2,1)}, u32[]{:S(2)}) copy-start(bf16[128,3584]{1,0:T(8,128)(2,1)} %param.6) | copy-start | bytes 2752516
  0.6 42.3 %all-to-all-start = ((bf16[16,336,128]{2,1,0:T(8,128)(2,1)}), bf16[16,336,128]{2,1,0:T(8,128)(2,1)S(1)}, u32[]{:S(2)}, u32[]{:S(2)}) async-start(bf16[16,336,128]{2,1,0:T(8,128)(2,1)} %bitcast.112), calls=%async_computation | async-start | bytes 2752512 | tf_op jit(solution)/shard_map/all_to_all | solution.py:123
  9.0 13.4 %copy-start.6 = (s32[32]{0:T(128)S(1)}, s32[32]{0:T(128)}, u32[]{:S(2)}) copy-start(s32[32]{0:T(128)} %param.10) | copy-start | bytes 388
  9.0 13.4 %copy-start.7 = (s32[32]{0:T(128)S(1)}, s32[32]{0:T(128)}, u32[]{:S(2)}) copy-start(s32[32]{0:T(128)} %param.11) | copy-start | bytes 388
  9.0 14.1 %copy-start.8 = (s32[128,2]{0,1:T(2,128)S(1)}, s32[128,2]{0,1:T(2,128)}, u32[]{:S(2)}) copy-start(s32[128,2]{0,1:T(2,128)} %param.7) | copy-start | bytes 3076
  9.0 14.3 %copy-start.5 = (f32[128,2]{0,1:T(2,128)S(1)}, f32[128,2]{0,1:T(2,128)}, u32[]{:S(2)}) copy-start(f32[128,2]{0,1:T(2,128)} %param.8) | copy-start | bytes 3076
  11.3 31.6 %collective-permute-start = (bf16[64,1792]{1,0:T(8,128)(2,1)S(1)}, bf16[64,1792]{1,0:T(8,128)(2,1)S(1)}, u32[]{:S(2)}, u32[]{:S(2)}) collective-permute-start(bf16[64,1792]{1,0:T(8,128)(2,1)S(1)} %constant_dynamic-slice_fusion), channel_id=1, source_target_pairs={{0,23},{1,22},{2,21},{3,20},{4,19},{5,18},{6,17},{7,16},{16,7},{17... | collective-permute-start | bytes 688136 | tf_op jit(solution)/shard_map/ppermute | solution.py:18
  23.3 19.6 %collective-permute-start.1 = (f32[4,128]{1,0:T(4,128)S(1)}, f32[4,128]{1,0:T(4,128)S(1)}, u32[]{:S(2)}, u32[]{:S(2)}) collective-permute-start(f32[4,128]{1,0:T(4,128)S(1)} %pad_maximum_fusion), channel_id=1, source_target_pairs={{0,23},{1,22},{2,21},{3,20},{4,19},{5,18},{6,17},{7,16},{16,7},{17... | collective-permute-start | bytes 6152 | tf_op jit(solution)/shard_map/ppermute | solution.py:18
  43.0 32.8 %all-to-all-start.1 = ((bf16[32,16,1792]{2,1,0:T(8,128)(2,1)}), bf16[32,16,1792]{2,1,0:T(8,128)(2,1)S(1)}, u32[]{:S(2)}, u32[]{:S(2)}) async-start(bf16[32,16,1792]{2,1,0:T(8,128)(2,1)} %bitcast.16), calls=%async_computation.1 | async-start | bytes 3670016 | tf_op jit(solution)/shard_map/all_to_all | solution.py:53
  75.8 1.3 copy-start.3
  77.1 19.5 %copy-start.2 = (bf16[1,3,1792,128]{3,2,1,0:T(8,128)(2,1)S(1)}, bf16[1,3,1792,128]{3,2,1,0:T(8,128)(2,1)}, u32[]{:S(2)}) copy-start(bf16[1,3,1792,128]{3,2,1,0:T(8,128)(2,1)} %param.9) | copy-start | bytes 4128772
  77.1 34.4 %all-to-all-start.2 = ((bf16[32,16,1792]{2,1,0:T(8,128)(2,1)}), bf16[32,16,1792]{2,1,0:T(8,128)(2,1)}, u32[]{:S(2)}, u32[]{:S(2)}) async-start(bf16[32,16,1792]{2,1,0:T(8,128)(2,1)} %bitcast.23), calls=%async_computation.2 | async-start | bytes 3670016 | tf_op jit(solution)/shard_map/all_to_all | solution.py:53
  87.7 20.4 %collective-permute-start.3 = (bf16[336,128]{1,0:T(8,128)(2,1)S(1)}, bf16[336,128]{1,0:T(8,128)(2,1)S(1)}, u32[]{:S(2)}, u32[]{:S(2)}) collective-permute-start(bf16[336,128]{1,0:T(8,128)(2,1)S(1)} %bitcast_select_fusion.1), channel_id=1, source_target_pairs={{0,16},{16,0},{1,17},{17,1},{2,18},{18,2},{3,19},{19,3},{4,20},{20... | collective-permute-start | bytes 258056 | tf_op jit(solution)/shard_map/ppermute | solution.py:14
  98.8 10.7 %collective-permute-start.2 = (f32[2,512,128]{2,1,0:T(8,128)S(1)}, f32[2,512,128]{2,1,0:T(8,128)S(1)}, u32[]{:S(2)}, u32[]{:S(2)}) collective-permute-start(f32[2,512,128]{2,1,0:T(8,128)S(1)} %fusion.6), channel_id=1, source_target_pairs={{0,8},{8,0},{1,9},{9,1},{2,10},{10,2},{3,11},{11,3},{4,12},{12,4},... | collective-permute-start | bytes 1572872 | tf_op jit(solution)/shard_map/ppermute | solution.py:14
  111.4 32.5 %all-to-all-start.3 = ((bf16[32,16,1792]{2,1,0:T(8,128)(2,1)}), bf16[32,16,1792]{2,1,0:T(8,128)(2,1)S(1)}, u32[]{:S(2)}, u32[]{:S(2)}) async-start(bf16[32,16,1792]{2,1,0:T(8,128)(2,1)} %bitcast.110), calls=%async_computation.3 | async-start | bytes 3670016 | tf_op jit(solution)/shard_map/all_to_all | solution.py:53
  121.2 3.8 %collective-permute-start.4 = (f32[2,512,128]{2,1,0:T(8,128)S(1)}, f32[2,512,128]{2,1,0:T(8,128)S(1)}, u32[]{:S(2)}, u32[]{:S(2)}) collective-permute-start(f32[2,512,128]{2,1,0:T(8,128)S(1)} %fusion.9), channel_id=1, source_target_pairs={{0,8},{8,0},{1,9},{9,1},{2,10},{10,2},{3,11},{11,3},{4,12},{12,4},... | collective-permute-start | bytes 1572872 | tf_op jit(solution)/shard_map/ppermute | solution.py:14
  144.0 1.2 copy-start
  145.2 30.9 %all-to-all-start.4 = ((bf16[32,16,1792]{2,1,0:T(8,128)(2,1)}), bf16[32,16,1792]{2,1,0:T(8,128)(2,1)S(1)}, u32[]{:S(2)}, u32[]{:S(2)}) async-start(bf16[32,16,1792]{2,1,0:T(8,128)(2,1)} %bitcast.109), calls=%async_computation.4 | async-start | bytes 3670016 | tf_op jit(solution)/shard_map/all_to_all | solution.py:53
  151.2 2.4 %copy-start.1 = (bf16[32,16,1792]{2,1,0:T(8,128)(2,1)S(1)}, bf16[32,16,1792]{2,1,0:T(8,128)(2,1)}, u32[]{:S(2)}) copy-start(bf16[32,16,1792]{2,1,0:T(8,128)(2,1)} %copy-done) | copy-start | bytes 5505028
  163.2 25.9 %collective-permute-start.5 = (bf16[2,128,448]{1,2,0:T(8,128)(2,1)}, bf16[2,128,448]{1,2,0:T(8,128)(2,1)}, u32[]{:S(2)}, u32[]{:S(2)}) collective-permute-start(bf16[2,128,448]{1,2,0:T(8,128)(2,1)} %get-tuple-element.40), channel_id=1, source_target_pairs={{0,1},{1,0},{2,3},{3,2},{4,5},{5,4},{6,7},{7,6},{8,9},{9,8},{10,11... | collective-permute-start | bytes 688136 | tf_op jit(solution)/shard_map/ppermute | solution.py:89
  165.1 28.6 %collective-permute-start.6 = (bf16[2,128,448]{1,2,0:T(8,128)(2,1)S(1)}, bf16[2,128,448]{1,2,0:T(8,128)(2,1)}, u32[]{:S(2)}, u32[]{:S(2)}) collective-permute-start(bf16[2,128,448]{1,2,0:T(8,128)(2,1)S(1)} %get-tuple-element.42), channel_id=1, source_target_pairs={{0,2},{1,3},{2,0},{3,1},{4,6},{5,7},{6,4},{7,5},{8,10},{9,11},{10,... | collective-permute-start | bytes 688136 | tf_op jit(solution)/shard_map/ppermute | solution.py:89
  167.0 26.6 %collective-permute-start.7 = (bf16[2,128,448]{1,2,0:T(8,128)(2,1)S(1)}, bf16[2,128,448]{1,2,0:T(8,128)(2,1)}, u32[]{:S(2)}, u32[]{:S(2)}) collective-permute-start(bf16[2,128,448]{1,2,0:T(8,128)(2,1)S(1)} %get-tuple-element.41), channel_id=1, source_target_pairs={{0,3},{1,2},{2,1},{3,0},{4,7},{5,6},{6,5},{7,4},{8,11},{9,10},{10,... | collective-permute-start | bytes 688136 | tf_op jit(solution)/shard_map/ppermute | solution.py:89
  180.7 52.4 %all-to-all-start.5 = ((bf16[16,336,128]{2,1,0:T(8,128)(2,1)}), bf16[16,336,128]{2,1,0:T(8,128)(2,1)S(1)}, u32[]{:S(2)}, u32[]{:S(2)}) async-start(bf16[16,336,128]{2,1,0:T(8,128)(2,1)} %select_select_fusion), calls=%async_computation.5 | async-start | bytes 2752512 | tf_op jit(solution)/shard_map/all_to_all | solution.py:143
  185.2 20.1 %collective-permute-start.10 = (bf16[2,128,448]{1,2,0:T(8,128)(2,1)S(1)}, bf16[2,128,448]{1,2,0:T(8,128)(2,1)S(1)}, u32[]{:S(2)}, u32[]{:S(2)}) collective-permute-start(bf16[2,128,448]{1,2,0:T(8,128)(2,1)S(1)} %get-tuple-element.46), channel_id=1, source_target_pairs={{0,2},{1,3},{2,0},{3,1},{4,6},{5,7},{6,4},{7,5},{8,10},{9,11},{10,... | collective-permute-start | bytes 688136 | tf_op jit(solution)/shard_map/ppermute | solution.py:89
  187.2 18.2 %collective-permute-start.11 = (bf16[2,128,448]{1,2,0:T(8,128)(2,1)S(1)}, bf16[2,128,448]{1,2,0:T(8,128)(2,1)S(1)}, u32[]{:S(2)}, u32[]{:S(2)}) collective-permute-start(bf16[2,128,448]{1,2,0:T(8,128)(2,1)S(1)} %get-tuple-element.45), channel_id=1, source_target_pairs={{0,3},{1,2},{2,1},{3,0},{4,7},{5,6},{6,5},{7,4},{8,11},{9,10},{10,... | collective-permute-start | bytes 688136 | tf_op jit(solution)/shard_map/ppermute | solution.py:89
  189.1 21.4 %collective-permute-start.9 = (bf16[2,128,448]{1,2,0:T(8,128)(2,1)S(1)}, bf16[2,128,448]{1,2,0:T(8,128)(2,1)S(1)}, u32[]{:S(2)}, u32[]{:S(2)}) collective-permute-start(bf16[2,128,448]{1,2,0:T(8,128)(2,1)S(1)} %get-tuple-element.47), channel_id=1, source_target_pairs={{0,1},{1,0},{2,3},{3,2},{4,5},{5,4},{6,7},{7,6},{8,9},{9,8},{10,11... | collective-permute-start | bytes 688136 | tf_op jit(solution)/shard_map/ppermute | solution.py:89
  195.0 27.4 %collective-permute-start.8 = (bf16[128,448]{0,1:T(8,128)(2,1)S(1)}, bf16[128,448]{0,1:T(8,128)(2,1)S(1)}, u32[]{:S(2)}, u32[]{:S(2)}) collective-permute-start(bf16[128,448]{0,1:T(8,128)(2,1)S(1)} %dynamic-slice_bitcast_fusion.10), channel_id=1, source_target_pairs={{0,4},{4,0},{1,5},{5,1},{2,6},{6,2},{3,7},{7,3},{8,12},{12,8},{9,1... | collective-permute-start | bytes 344072 | tf_op jit(solution)/shard_map/ppermute | solution.py:14
  210.7 11.7 %collective-permute-start.12 = (bf16[128,448]{0,1:T(8,128)(2,1)S(1)}, bf16[128,448]{0,1:T(8,128)(2,1)S(1)}, u32[]{:S(2)}, u32[]{:S(2)}) collective-permute-start(bf16[128,448]{0,1:T(8,128)(2,1)S(1)} %get-tuple-element.48), channel_id=1, source_target_pairs={{0,23},{1,22},{2,21},{3,20},{4,19},{5,18},{6,17},{7,16},{16,7},{17... | collective-permute-start | bytes 344072 | tf_op jit(solution)/shard_map/ppermute | solution.py:18
  212.6 19.8 %collective-permute-start.13 = (bf16[128,448]{0,1:T(8,128)(2,1)S(1)}, bf16[128,448]{0,1:T(8,128)(2,1)S(1)}, u32[]{:S(2)}, u32[]{:S(2)}) collective-permute-start(bf16[128,448]{0,1:T(8,128)(2,1)S(1)} %get-tuple-element.49), channel_id=1, source_target_pairs={{0,19},{1,18},{2,17},{3,16},{4,23},{5,22},{6,21},{7,20},{16,3},{17... | collective-permute-start | bytes 344072 | tf_op jit(solution)/shard_map/ppermute | solution.py:151

commit v10 on v9

--- a/solution.py
+++ b/solution.py
@@ -132,14 +132,15 @@
     other_sent = exchange(payload)
     chosen = pick_pieces(spread, old_owner, new_owner, zh)
     payload, other_sent, chosen = tied((expert_part(sent, own), other_sent, chosen))
+    other_back = exchange(expert_part(other_sent, own))
+    payload, other_back = tied((payload, other_back))
     back = exchange(payload)
-    payload, back = tied((expert_part(other_sent, own), back))
-    other_back = exchange(payload)
 
+    other_parts = by_columns(weighted(other_back, other_codes, other_rows), near)
+    other_kept, back = near_sum(other_parts, place, near - 1, back)
     parts = by_columns(weighted(back, codes, rows), near)
-    kept, other_back = near_sum(parts, place, 0, other_back)
-    other_parts = by_columns(weighted(other_back, other_codes, other_rows), near)
-    other_kept, chosen = near_sum(other_parts, place, near - 1, chosen)
+    kept, chosen = near_sum(parts, place, 0, chosen)
+    other_kept, chosen = tied((other_kept, chosen))
     arrived = lax.all_to_all(chosen, ("y", "x"), split_axis=0, concat_axis=0, tiled=True)
 
     def of(value, index):

time: 238 us -> 246 us (1.034)
  the two profiles are of different devices: /device:TPU:1 before, /device:TPU:2 now
where the time goes in v10:
time: 246 us; the launch traced here: 245 us
  starting transfers between devices  93.7 us (38%)
  waiting for transfers between devices  57.7 us (23%)
  blocking collectives  51.6 us (21%)
  matrix products  16.4 us (7%)
  local copies, waits for them, and re-layouts  16.2 us (7%)
  other arithmetic  5.65 us (2%)
  between operations  3.78 us (2%)
    all_to_all x1, blocking collectives, exchange(): lax.all_to_all(blocks, axes, split_axis=0, concat_axis=0, tiled=True)  31.9 us
    ppermute x4, waiting for transfers between devices, swap(): return lax.ppermute(value, axis, [(0, 1), (1, 0)])  24.7 us
    all_gather x1, blocking collectives, shards(): other_table = lax.all_gather(quarter, NEAR, tiled=True)  19.6 us
    ppermute x6, starting transfers between devices, near_sum(): lax.ppermute(block, NEAR, [(i, i ^ step) for i in range(count)])  19.3 us
    all_to_all x3, starting transfers between devices, exchange(): lax.all_to_all(blocks, axes, split_axis=0, concat_axis=0, tiled=True)  19.2 us
    ppermute x3, starting transfers between devices, mirrored(): return lax.ppermute(value, RING, [(i, 15 - i) for i in range(16)])  16 us
    ppermute x3, waiting for transfers between devices, mirrored(): return lax.ppermute(value, RING, [(i, 15 - i) for i in range(16)])  15.2 us
    ppermute x4, starting transfers between devices, swap(): return lax.ppermute(value, axis, [(0, 1), (1, 0)])  15 us
  transfers between devices with their start and end apart: 19, of which 9 were waited for; matrix products, arithmetic and copies ran while one was open for 13% of the time, Pallas kernels for 0%

profile of v10, /device:TPU:2, one launch (start us, length us, event | category | flops | bytes accessed | tf_op | source)
XLA Modules:
  0.0 245.0 jit_solution(17241639474353615847)
XLA Ops:
  0.6 9.5 %all-to-all-start = ((bf16[16,336,128]{2,1,0:T(8,128)(2,1)}), bf16[16,336,128]{2,1,0:T(8,128)(2,1)S(1)}, u32[]{:S(2)}, u32[]{:S(2)}) async-start(bf16[16,336,128]{2,1,0:T(8,128)(2,1)} %bitcast.112), calls=%async_computation | async-start | bytes 2752512 | tf_op jit(solution)/shard_map/all_to_all | solution.py:123
  10.9 0.9 copy.16
  11.8 1.3 reshape.274
  13.1 9.5 %collective-permute-start = (bf16[64,1792]{1,0:T(8,128)(2,1)S(1)}, bf16[64,1792]{1,0:T(8,128)(2,1)S(1)}, u32[]{:S(2)}, u32[]{:S(2)}) collective-permute-start(bf16[64,1792]{1,0:T(8,128)(2,1)S(1)} %constant_dynamic-slice_fusion), channel_id=1, source_target_pairs={{0,23},{1,22},{2,21},{3,20},{4,19},{5,18},{6,17},{7,16},{16,7},{17... | collective-permute-start | bytes 688136 | tf_op jit(solution)/shard_map/ppermute | solution.py:18
  23.5 1.9 collective-permute-start.1
  25.5 1.9 convolution_convert_fusion.1
  27.4 15.2 %collective-permute-done.1 = f32[4,128]{1,0:T(4,128)S(1)} collective-permute-done((f32[4,128]{1,0:T(4,128)S(1)}, f32[4,128]{1,0:T(4,128)S(1)}, u32[]{:S(2)}, u32[]{:S(2)}) %collective-permute-start.1) | collective-permute-done | bytes 2080 | tf_op jit(solution)/shard_map/ppermute | solution.py:18
  42.6 7.4 %all-to-all-start.1 = ((bf16[32,16,1792]{2,1,0:T(8,128)(2,1)}), bf16[32,16,1792]{2,1,0:T(8,128)(2,1)S(1)}, u32[]{:S(2)}, u32[]{:S(2)}) async-start(bf16[32,16,1792]{2,1,0:T(8,128)(2,1)} %bitcast.18), calls=%async_computation.1 | async-start | bytes 3670016 | tf_op jit(solution)/shard_map/all_to_all | solution.py:53
  50.0 19.6 %all_gather.3 = bf16[256,1792]{1,0:T(8,128)(2,1)S(1)} all-gather(bf16[64,1792]{1,0:T(8,128)(2,1)S(1)} %collective-permute-done), channel_id=1, replica_groups=mesh['y'=4,'x'=4,'zh'=2,'c'=2,'ma'=2,'mb'=2,'mc'=2] {'mb','mc'}, dimensions={0}, use_global_device_ids=true | all-gather | bytes 1146880 | tf_op jit(solution)/shard_map/all_gather | solution.py:130
  69.6 1.9 convolution_convert_fusion
  71.5 3.4 %all-to-all-done.1 = bf16[32,16,1792]{2,1,0:T(8,128)(2,1)S(1)} async-done(((bf16[32,16,1792]{2,1,0:T(8,128)(2,1)}), bf16[32,16,1792]{2,1,0:T(8,128)(2,1)S(1)}, u32[]{:S(2)}, u32[]{:S(2)}) %all-to-all-start.1) | async-done | bytes 1835040 | tf_op jit(solution)/shard_map/all_to_all | solution.py:53
  74.8 1.3 copy-done.2
  76.1 6.7 %all-to-all-start.2 = ((bf16[32,16,1792]{2,1,0:T(8,128)(2,1)}), bf16[32,16,1792]{2,1,0:T(8,128)(2,1)}, u32[]{:S(2)}, u32[]{:S(2)}) async-start(bf16[32,16,1792]{2,1,0:T(8,128)(2,1)} %bitcast.25), calls=%async_computation.2 | async-start | bytes 3670016 | tf_op jit(solution)/shard_map/all_to_all | solution.py:53
  85.4 1.3 fusion.69
  86.7 9.2 %collective-permute-start.3 = (bf16[336,128]{1,0:T(8,128)(2,1)S(1)}, bf16[336,128]{1,0:T(8,128)(2,1)S(1)}, u32[]{:S(2)}, u32[]{:S(2)}) collective-permute-start(bf16[336,128]{1,0:T(8,128)(2,1)S(1)} %bitcast_select_fusion.1), channel_id=1, source_target_pairs={{0,16},{16,0},{1,17},{17,1},{2,18},{18,2},{3,19},{19,3},{4,20},{20... | collective-permute-start | bytes 258056 | tf_op jit(solution)/shard_map/ppermute | solution.py:14
  95.9 2.1 fusion.6
  98.1 1.9 collective-permute-start.2
  100.0 7.2 %collective-permute-done.3 = bf16[336,128]{1,0:T(8,128)(2,1)S(1)} collective-permute-done((bf16[336,128]{1,0:T(8,128)(2,1)S(1)}, bf16[336,128]{1,0:T(8,128)(2,1)S(1)}, u32[]{:S(2)}, u32[]{:S(2)}) %collective-permute-start.3) | collective-permute-done | bytes 86048 | tf_op jit(solution)/shard_map/ppermute | solution.py:14
  107.3 1.3 select_select_fusion
  108.7 1.9 convolution_convert_fusion.3
  110.6 2.1 fusion.9
  112.7 1.9 collective-permute-start.4
  114.7 1.8 collective-permute-done.4
  117.3 31.9 %all_to_all.30 = bf16[32,16,1792]{2,1,0:T(8,128)(2,1)} all-to-all(bf16[32,16,1792]{2,1,0:T(8,128)(2,1)S(1)} %bitcast.110), channel_id=1, replica_groups=mesh['y'=4,'x'=4,'zh'=2,'c'=2,'ma'=2,'mb'=2,'mc'=2] {'y','x','c'}, dimensions={0} | all-to-all | bytes 3670016 | tf_op jit(solution)/shard_map/all_to_all | solution.py:53
  149.2 5.2 %all-to-all-start.4 = ((bf16[32,16,1792]{2,1,0:T(8,128)(2,1)}), bf16[32,16,1792]{2,1,0:T(8,128)(2,1)S(1)}, u32[]{:S(2)}, u32[]{:S(2)}) async-start(bf16[32,16,1792]{2,1,0:T(8,128)(2,1)} %bitcast.109), calls=%async_computation.4 | async-start | bytes 3670016 | tf_op jit(solution)/shard_map/all_to_all | solution.py:53
  154.4 2.4 fusion.48
  156.8 1.7 fusion
  158.5 3.5 %reshape.275 = bf16[2,128,2,4,224]{4,3,2,1,0:T(4,128)(2,1)S(1)} reshape(bf16[256,1792]{1,0:T(8,128)(2,1)} %fusion) | data formatting | bytes 1835008 | tf_op jit(solution)/shard_map/reshape | solution.py:78
  162.1 2.3 copy.18
  164.4 1.3 copy.13
  166.4 1.9 collective-permute-start.10
  168.3 1.9 collective-permute-start.11
  170.3 5.4 %collective-permute-start.9 = (bf16[2,128,448]{1,2,0:T(8,128)(2,1)S(1)}, bf16[2,128,448]{1,2,0:T(8,128)(2,1)}, u32[]{:S(2)}, u32[]{:S(2)}) collective-permute-start(bf16[2,128,448]{1,2,0:T(8,128)(2,1)S(1)} %get-tuple-element.51), channel_id=1, source_target_pairs={{0,1},{1,0},{2,3},{3,2},{4,5},{5,4},{6,7},{7,6},{8,9},{9,8},{10,11... | collective-permute-start | bytes 688136 | tf_op jit(solution)/shard_map/ppermute | solution.py:89
  175.7 3.7 %all-to-all-done.4 = bf16[32,16,1792]{2,1,0:T(8,128)(2,1)S(1)} async-done(((bf16[32,16,1792]{2,1,0:T(8,128)(2,1)}), bf16[32,16,1792]{2,1,0:T(8,128)(2,1)S(1)}, u32[]{:S(2)}, u32[]{:S(2)}) %all-to-all-start.4) | async-done | bytes 1835040 | tf_op jit(solution)/shard_map/all_to_all | solution.py:53
  180.9 1.5 reshape.276
  182.4 1.4 copy.19
  184.0 3.0 %collective-permute-done.9 = bf16[2,128,448]{1,2,0:T(8,128)(2,1)} collective-permute-done((bf16[2,128,448]{1,2,0:T(8,128)(2,1)S(1)}, bf16[2,128,448]{1,2,0:T(8,128)(2,1)}, u32[]{:S(2)}, u32[]{:S(2)}) %collective-permute-start.9) | collective-permute-done | bytes 229408 | tf_op jit(solution)/shard_map/ppermute | solution.py:89
  187.0 1.3 add_convert_fusion
  188.3 7.4 %all-to-all-start.5 = ((bf16[16,336,128]{2,1,0:T(8,128)(2,1)}), bf16[16,336,128]{2,1,0:T(8,128)(2,1)S(1)}, u32[]{:S(2)}, u32[]{:S(2)}) async-start(bf16[16,336,128]{2,1,0:T(8,128)(2,1)} %select_select_fusion), calls=%async_computation.5 | async-start | bytes 2752512 | tf_op jit(solution)/shard_map/all_to_all | solution.py:144
  195.6 2.5 %collective-permute-start.5 = (bf16[2,128,448]{1,2,0:T(8,128)(2,1)S(1)}, bf16[2,128,448]{1,2,0:T(8,128)(2,1)S(1)}, u32[]{:S(2)}, u32[]{:S(2)}) collective-permute-start(bf16[2,128,448]{1,2,0:T(8,128)(2,1)S(1)} %get-tuple-element.44), channel_id=1, source_target_pairs={{0,1},{1,0},{2,3},{3,2},{4,5},{5,4},{6,7},{7,6},{8,9},{9,8},{10,11... | collective-permute-start | bytes 688136 | tf_op jit(solution)/shard_map/ppermute | solution.py:89
  198.2 3.0 %collective-permute-start.6 = (bf16[2,128,448]{1,2,0:T(8,128)(2,1)S(1)}, bf16[2,128,448]{1,2,0:T(8,128)(2,1)S(1)}, u32[]{:S(2)}, u32[]{:S(2)}) collective-permute-start(bf16[2,128,448]{1,2,0:T(8,128)(2,1)S(1)} %get-tuple-element.46), channel_id=1, source_target_pairs={{0,2},{1,3},{2,0},{3,1},{4,6},{5,7},{6,4},{7,5},{8,10},{9,11},{10,... | collective-permute-start | bytes 688136 | tf_op jit(solution)/shard_map/ppermute | solution.py:89
  201.1 4.6 %collective-permute-start.7 = (bf16[2,128,448]{1,2,0:T(8,128)(2,1)S(1)}, bf16[2,128,448]{1,2,0:T(8,128)(2,1)S(1)}, u32[]{:S(2)}, u32[]{:S(2)}) collective-permute-start(bf16[2,128,448]{1,2,0:T(8,128)(2,1)S(1)} %get-tuple-element.45), channel_id=1, source_target_pairs={{0,3},{1,2},{2,1},{3,0},{4,7},{5,6},{6,5},{7,4},{8,11},{9,10},{10,... | collective-permute-start | bytes 688136 | tf_op jit(solution)/shard_map/ppermute | solution.py:89
  205.8 4.6 %collective-permute-start.12 = (bf16[128,448]{0,1:T(8,128)(2,1)S(1)}, bf16[128,448]{0,1:T(8,128)(2,1)S(1)}, u32[]{:S(2)}, u32[]{:S(2)}) collective-permute-start(bf16[128,448]{0,1:T(8,128)(2,1)S(1)} %get-tuple-element.52), channel_id=1, source_target_pairs={{0,23},{1,22},{2,21},{3,20},{4,19},{5,18},{6,17},{7,16},{16,7},{17... | collective-permute-start | bytes 344072 | tf_op jit(solution)/shard_map/ppermute | solution.py:18
  210.5 7.3 %collective-permute-start.13 = (bf16[128,448]{0,1:T(8,128)(2,1)S(1)}, bf16[128,448]{0,1:T(8,128)(2,1)S(1)}, u32[]{:S(2)}, u32[]{:S(2)}) collective-permute-start(bf16[128,448]{0,1:T(8,128)(2,1)S(1)} %get-tuple-element.53), channel_id=1, source_target_pairs={{0,19},{1,18},{2,17},{3,16},{4,23},{5,22},{6,21},{7,20},{16,3},{17... | collective-permute-start | bytes 344072 | tf_op jit(solution)/shard_map/ppermute | solution.py:152
  217.8 7.5 %collective-permute-done.6 = bf16[2,128,448]{1,2,0:T(8,128)(2,1)S(1)} collective-permute-done((bf16[2,128,448]{1,2,0:T(8,128)(2,1)S(1)}, bf16[2,128,448]{1,2,0:T(8,128)(2,1)S(1)}, u32[]{:S(2)}, u32[]{:S(2)}) %collective-permute-start.6) | collective-permute-done | bytes 229408 | tf_op jit(solution)/shard_map/ppermute | solution.py:89
  225.4 1.9 collective-permute-start.8
  227.6 15.6 %collective-permute-done.8 = bf16[128,448]{0,1:T(8,128)(2,1)S(1)} collective-permute-done((bf16[128,448]{0,1:T(8,128)(2,1)S(1)}, bf16[128,448]{0,1:T(8,128)(2,1)S(1)}, u32[]{:S(2)}, u32[]{:S(2)}) %collective-permute-start.8) | collective-permute-done | bytes 114720 | tf_op jit(solution)/shard_map/ppermute | solution.py:14
  244.0 1.1 copy.21
  (53 shorter events, 6.2 us)
Async XLA Ops:
  0.6 9.6 %copy-start.3 = (bf16[128,3584]{1,0:T(8,128)(2,1)S(1)}, bf16[128,3584]{1,0:T(8,128)(2,1)}, u32[]{:S(2)}) copy-start(bf16[128,3584]{1,0:T(8,128)(2,1)} %param.6) | copy-start | bytes 2752516
  0.6 41.9 %all-to-all-start = ((bf16[16,336,128]{2,1,0:T(8,128)(2,1)}), bf16[16,336,128]{2,1,0:T(8,128)(2,1)S(1)}, u32[]{:S(2)}, u32[]{:S(2)}) async-start(bf16[16,336,128]{2,1,0:T(8,128)(2,1)} %bitcast.112), calls=%async_computation | async-start | bytes 2752512 | tf_op jit(solution)/shard_map/all_to_all | solution.py:123
  10.8 11.8 %copy-start.5 = (s32[32]{0:T(128)S(1)}, s32[32]{0:T(128)}, u32[]{:S(2)}) copy-start(s32[32]{0:T(128)} %param.10) | copy-start | bytes 388
  10.8 11.8 %copy-start.6 = (s32[32]{0:T(128)S(1)}, s32[32]{0:T(128)}, u32[]{:S(2)}) copy-start(s32[32]{0:T(128)} %param.11) | copy-start | bytes 388
  10.8 12.4 %copy-start.7 = (s32[128,2]{0,1:T(2,128)S(1)}, s32[128,2]{0,1:T(2,128)}, u32[]{:S(2)}) copy-start(s32[128,2]{0,1:T(2,128)} %param.7) | copy-start | bytes 3076
  10.8 12.6 %copy-start.4 = (f32[128,2]{0,1:T(2,128)S(1)}, f32[128,2]{0,1:T(2,128)}, u32[]{:S(2)}) copy-start(f32[128,2]{0,1:T(2,128)} %param.8) | copy-start | bytes 3076
  13.1 29.4 %collective-permute-start = (bf16[64,1792]{1,0:T(8,128)(2,1)S(1)}, bf16[64,1792]{1,0:T(8,128)(2,1)S(1)}, u32[]{:S(2)}, u32[]{:S(2)}) collective-permute-start(bf16[64,1792]{1,0:T(8,128)(2,1)S(1)} %constant_dynamic-slice_fusion), channel_id=1, source_target_pairs={{0,23},{1,22},{2,21},{3,20},{4,19},{5,18},{6,17},{7,16},{16,7},{17... | collective-permute-start | bytes 688136 | tf_op jit(solution)/shard_map/ppermute | solution.py:18
  23.5 19.1 %collective-permute-start.1 = (f32[4,128]{1,0:T(4,128)S(1)}, f32[4,128]{1,0:T(4,128)S(1)}, u32[]{:S(2)}, u32[]{:S(2)}) collective-permute-start(f32[4,128]{1,0:T(4,128)S(1)} %pad_maximum_fusion), channel_id=1, source_target_pairs={{0,23},{1,22},{2,21},{3,20},{4,19},{5,18},{6,17},{7,16},{16,7},{17... | collective-permute-start | bytes 6152 | tf_op jit(solution)/shard_map/ppermute | solution.py:18
  42.6 32.3 %all-to-all-start.1 = ((bf16[32,16,1792]{2,1,0:T(8,128)(2,1)}), bf16[32,16,1792]{2,1,0:T(8,128)(2,1)S(1)}, u32[]{:S(2)}, u32[]{:S(2)}) async-start(bf16[32,16,1792]{2,1,0:T(8,128)(2,1)} %bitcast.18), calls=%async_computation.1 | async-start | bytes 3670016 | tf_op jit(solution)/shard_map/all_to_all | solution.py:53
  74.8 1.3 copy-start.2
  76.1 19.8 %copy-start.1 = (bf16[1,3,1792,128]{3,2,1,0:T(8,128)(2,1)S(1)}, bf16[1,3,1792,128]{3,2,1,0:T(8,128)(2,1)}, u32[]{:S(2)}) copy-start(bf16[1,3,1792,128]{3,2,1,0:T(8,128)(2,1)} %param.9) | copy-start | bytes 4128772
  76.1 34.5 %all-to-all-start.2 = ((bf16[32,16,1792]{2,1,0:T(8,128)(2,1)}), bf16[32,16,1792]{2,1,0:T(8,128)(2,1)}, u32[]{:S(2)}, u32[]{:S(2)}) async-start(bf16[32,16,1792]{2,1,0:T(8,128)(2,1)} %bitcast.25), calls=%async_computation.2 | async-start | bytes 3670016 | tf_op jit(solution)/shard_map/all_to_all | solution.py:53
  86.7 20.5 %collective-permute-start.3 = (bf16[336,128]{1,0:T(8,128)(2,1)S(1)}, bf16[336,128]{1,0:T(8,128)(2,1)S(1)}, u32[]{:S(2)}, u32[]{:S(2)}) collective-permute-start(bf16[336,128]{1,0:T(8,128)(2,1)S(1)} %bitcast_select_fusion.1), channel_id=1, source_target_pairs={{0,16},{16,0},{1,17},{17,1},{2,18},{18,2},{3,19},{19,3},{4,20},{20... | collective-permute-start | bytes 258056 | tf_op jit(solution)/shard_map/ppermute | solution.py:14
  98.1 10.5 %collective-permute-start.2 = (f32[2,512,128]{2,1,0:T(8,128)S(1)}, f32[2,512,128]{2,1,0:T(8,128)S(1)}, u32[]{:S(2)}, u32[]{:S(2)}) collective-permute-start(f32[2,512,128]{2,1,0:T(8,128)S(1)} %fusion.6), channel_id=1, source_target_pairs={{0,8},{8,0},{1,9},{9,1},{2,10},{10,2},{3,11},{11,3},{4,12},{12,4},... | collective-permute-start | bytes 1572872 | tf_op jit(solution)/shard_map/ppermute | solution.py:14
  112.7 3.8 %collective-permute-start.4 = (f32[2,512,128]{2,1,0:T(8,128)S(1)}, f32[2,512,128]{2,1,0:T(8,128)S(1)}, u32[]{:S(2)}, u32[]{:S(2)}) collective-permute-start(f32[2,512,128]{2,1,0:T(8,128)S(1)} %fusion.9), channel_id=1, source_target_pairs={{0,8},{8,0},{1,9},{9,1},{2,10},{10,2},{3,11},{11,3},{4,12},{12,4},... | collective-permute-start | bytes 1572872 | tf_op jit(solution)/shard_map/ppermute | solution.py:14
  149.2 30.2 %all-to-all-start.4 = ((bf16[32,16,1792]{2,1,0:T(8,128)(2,1)}), bf16[32,16,1792]{2,1,0:T(8,128)(2,1)S(1)}, u32[]{:S(2)}, u32[]{:S(2)}) async-start(bf16[32,16,1792]{2,1,0:T(8,128)(2,1)} %bitcast.109), calls=%async_computation.4 | async-start | bytes 3670016 | tf_op jit(solution)/shard_map/all_to_all | solution.py:53
  154.4 2.4 copy-start
  166.4 17.6 %collective-permute-start.10 = (bf16[2,128,448]{1,2,0:T(8,128)(2,1)}, bf16[2,128,448]{1,2,0:T(8,128)(2,1)}, u32[]{:S(2)}, u32[]{:S(2)}) collective-permute-start(bf16[2,128,448]{1,2,0:T(8,128)(2,1)} %get-tuple-element.50), channel_id=1, source_target_pairs={{0,2},{1,3},{2,0},{3,1},{4,6},{5,7},{6,4},{7,5},{8,10},{9,11},{10,... | collective-permute-start | bytes 688136 | tf_op jit(solution)/shard_map/ppermute | solution.py:89
  168.3 15.7 %collective-permute-start.11 = (bf16[2,128,448]{1,2,0:T(8,128)(2,1)S(1)}, bf16[2,128,448]{1,2,0:T(8,128)(2,1)}, u32[]{:S(2)}, u32[]{:S(2)}) collective-permute-start(bf16[2,128,448]{1,2,0:T(8,128)(2,1)S(1)} %get-tuple-element.49), channel_id=1, source_target_pairs={{0,3},{1,2},{2,1},{3,0},{4,7},{5,6},{6,5},{7,4},{8,11},{9,10},{10,... | collective-permute-start | bytes 688136 | tf_op jit(solution)/shard_map/ppermute | solution.py:89
  170.3 16.7 %collective-permute-start.9 = (bf16[2,128,448]{1,2,0:T(8,128)(2,1)S(1)}, bf16[2,128,448]{1,2,0:T(8,128)(2,1)}, u32[]{:S(2)}, u32[]{:S(2)}) collective-permute-start(bf16[2,128,448]{1,2,0:T(8,128)(2,1)S(1)} %get-tuple-element.51), channel_id=1, source_target_pairs={{0,1},{1,0},{2,3},{3,2},{4,5},{5,4},{6,7},{7,6},{8,9},{9,8},{10,11... | collective-permute-start | bytes 688136 | tf_op jit(solution)/shard_map/ppermute | solution.py:89
  188.3 55.7 %all-to-all-start.5 = ((bf16[16,336,128]{2,1,0:T(8,128)(2,1)}), bf16[16,336,128]{2,1,0:T(8,128)(2,1)S(1)}, u32[]{:S(2)}, u32[]{:S(2)}) async-start(bf16[16,336,128]{2,1,0:T(8,128)(2,1)} %select_select_fusion), calls=%async_computation.5 | async-start | bytes 2752512 | tf_op jit(solution)/shard_map/all_to_all | solution.py:144
  195.6 22.1 %collective-permute-start.5 = (bf16[2,128,448]{1,2,0:T(8,128)(2,1)S(1)}, bf16[2,128,448]{1,2,0:T(8,128)(2,1)S(1)}, u32[]{:S(2)}, u32[]{:S(2)}) collective-permute-start(bf16[2,128,448]{1,2,0:T(8,128)(2,1)S(1)} %get-tuple-element.44), channel_id=1, source_target_pairs={{0,1},{1,0},{2,3},{3,2},{4,5},{5,4},{6,7},{7,6},{8,9},{9,8},{10,11... | collective-permute-start | bytes 688136 | tf_op jit(solution)/shard_map/ppermute | solution.py:89
  198.2 27.0 %collective-permute-start.6 = (bf16[2,128,448]{1,2,0:T(8,128)(2,1)S(1)}, bf16[2,128,448]{1,2,0:T(8,128)(2,1)S(1)}, u32[]{:S(2)}, u32[]{:S(2)}) collective-permute-start(bf16[2,128,448]{1,2,0:T(8,128)(2,1)S(1)} %get-tuple-element.46), channel_id=1, source_target_pairs={{0,2},{1,3},{2,0},{3,1},{4,6},{5,7},{6,4},{7,5},{8,10},{9,11},{10,... | collective-permute-start | bytes 688136 | tf_op jit(solution)/shard_map/ppermute | solution.py:89
  201.1 24.1 %collective-permute-start.7 = (bf16[2,128,448]{1,2,0:T(8,128)(2,1)S(1)}, bf16[2,128,448]{1,2,0:T(8,128)(2,1)S(1)}, u32[]{:S(2)}, u32[]{:S(2)}) collective-permute-start(bf16[2,128,448]{1,2,0:T(8,128)(2,1)S(1)} %get-tuple-element.45), channel_id=1, source_target_pairs={{0,3},{1,2},{2,1},{3,0},{4,7},{5,6},{6,5},{7,4},{8,11},{9,10},{10,... | collective-permute-start | bytes 688136 | tf_op jit(solution)/shard_map/ppermute | solution.py:89
  205.8 21.5 %collective-permute-start.12 = (bf16[128,448]{0,1:T(8,128)(2,1)S(1)}, bf16[128,448]{0,1:T(8,128)(2,1)S(1)}, u32[]{:S(2)}, u32[]{:S(2)}) collective-permute-start(bf16[128,448]{0,1:T(8,128)(2,1)S(1)} %get-tuple-element.52), channel_id=1, source_target_pairs={{0,23},{1,22},{2,21},{3,20},{4,19},{5,18},{6,17},{7,16},{16,7},{17... | collective-permute-start | bytes 344072 | tf_op jit(solution)/shard_map/ppermute | solution.py:18
  210.5 17.2 %collective-permute-start.13 = (bf16[128,448]{0,1:T(8,128)(2,1)S(1)}, bf16[128,448]{0,1:T(8,128)(2,1)S(1)}, u32[]{:S(2)}, u32[]{:S(2)}) collective-permute-start(bf16[128,448]{0,1:T(8,128)(2,1)S(1)} %get-tuple-element.53), channel_id=1, source_target_pairs={{0,19},{1,18},{2,17},{3,16},{4,23},{5,22},{6,21},{7,20},{16,3},{17... | collective-permute-start | bytes 344072 | tf_op jit(solution)/shard_map/ppermute | solution.py:152
  225.4 17.9 %collective-permute-start.8 = (bf16[128,448]{0,1:T(8,128)(2,1)S(1)}, bf16[128,448]{0,1:T(8,128)(2,1)S(1)}, u32[]{:S(2)}, u32[]{:S(2)}) collective-permute-start(bf16[128,448]{0,1:T(8,128)(2,1)S(1)} %dynamic-slice_bitcast_fusion.10), channel_id=1, source_target_pairs={{0,4},{4,0},{1,5},{5,1},{2,6},{6,2},{3,7},{7,3},{8,12},{12,8},{9,1... | collective-permute-start | bytes 344072 | tf_op jit(solution)/shard_map/ppermute | solution.py:14

commit v11 on v9

--- a/solution.py
+++ b/solution.py
@@ -120,15 +120,13 @@
     rows = placed_rows(codes, zh)
     quarter = mirrored(part)
     chips = lax.axis_size("y") * lax.axis_size("x")
-    spread = lax.all_to_all(
-        own.reshape(chips, -1, own.shape[-1]), ("y", "x"), split_axis=0, concat_axis=0, tiled=True
-    )
     other_codes = mirrored(codes)
-    payload, spread, quarter, other_codes = tied((gather_rows(rows, table), spread, quarter, other_codes))
-    sent = exchange(payload)
+    sent = exchange(gather_rows(rows, table))
+    pieces, sent, quarter, other_codes = tied((own.reshape(chips, -1, own.shape[-1]), sent, quarter, other_codes))
+    spread = lax.all_to_all(pieces, ("y", "x"), split_axis=0, concat_axis=0, tiled=True)
     other_rows = placed_rows(other_codes, zh)
     other_table = lax.all_gather(quarter, NEAR, tiled=True)
-    payload, sent = tied((gather_rows(other_rows, other_table), sent))
+    payload, spread = tied((gather_rows(other_rows, other_table), spread))
     other_sent = exchange(payload)
     chosen = pick_pieces(spread, old_owner, new_owner, zh)
     payload, other_sent, chosen = tied((expert_part(sent, own), other_sent, chosen))

time: 238 us -> 245 us (1.029)
  starting transfers between devices: 101 us -> 115 us
  waiting for transfers between devices: 70.2 us -> 59.8 us
  matrix products: 17.7 us -> 21.2 us
    all_to_all x4, waiting for transfers between devices: 24.9 us -> 15.7 us  [exchange(): lax.all_to_all(blocks, axes, split_axis=0, concat_axis=0, tiled=True)]
    all_to_all x4, starting transfers between devices: 28.2 us -> 34.6 us  [exchange(): lax.all_to_all(blocks, axes, split_axis=0, concat_axis=0, tiled=True)]
    ppermute x6, starting transfers between devices: 17.6 us -> 24 us  [near_sum(): lax.ppermute(block, NEAR, [(i, i ^ step) for i in range(count)])]
    ppermute x4, waiting for transfers between devices: 8.37 us -> 4.37 us  [swap(): return lax.ppermute(value, axis, [(0, 1), (1, 0)])]
    ppermute x3, waiting for transfers between devices: 15.8 us -> 18.8 us  [mirrored(): return lax.ppermute(value, RING, [(i, 15 - i) for i in range(16)])]
  transfers between devices with their start and end apart: 20 -> 20, of which waited for: 9 -> 8; matrix products, arithmetic and copies ran while one was open for 16% -> 15% of each run, Pallas kernels for 0% -> 0%
where the time goes in v11:
time: 245 us; the launch traced here: 241 us
  starting transfers between devices  115 us (47%)
  waiting for transfers between devices  59.8 us (24%)
  matrix products  21.2 us (9%)
  blocking collectives  17.3 us (7%)
  local copies, waits for them, and re-layouts  17.1 us (7%)
  other arithmetic  7.37 us (3%)
  between operations  3.66 us (1%)
    all_to_all x4, starting transfers between devices, exchange(): lax.all_to_all(blocks, axes, split_axis=0, concat_axis=0, tiled=True)  34.6 us
    ppermute x6, starting transfers between devices, near_sum(): lax.ppermute(block, NEAR, [(i, i ^ step) for i in range(count)])  24 us
    ppermute x3, waiting for transfers between devices, mirrored(): return lax.ppermute(value, RING, [(i, 15 - i) for i in range(16)])  18.8 us
    ppermute x4, starting transfers between devices, swap(): return lax.ppermute(value, axis, [(0, 1), (1, 0)])  18.6 us
    all_gather x1, blocking collectives, shards(): other_table = lax.all_gather(quarter, NEAR, tiled=True)  17.3 us
    all_to_all x4, waiting for transfers between devices, exchange(): lax.all_to_all(blocks, axes, split_axis=0, concat_axis=0, tiled=True)  15.7 us
    ppermute x3, starting transfers between devices, mirrored(): return lax.ppermute(value, RING, [(i, 15 - i) for i in range(16)])  14.5 us
    ppermute x1, waiting for transfers between devices, shards(): lax.ppermute(of(other_kept, far), RING, [(i, i ^ 11) for i in range(16)])  10.5 us
  transfers between devices with their start and end apart: 20, of which 8 were waited for; matrix products, arithmetic and copies ran while one was open for 15% of the time, Pallas kernels for 0%

profile of v11, /device:TPU:1, one launch (start us, length us, event | category | flops | bytes accessed | tf_op | source)
XLA Modules:
  0.0 241.4 jit_solution(5553219532738795213)
XLA Ops:
  0.6 1.3 fusion.67
  3.0 1.6 copy.9
  5.4 1.3 reshape.274
  6.8 1.9 convolution_convert_fusion.1
  8.7 10.7 %all-to-all-start = ((bf16[32,16,1792]{2,1,0:T(8,128)(2,1)}), bf16[32,16,1792]{2,1,0:T(8,128)(2,1)S(1)}, u32[]{:S(2)}, u32[]{:S(2)}) async-start(bf16[32,16,1792]{2,1,0:T(8,128)(2,1)} %bitcast.11), calls=%async_computation | async-start | bytes 3670016 | tf_op jit(solution)/shard_map/all_to_all | solution.py:53
  19.4 9.2 %collective-permute-start = (bf16[64,1792]{1,0:T(8,128)(2,1)S(1)}, bf16[64,1792]{1,0:T(8,128)(2,1)S(1)}, u32[]{:S(2)}, u32[]{:S(2)}) collective-permute-start(bf16[64,1792]{1,0:T(8,128)(2,1)S(1)} %constant_dynamic-slice_fusion), channel_id=1, source_target_pairs={{0,23},{1,22},{2,21},{3,20},{4,19},{5,18},{6,17},{7,16},{16,7},{17... | collective-permute-start | bytes 688136 | tf_op jit(solution)/shard_map/ppermute | solution.py:18
  28.6 1.9 collective-permute-start.1
  30.5 18.8 %collective-permute-done.1 = f32[4,128]{1,0:T(4,128)S(1)} collective-permute-done((f32[4,128]{1,0:T(4,128)S(1)}, f32[4,128]{1,0:T(4,128)S(1)}, u32[]{:S(2)}, u32[]{:S(2)}) %collective-permute-start.1) | collective-permute-done | bytes 2080 | tf_op jit(solution)/shard_map/ppermute | solution.py:18
  49.3 6.6 %all-to-all-start.1 = ((bf16[16,336,128]{2,1,0:T(8,128)(2,1)}), bf16[16,336,128]{2,1,0:T(8,128)(2,1)S(1)}, u32[]{:S(2)}, u32[]{:S(2)}) async-start(bf16[16,336,128]{2,1,0:T(8,128)(2,1)} %bitcast.8), calls=%async_computation.1 | async-start | bytes 2752512 | tf_op jit(solution)/shard_map/all_to_all | solution.py:126
  55.9 17.3 %all_gather.3 = bf16[256,1792]{1,0:T(8,128)(2,1)S(1)} all-gather(bf16[64,1792]{1,0:T(8,128)(2,1)S(1)} %collective-permute-done), channel_id=1, replica_groups=mesh['y'=4,'x'=4,'zh'=2,'c'=2,'ma'=2,'mb'=2,'mc'=2] {'mb','mc'}, dimensions={0}, use_global_device_ids=true | all-gather | bytes 1146880 | tf_op jit(solution)/shard_map/all_gather | solution.py:128
  73.3 1.9 convolution_convert_fusion
  75.2 9.7 %all-to-all-start.2 = ((bf16[32,16,1792]{2,1,0:T(8,128)(2,1)}), bf16[32,16,1792]{2,1,0:T(8,128)(2,1)}, u32[]{:S(2)}, u32[]{:S(2)}) async-start(bf16[32,16,1792]{2,1,0:T(8,128)(2,1)} %bitcast.23), calls=%async_computation.2 | async-start | bytes 3670016 | tf_op jit(solution)/shard_map/all_to_all | solution.py:53
  84.9 2.6 %fusion.6 = f32[2,512,128]{2,1,0:T(8,128)} fusion(bf16[512,1792]{1,0:T(8,128)(2,1)S(1)} %bitcast.117, bf16[1,3,1792,128]{3,2,1,0:T(8,128)(2,1)} %param.9), kind=kOutput, calls=%fused_computation.13 | convolution fusion | flops 469762048 | bytes 3276800 | tf_op jit(solution)/shard_map/rd,gdf->grf/dot_general | solution.py:57
  87.5 2.2 collective-permute-start.2
  92.2 1.3 fusion.69
  94.6 8.9 %collective-permute-start.3 = (bf16[336,128]{1,0:T(8,128)(2,1)S(1)}, bf16[336,128]{1,0:T(8,128)(2,1)S(1)}, u32[]{:S(2)}, u32[]{:S(2)}) collective-permute-start(bf16[336,128]{1,0:T(8,128)(2,1)S(1)} %bitcast_select_fusion.1), channel_id=1, source_target_pairs={{0,16},{16,0},{1,17},{17,1},{2,18},{18,2},{3,19},{19,3},{4,20},{20... | collective-permute-start | bytes 258056 | tf_op jit(solution)/shard_map/ppermute | solution.py:14
  103.6 2.9 %convolution_convert_fusion.3 = bf16[512,1792]{1,0:T(8,128)(2,1)} fusion(bf16[1,3,1792,128]{3,2,1,0:T(8,128)(2,1)} %param.9, f32[2,512,128]{2,1,0:T(8,128)S(1)} %add.227), kind=kOutput, calls=%fused_computation.3 | convolution fusion | flops 236191744 | bytes 2818048 | tf_op jit(solution)/shard_map/dot_general | solution.py:60
  106.5 2.7 %collective-permute-done.3 = bf16[336,128]{1,0:T(8,128)(2,1)S(1)} collective-permute-done((bf16[336,128]{1,0:T(8,128)(2,1)S(1)}, bf16[336,128]{1,0:T(8,128)(2,1)S(1)}, u32[]{:S(2)}, u32[]{:S(2)}) %collective-permute-start.3) | collective-permute-done | bytes 86048 | tf_op jit(solution)/shard_map/ppermute | solution.py:14
  109.2 1.3 select_select_fusion
  110.6 8.4 %all-to-all-start.3 = ((bf16[32,16,1792]{2,1,0:T(8,128)(2,1)}), bf16[32,16,1792]{2,1,0:T(8,128)(2,1)S(1)}, u32[]{:S(2)}, u32[]{:S(2)}) async-start(bf16[32,16,1792]{2,1,0:T(8,128)(2,1)} %bitcast.110), calls=%async_computation.3 | async-start | bytes 3670016 | tf_op jit(solution)/shard_map/all_to_all | solution.py:53
  119.0 2.4 fusion.9
  121.4 2.1 collective-permute-start.4
  123.5 1.7 collective-permute-done.4
  125.2 2.9 %convolution_convert_fusion.2 = bf16[512,1792]{1,0:T(8,128)(2,1)} fusion(bf16[1,3,1792,128]{3,2,1,0:T(8,128)(2,1)} %param.9, f32[2,512,128]{2,1,0:T(8,128)S(1)} %add.237), kind=kOutput, calls=%fused_computation.2 | convolution fusion | flops 236191744 | bytes 2818048 | tf_op jit(solution)/shard_map/dot_general | solution.py:60
  128.2 15.7 %all-to-all-done.3 = bf16[32,16,1792]{2,1,0:T(8,128)(2,1)S(1)} async-done(((bf16[32,16,1792]{2,1,0:T(8,128)(2,1)}), bf16[32,16,1792]{2,1,0:T(8,128)(2,1)S(1)}, u32[]{:S(2)}, u32[]{:S(2)}) %all-to-all-start.3) | async-done | bytes 1835040 | tf_op jit(solution)/shard_map/all_to_all | solution.py:53
  143.9 1.2 copy-done
  145.1 5.9 %all-to-all-start.4 = ((bf16[32,16,1792]{2,1,0:T(8,128)(2,1)}), bf16[32,16,1792]{2,1,0:T(8,128)(2,1)S(1)}, u32[]{:S(2)}, u32[]{:S(2)}) async-start(bf16[32,16,1792]{2,1,0:T(8,128)(2,1)} %bitcast.109), calls=%async_computation.4 | async-start | bytes 3670016 | tf_op jit(solution)/shard_map/all_to_all | solution.py:53
  151.1 2.4 fusion.45
  153.5 1.7 fusion
  155.2 3.5 %reshape.275 = bf16[2,128,2,4,224]{4,3,2,1,0:T(4,128)(2,1)S(1)} reshape(bf16[256,1792]{1,0:T(8,128)(2,1)} %fusion) | data formatting | bytes 1835008 | tf_op jit(solution)/shard_map/reshape | solution.py:78
  158.7 2.2 copy.18
  161.0 1.3 copy.13
  163.1 2.2 collective-permute-start.5
  165.3 9.3 %collective-permute-start.6 = (bf16[2,128,448]{1,2,0:T(8,128)(2,1)S(1)}, bf16[2,128,448]{1,2,0:T(8,128)(2,1)}, u32[]{:S(2)}, u32[]{:S(2)}) collective-permute-start(bf16[2,128,448]{1,2,0:T(8,128)(2,1)S(1)} %get-tuple-element.42), channel_id=1, source_target_pairs={{0,2},{1,3},{2,0},{3,1},{4,6},{5,7},{6,4},{7,5},{8,10},{9,11},{10,... | collective-permute-start | bytes 688136 | tf_op jit(solution)/shard_map/ppermute | solution.py:89
  174.6 1.9 collective-permute-start.7
  178.1 1.5 reshape.276
  179.5 1.4 copy.19
  181.2 6.8 %all-to-all-start.5 = ((bf16[16,336,128]{2,1,0:T(8,128)(2,1)}), bf16[16,336,128]{2,1,0:T(8,128)(2,1)S(1)}, u32[]{:S(2)}, u32[]{:S(2)}) async-start(bf16[16,336,128]{2,1,0:T(8,128)(2,1)} %select_select_fusion), calls=%async_computation.5 | async-start | bytes 2752512 | tf_op jit(solution)/shard_map/all_to_all | solution.py:141
  188.0 3.1 %collective-permute-start.10 = (bf16[2,128,448]{1,2,0:T(8,128)(2,1)S(1)}, bf16[2,128,448]{1,2,0:T(8,128)(2,1)S(1)}, u32[]{:S(2)}, u32[]{:S(2)}) collective-permute-start(bf16[2,128,448]{1,2,0:T(8,128)(2,1)S(1)} %get-tuple-element.46), channel_id=1, source_target_pairs={{0,2},{1,3},{2,0},{3,1},{4,6},{5,7},{6,4},{7,5},{8,10},{9,11},{10,... | collective-permute-start | bytes 688136 | tf_op jit(solution)/shard_map/ppermute | solution.py:89
  191.1 5.3 %collective-permute-start.11 = (bf16[2,128,448]{1,2,0:T(8,128)(2,1)S(1)}, bf16[2,128,448]{1,2,0:T(8,128)(2,1)S(1)}, u32[]{:S(2)}, u32[]{:S(2)}) collective-permute-start(bf16[2,128,448]{1,2,0:T(8,128)(2,1)S(1)} %get-tuple-element.45), channel_id=1, source_target_pairs={{0,3},{1,2},{2,1},{3,0},{4,7},{5,6},{6,5},{7,4},{8,11},{9,10},{10,... | collective-permute-start | bytes 688136 | tf_op jit(solution)/shard_map/ppermute | solution.py:89
  196.4 2.2 collective-permute-start.9
  198.7 1.3 add_convert_fusion.1
  200.0 5.4 %collective-permute-start.8 = (bf16[128,448]{0,1:T(8,128)(2,1)S(1)}, bf16[128,448]{0,1:T(8,128)(2,1)S(1)}, u32[]{:S(2)}, u32[]{:S(2)}) collective-permute-start(bf16[128,448]{0,1:T(8,128)(2,1)S(1)} %dynamic-slice_bitcast_fusion.10), channel_id=1, source_target_pairs={{0,4},{4,0},{1,5},{5,1},{2,6},{6,2},{3,7},{7,3},{8,12},{12,8},{9,1... | collective-permute-start | bytes 344072 | tf_op jit(solution)/shard_map/ppermute | solution.py:14
  205.4 5.2 %collective-permute-done.10 = bf16[2,128,448]{1,2,0:T(8,128)(2,1)S(1)} collective-permute-done((bf16[2,128,448]{1,2,0:T(8,128)(2,1)S(1)}, bf16[2,128,448]{1,2,0:T(8,128)(2,1)S(1)}, u32[]{:S(2)}, u32[]{:S(2)}) %collective-permute-start.10) | collective-permute-done | bytes 229408 | tf_op jit(solution)/shard_map/ppermute | solution.py:89
  210.5 5.2 %collective-permute-done.9 = bf16[2,128,448]{1,2,0:T(8,128)(2,1)S(1)} collective-permute-done((bf16[2,128,448]{1,2,0:T(8,128)(2,1)S(1)}, bf16[2,128,448]{1,2,0:T(8,128)(2,1)S(1)}, u32[]{:S(2)}, u32[]{:S(2)}) %collective-permute-start.9) | collective-permute-done | bytes 229408 | tf_op jit(solution)/shard_map/ppermute | solution.py:89
  215.9 3.4 %collective-permute-start.12 = (bf16[128,448]{0,1:T(8,128)(2,1)S(1)}, bf16[128,448]{0,1:T(8,128)(2,1)S(1)}, u32[]{:S(2)}, u32[]{:S(2)}) collective-permute-start(bf16[128,448]{0,1:T(8,128)(2,1)S(1)} %get-tuple-element.48), channel_id=1, source_target_pairs={{0,23},{1,22},{2,21},{3,20},{4,19},{5,18},{6,17},{7,16},{16,7},{17... | collective-permute-start | bytes 344072 | tf_op jit(solution)/shard_map/ppermute | solution.py:18
  219.3 9.8 %collective-permute-start.13 = (bf16[128,448]{0,1:T(8,128)(2,1)S(1)}, bf16[128,448]{0,1:T(8,128)(2,1)S(1)}, u32[]{:S(2)}, u32[]{:S(2)}) collective-permute-start(bf16[128,448]{0,1:T(8,128)(2,1)S(1)} %get-tuple-element.49), channel_id=1, source_target_pairs={{0,19},{1,18},{2,17},{3,16},{4,23},{5,22},{6,21},{7,20},{16,3},{17... | collective-permute-start | bytes 344072 | tf_op jit(solution)/shard_map/ppermute | solution.py:149
  229.2 10.5 %collective-permute-done.13 = bf16[128,448]{0,1:T(8,128)(2,1)S(1)} collective-permute-done((bf16[128,448]{0,1:T(8,128)(2,1)S(1)}, bf16[128,448]{0,1:T(8,128)(2,1)S(1)}, u32[]{:S(2)}, u32[]{:S(2)}) %collective-permute-start.13) | collective-permute-done | bytes 114720 | tf_op jit(solution)/shard_map/ppermute | solution.py:149
  (44 shorter events, 7.7 us)
Async XLA Ops:
  8.7 19.9 %copy-start.2 = (f32[128,2]{0,1:T(2,128)S(1)}, f32[128,2]{0,1:T(2,128)}, u32[]{:S(2)}) copy-start(f32[128,2]{0,1:T(2,128)} %param.8) | copy-start | bytes 3076
  8.7 40.6 %all-to-all-start = ((bf16[32,16,1792]{2,1,0:T(8,128)(2,1)}), bf16[32,16,1792]{2,1,0:T(8,128)(2,1)S(1)}, u32[]{:S(2)}, u32[]{:S(2)}) async-start(bf16[32,16,1792]{2,1,0:T(8,128)(2,1)} %bitcast.11), calls=%async_computation | async-start | bytes 3670016 | tf_op jit(solution)/shard_map/all_to_all | solution.py:53
  19.4 29.9 %collective-permute-start = (bf16[64,1792]{1,0:T(8,128)(2,1)S(1)}, bf16[64,1792]{1,0:T(8,128)(2,1)S(1)}, u32[]{:S(2)}, u32[]{:S(2)}) collective-permute-start(bf16[64,1792]{1,0:T(8,128)(2,1)S(1)} %constant_dynamic-slice_fusion), channel_id=1, source_target_pairs={{0,23},{1,22},{2,21},{3,20},{4,19},{5,18},{6,17},{7,16},{16,7},{17... | collective-permute-start | bytes 688136 | tf_op jit(solution)/shard_map/ppermute | solution.py:18
  28.6 20.7 %collective-permute-start.1 = (f32[4,128]{1,0:T(4,128)S(1)}, f32[4,128]{1,0:T(4,128)S(1)}, u32[]{:S(2)}, u32[]{:S(2)}) collective-permute-start(f32[4,128]{1,0:T(4,128)S(1)} %pad_maximum_fusion), channel_id=1, source_target_pairs={{0,23},{1,22},{2,21},{3,20},{4,19},{5,18},{6,17},{7,16},{16,7},{17... | collective-permute-start | bytes 6152 | tf_op jit(solution)/shard_map/ppermute | solution.py:18
  49.3 25.9 %all-to-all-start.1 = ((bf16[16,336,128]{2,1,0:T(8,128)(2,1)}), bf16[16,336,128]{2,1,0:T(8,128)(2,1)S(1)}, u32[]{:S(2)}, u32[]{:S(2)}) async-start(bf16[16,336,128]{2,1,0:T(8,128)(2,1)} %bitcast.8), calls=%async_computation.1 | async-start | bytes 2752512 | tf_op jit(solution)/shard_map/all_to_all | solution.py:126
  75.2 35.4 %all-to-all-start.2 = ((bf16[32,16,1792]{2,1,0:T(8,128)(2,1)}), bf16[32,16,1792]{2,1,0:T(8,128)(2,1)}, u32[]{:S(2)}, u32[]{:S(2)}) async-start(bf16[32,16,1792]{2,1,0:T(8,128)(2,1)} %bitcast.23), calls=%async_computation.2 | async-start | bytes 3670016 | tf_op jit(solution)/shard_map/all_to_all | solution.py:53
  87.5 6.0 %collective-permute-start.2 = (f32[2,512,128]{2,1,0:T(8,128)}, f32[2,512,128]{2,1,0:T(8,128)S(1)}, u32[]{:S(2)}, u32[]{:S(2)}) collective-permute-start(f32[2,512,128]{2,1,0:T(8,128)} %fusion.6), channel_id=1, source_target_pairs={{0,8},{8,0},{1,9},{9,1},{2,10},{10,2},{3,11},{11,3},{4,12},{12,4},... | collective-permute-start | bytes 1572872 | tf_op jit(solution)/shard_map/ppermute | solution.py:14
  94.6 14.6 %collective-permute-start.3 = (bf16[336,128]{1,0:T(8,128)(2,1)S(1)}, bf16[336,128]{1,0:T(8,128)(2,1)S(1)}, u32[]{:S(2)}, u32[]{:S(2)}) collective-permute-start(bf16[336,128]{1,0:T(8,128)(2,1)S(1)} %bitcast_select_fusion.1), channel_id=1, source_target_pairs={{0,16},{16,0},{1,17},{17,1},{2,18},{18,2},{3,19},{19,3},{4,20},{20... | collective-permute-start | bytes 258056 | tf_op jit(solution)/shard_map/ppermute | solution.py:14
  110.6 33.3 %all-to-all-start.3 = ((bf16[32,16,1792]{2,1,0:T(8,128)(2,1)}), bf16[32,16,1792]{2,1,0:T(8,128)(2,1)S(1)}, u32[]{:S(2)}, u32[]{:S(2)}) async-start(bf16[32,16,1792]{2,1,0:T(8,128)(2,1)} %bitcast.110), calls=%async_computation.3 | async-start | bytes 3670016 | tf_op jit(solution)/shard_map/all_to_all | solution.py:53
  121.4 3.8 %collective-permute-start.4 = (f32[2,512,128]{2,1,0:T(8,128)S(1)}, f32[2,512,128]{2,1,0:T(8,128)S(1)}, u32[]{:S(2)}, u32[]{:S(2)}) collective-permute-start(f32[2,512,128]{2,1,0:T(8,128)S(1)} %fusion.9), channel_id=1, source_target_pairs={{0,8},{8,0},{1,9},{9,1},{2,10},{10,2},{3,11},{11,3},{4,12},{12,4},... | collective-permute-start | bytes 1572872 | tf_op jit(solution)/shard_map/ppermute | solution.py:14
  143.9 1.2 copy-start
  145.1 31.4 %all-to-all-start.4 = ((bf16[32,16,1792]{2,1,0:T(8,128)(2,1)}), bf16[32,16,1792]{2,1,0:T(8,128)(2,1)S(1)}, u32[]{:S(2)}, u32[]{:S(2)}) async-start(bf16[32,16,1792]{2,1,0:T(8,128)(2,1)} %bitcast.109), calls=%async_computation.4 | async-start | bytes 3670016 | tf_op jit(solution)/shard_map/all_to_all | solution.py:53
  151.1 2.4 copy-start.1
  163.1 33.4 %collective-permute-start.5 = (bf16[2,128,448]{1,2,0:T(8,128)(2,1)}, bf16[2,128,448]{1,2,0:T(8,128)(2,1)}, u32[]{:S(2)}, u32[]{:S(2)}) collective-permute-start(bf16[2,128,448]{1,2,0:T(8,128)(2,1)} %get-tuple-element.40), channel_id=1, source_target_pairs={{0,1},{1,0},{2,3},{3,2},{4,5},{5,4},{6,7},{7,6},{8,9},{9,8},{10,11... | collective-permute-start | bytes 688136 | tf_op jit(solution)/shard_map/ppermute | solution.py:89
  165.3 33.4 %collective-permute-start.6 = (bf16[2,128,448]{1,2,0:T(8,128)(2,1)S(1)}, bf16[2,128,448]{1,2,0:T(8,128)(2,1)}, u32[]{:S(2)}, u32[]{:S(2)}) collective-permute-start(bf16[2,128,448]{1,2,0:T(8,128)(2,1)S(1)} %get-tuple-element.42), channel_id=1, source_target_pairs={{0,2},{1,3},{2,0},{3,1},{4,6},{5,7},{6,4},{7,5},{8,10},{9,11},{10,... | collective-permute-start | bytes 688136 | tf_op jit(solution)/shard_map/ppermute | solution.py:89
  174.6 24.1 %collective-permute-start.7 = (bf16[2,128,448]{1,2,0:T(8,128)(2,1)S(1)}, bf16[2,128,448]{1,2,0:T(8,128)(2,1)}, u32[]{:S(2)}, u32[]{:S(2)}) collective-permute-start(bf16[2,128,448]{1,2,0:T(8,128)(2,1)S(1)} %get-tuple-element.41), channel_id=1, source_target_pairs={{0,3},{1,2},{2,1},{3,0},{4,7},{5,6},{6,5},{7,4},{8,11},{9,10},{10,... | collective-permute-start | bytes 688136 | tf_op jit(solution)/shard_map/ppermute | solution.py:89
  181.2 59.2 %all-to-all-start.5 = ((bf16[16,336,128]{2,1,0:T(8,128)(2,1)}), bf16[16,336,128]{2,1,0:T(8,128)(2,1)S(1)}, u32[]{:S(2)}, u32[]{:S(2)}) async-start(bf16[16,336,128]{2,1,0:T(8,128)(2,1)} %select_select_fusion), calls=%async_computation.5 | async-start | bytes 2752512 | tf_op jit(solution)/shard_map/all_to_all | solution.py:141
  188.0 22.5 %collective-permute-start.10 = (bf16[2,128,448]{1,2,0:T(8,128)(2,1)S(1)}, bf16[2,128,448]{1,2,0:T(8,128)(2,1)S(1)}, u32[]{:S(2)}, u32[]{:S(2)}) collective-permute-start(bf16[2,128,448]{1,2,0:T(8,128)(2,1)S(1)} %get-tuple-element.46), channel_id=1, source_target_pairs={{0,2},{1,3},{2,0},{3,1},{4,6},{5,7},{6,4},{7,5},{8,10},{9,11},{10,... | collective-permute-start | bytes 688136 | tf_op jit(solution)/shard_map/ppermute | solution.py:89
  191.1 19.4 %collective-permute-start.11 = (bf16[2,128,448]{1,2,0:T(8,128)(2,1)S(1)}, bf16[2,128,448]{1,2,0:T(8,128)(2,1)S(1)}, u32[]{:S(2)}, u32[]{:S(2)}) collective-permute-start(bf16[2,128,448]{1,2,0:T(8,128)(2,1)S(1)} %get-tuple-element.45), channel_id=1, source_target_pairs={{0,3},{1,2},{2,1},{3,0},{4,7},{5,6},{6,5},{7,4},{8,11},{9,10},{10,... | collective-permute-start | bytes 688136 | tf_op jit(solution)/shard_map/ppermute | solution.py:89
  196.4 19.3 %collective-permute-start.9 = (bf16[2,128,448]{1,2,0:T(8,128)(2,1)S(1)}, bf16[2,128,448]{1,2,0:T(8,128)(2,1)S(1)}, u32[]{:S(2)}, u32[]{:S(2)}) collective-permute-start(bf16[2,128,448]{1,2,0:T(8,128)(2,1)S(1)} %get-tuple-element.47), channel_id=1, source_target_pairs={{0,1},{1,0},{2,3},{3,2},{4,5},{5,4},{6,7},{7,6},{8,9},{9,8},{10,11... | collective-permute-start | bytes 688136 | tf_op jit(solution)/shard_map/ppermute | solution.py:89
  200.0 29.2 %collective-permute-start.8 = (bf16[128,448]{0,1:T(8,128)(2,1)S(1)}, bf16[128,448]{0,1:T(8,128)(2,1)S(1)}, u32[]{:S(2)}, u32[]{:S(2)}) collective-permute-start(bf16[128,448]{0,1:T(8,128)(2,1)S(1)} %dynamic-slice_bitcast_fusion.10), channel_id=1, source_target_pairs={{0,4},{4,0},{1,5},{5,1},{2,6},{6,2},{3,7},{7,3},{8,12},{12,8},{9,1... | collective-permute-start | bytes 344072 | tf_op jit(solution)/shard_map/ppermute | solution.py:14
  215.9 13.3 %collective-permute-start.12 = (bf16[128,448]{0,1:T(8,128)(2,1)S(1)}, bf16[128,448]{0,1:T(8,128)(2,1)S(1)}, u32[]{:S(2)}, u32[]{:S(2)}) collective-permute-start(bf16[128,448]{0,1:T(8,128)(2,1)S(1)} %get-tuple-element.48), channel_id=1, source_target_pairs={{0,23},{1,22},{2,21},{3,20},{4,19},{5,18},{6,17},{7,16},{16,7},{17... | collective-permute-start | bytes 344072 | tf_op jit(solution)/shard_map/ppermute | solution.py:18
  219.3 20.4 %collective-permute-start.13 = (bf16[128,448]{0,1:T(8,128)(2,1)S(1)}, bf16[128,448]{0,1:T(8,128)(2,1)S(1)}, u32[]{:S(2)}, u32[]{:S(2)}) collective-permute-start(bf16[128,448]{0,1:T(8,128)(2,1)S(1)} %get-tuple-element.49), channel_id=1, source_target_pairs={{0,19},{1,18},{2,17},{3,16},{4,23},{5,22},{6,21},{7,20},{16,3},{17... | collective-permute-start | bytes 344072 | tf_op jit(solution)/shard_map/ppermute | solution.py:149

commit v12 on v9

--- a/solution.py
+++ b/solution.py
@@ -1,6 +1,10 @@
+import functools
+
 import jax
 import jax.numpy as jnp
 from jax import lax
+from jax.experimental import pallas as pl
+from jax.experimental.pallas import tpu as pltpu
 from jax.experimental.layout import Layout, with_layout_constraint
 from jax.sharding import Mesh, PartitionSpec as P
 
@@ -62,21 +66,43 @@
     ).astype(jnp.bfloat16)
 
 
-def weighted(back, codes, rows):
+def columns_kernel(near, high, low, back, out):
+    total = jnp.dot(high[...], back[...], preferred_element_type=jnp.float32)
+    total += jnp.dot(low[...], back[...], preferred_element_type=jnp.float32)
+    total = total.astype(jnp.bfloat16)
+    tok_rows = total.shape[0] // 2
+    cols = total.shape[1] // (2 * near)
+    for z in range(2 * near):
+        base = z * cols // 128 * 128
+        offset = z * cols - base
+        span = -(-(offset + cols) // 128) * 128
+        at = lax.broadcasted_iota(jnp.int32, (span, 2 * cols), 0) - offset
+        to = lax.broadcasted_iota(jnp.int32, (span, 2 * cols), 1)
+        block = jnp.zeros((2 * cols, tok_rows), jnp.float32)
+        for half in range(2):
+            hit = (at + half * cols == to) & (at >= 0) & (at < cols)
+            take = jnp.where(hit, 1.0, 0.0).astype(jnp.bfloat16)
+            rows = total[half * tok_rows : (half + 1) * tok_rows, base : base + span]
+            block += lax.dot_general(take, rows, (((0,), (1,)), ((), ())), preferred_element_type=jnp.float32)
+        out[z % near, z // near] = block.astype(jnp.bfloat16)
+
+
+def combined(back, codes, rows, near):
     at = jnp.arange(back.shape[0], dtype=jnp.int32)
     gate = jnp.concatenate([codes[2:4], codes[2:4]], axis=1)
     mix = sum(jnp.where(rows[k][:, None] == at[None, :], gate[k][:, None], 0.0) for k in range(2))
     high = mix.astype(jnp.bfloat16)
     low = (mix - high.astype(jnp.float32)).astype(jnp.bfloat16)
-    return jnp.dot(high, back, preferred_element_type=jnp.float32) + jnp.dot(
-        low, back, preferred_element_type=jnp.float32
-    )
-
-
-def by_columns(mixed, near):
-    tok_rows = mixed.shape[0] // 2
-    parts = mixed.astype(jnp.bfloat16).reshape(2, tok_rows, 2, near, -1)
-    return jnp.transpose(parts, (3, 2, 1, 0, 4)).reshape(near, 2, tok_rows, -1)
+    shape = (near, 2, back.shape[1] // near, mix.shape[0] // 2)
+    flops = 4 * mix.shape[0] * back.shape[0] * back.shape[1]
+    return pl.pallas_call(
+        functools.partial(columns_kernel, near),
+        out_shape=jax.ShapeDtypeStruct(shape, jnp.bfloat16),
+        in_specs=[pl.BlockSpec(memory_space=pltpu.VMEM)] * 3,
+        out_specs=pl.BlockSpec(memory_space=pltpu.VMEM),
+        compiler_params=pltpu.CompilerParams(vmem_limit_bytes=32 * 2**20),
+        cost_estimate=pl.CostEstimate(flops=flops, bytes_accessed=4 * back.size, transcendentals=0),
+    )(high, low, back)
 
 
 def near_sum(parts, place, mine, beside):
@@ -136,9 +162,9 @@
     payload, back = tied((expert_part(other_sent, own), back))
     other_back = exchange(payload)
 
-    parts = by_columns(weighted(back, codes, rows), near)
+    parts = combined(back, codes, rows, near)
     kept, other_back = near_sum(parts, place, 0, other_back)
-    other_parts = by_columns(weighted(other_back, other_codes, other_rows), near)
+    other_parts = combined(other_back, other_codes, other_rows, near)
     other_kept, chosen = near_sum(other_parts, place, near - 1, chosen)
     arrived = lax.all_to_all(chosen, ("y", "x"), split_axis=0, concat_axis=0, tiled=True)
 
@@ -149,7 +175,7 @@
     total += swap(of(kept, 1 - far), "ma").astype(jnp.float32)
     total += mirrored(of(other_kept, 1 - far)).astype(jnp.float32)
     total += lax.ppermute(of(other_kept, far), RING, [(i, i ^ 11) for i in range(16)]).astype(jnp.float32)
-    return total.astype(jnp.bfloat16), arrived.reshape(expert_weights.shape)
+    return total.astype(jnp.bfloat16).T, arrived.reshape(expert_weights.shape)
 
 
 def solution(mesh):

time: 238 us -> 235 us (0.987)
  waiting for transfers between devices: 70.2 us -> 79.7 us
  local copies, waits for them, and re-layouts: 17.5 us -> 10.9 us
  matrix products: 17.7 us -> 12.1 us
  Pallas kernels: 0 us -> 4.63 us
  starting transfers between devices: 101 us -> 97.4 us
    ppermute x3, waiting for transfers between devices: 15.8 us -> 30.6 us  [mirrored(): return lax.ppermute(value, RING, [(i, 15 - i) for i in range(16)])]
    ppermute x1, waiting for transfers between devices: 10 us -> 0.96 us  [shards(): lax.ppermute(of(other_kept, far), RING, [(i, i ^ 11) for i in range(16)])]
    reshape x4 -> x0, local copies, waits for them, and re-layouts: 8.71 us -> none  [by_columns(): parts = mixed.astype(jnp.bfloat16).reshape(2, tok_rows, 2, near, -1)]
    all_to_all x4, waiting for transfers between devices: 24.9 us -> 31.8 us  [exchange(): lax.all_to_all(blocks, axes, split_axis=0, concat_axis=0, tiled=True)]
    ppermute x1, starting transfers between devices: 9.75 us -> 3.19 us  [shards(): lax.ppermute(of(other_kept, far), RING, [(i, i ^ 11) for i in range(16)])]
    dot_general x4 -> x0, matrix products: 5.58 us -> none  [the longest x2 3.13 us: weighted(): jnp.dot(high, back, preferred_element_type=jnp.float32)]
    pallas_call x0 -> x2, Pallas kernels: none -> 4.63 us  [combined(): pl.pallas_call(functools.partial(columns_kernel, near), out_shape=jax.Sha...]
    ppermute x6, waiting for transfers between devices: 11.1 us -> 8.04 us  [near_sum(): lax.ppermute(block, NEAR, [(i, i ^ step) for i in range(count)])]
  transfers between devices with their start and end apart: 20 -> 20, of which waited for: 9 -> 9; matrix products, arithmetic and copies ran while one was open for 16% -> 11% of each run, Pallas kernels for 0% -> 2%
where the time goes in v12:
time: 235 us; the launch traced here: 233 us
  starting transfers between devices  97.4 us (41%)
  waiting for transfers between devices  79.7 us (34%)
  blocking collectives  18.7 us (8%)
  matrix products  12.1 us (5%)
  local copies, waits for them, and re-layouts  10.9 us (5%)
  other arithmetic  5.87 us (2%)
  Pallas kernels  4.63 us (2%)
  between operations  3.75 us (2%)
    all_to_all x4, waiting for transfers between devices, exchange(): lax.all_to_all(blocks, axes, split_axis=0, concat_axis=0, tiled=True)  31.8 us
    ppermute x3, waiting for transfers between devices, mirrored(): return lax.ppermute(value, RING, [(i, 15 - i) for i in range(16)])  30.6 us
    all_to_all x4, starting transfers between devices, exchange(): lax.all_to_all(blocks, axes, split_axis=0, concat_axis=0, tiled=True)  28.2 us
    all_gather x1, blocking collectives, shards(): other_table = lax.all_gather(quarter, NEAR, tiled=True)  18.7 us
    ppermute x4, starting transfers between devices, swap(): return lax.ppermute(value, axis, [(0, 1), (1, 0)])  18.1 us
    ppermute x3, starting transfers between devices, mirrored(): return lax.ppermute(value, RING, [(i, 15 - i) for i in range(16)])  18 us
    ppermute x6, starting transfers between devices, near_sum(): lax.ppermute(block, NEAR, [(i, i ^ step) for i in range(count)])  17.8 us
    ppermute x4, waiting for transfers between devices, swap(): return lax.ppermute(value, axis, [(0, 1), (1, 0)])  8.37 us
  transfers between devices with their start and end apart: 20, of which 9 were waited for; matrix products, arithmetic and copies ran while one was open for 11% of the time, Pallas kernels for 2%

profile of v12, /device:TPU:1, one launch (start us, length us, event | category | flops | bytes accessed | tf_op | source)
XLA Modules:
  0.0 233.1 jit_solution(666393504657838515)
XLA Ops:
  0.6 7.6 %all-to-all-start = ((bf16[16,336,128]{2,1,0:T(8,128)(2,1)}), bf16[16,336,128]{2,1,0:T(8,128)(2,1)S(1)}, u32[]{:S(2)}, u32[]{:S(2)}) async-start(bf16[16,336,128]{2,1,0:T(8,128)(2,1)} %bitcast.104), calls=%async_computation | async-start | bytes 2752512 | tf_op jit(solution)/shard_map/all_to_all | solution.py:149
  8.2 1.6 copy.9
  9.8 1.7 copy.12
  11.5 2.3 reshape.258
  13.9 11.1 %collective-permute-start = (bf16[64,1792]{1,0:T(8,128)(2,1)S(1)}, bf16[64,1792]{1,0:T(8,128)(2,1)S(1)}, u32[]{:S(2)}, u32[]{:S(2)}) collective-permute-start(bf16[64,1792]{1,0:T(8,128)(2,1)S(1)} %constant_dynamic-slice_fusion), channel_id=1, source_target_pairs={{0,23},{1,22},{2,21},{3,20},{4,19},{5,18},{6,17},{7,16},{16,7},{17... | collective-permute-start | bytes 688136 | tf_op jit(solution)/shard_map/ppermute | solution.py:22
  25.9 1.9 collective-permute-start.1
  27.9 1.9 convolution_convert_fusion.1
  29.8 15.7 %collective-permute-done.1 = f32[4,128]{1,0:T(4,128)S(1)} collective-permute-done((f32[4,128]{1,0:T(4,128)S(1)}, f32[4,128]{1,0:T(4,128)S(1)}, u32[]{:S(2)}, u32[]{:S(2)}) %collective-permute-start.1) | collective-permute-done | bytes 2080 | tf_op jit(solution)/shard_map/ppermute | solution.py:22
  45.5 8.0 %all-to-all-start.1 = ((bf16[32,16,1792]{2,1,0:T(8,128)(2,1)}), bf16[32,16,1792]{2,1,0:T(8,128)(2,1)}, u32[]{:S(2)}, u32[]{:S(2)}) async-start(bf16[32,16,1792]{2,1,0:T(8,128)(2,1)} %bitcast.16), calls=%async_computation.1 | async-start | bytes 3670016 | tf_op jit(solution)/shard_map/all_to_all | solution.py:57
  53.5 18.7 %all_gather.3 = bf16[256,1792]{1,0:T(8,128)(2,1)S(1)} all-gather(bf16[64,1792]{1,0:T(8,128)(2,1)S(1)} %collective-permute-done), channel_id=1, replica_groups=mesh['y'=4,'x'=4,'zh'=2,'c'=2,'ma'=2,'mb'=2,'mc'=2] {'mb','mc'}, dimensions={0}, use_global_device_ids=true | all-gather | bytes 1146880 | tf_op jit(solution)/shard_map/all_gather | solution.py:156
  72.2 1.9 convolution_convert_fusion
  74.1 4.4 %all-to-all-done.1 = bf16[32,16,1792]{2,1,0:T(8,128)(2,1)} async-done(((bf16[32,16,1792]{2,1,0:T(8,128)(2,1)}), bf16[32,16,1792]{2,1,0:T(8,128)(2,1)}, u32[]{:S(2)}, u32[]{:S(2)}) %all-to-all-start.1) | async-done | bytes 1835040 | tf_op jit(solution)/shard_map/all_to_all | solution.py:57
  78.5 6.7 %all-to-all-start.2 = ((bf16[32,16,1792]{2,1,0:T(8,128)(2,1)}), bf16[32,16,1792]{2,1,0:T(8,128)(2,1)}, u32[]{:S(2)}, u32[]{:S(2)}) async-start(bf16[32,16,1792]{2,1,0:T(8,128)(2,1)} %bitcast.23), calls=%async_computation.2 | async-start | bytes 3670016 | tf_op jit(solution)/shard_map/all_to_all | solution.py:57
  87.8 1.3 fusion.52
  89.1 8.9 %collective-permute-start.3 = (bf16[336,128]{1,0:T(8,128)(2,1)S(1)}, bf16[336,128]{1,0:T(8,128)(2,1)S(1)}, u32[]{:S(2)}, u32[]{:S(2)}) collective-permute-start(bf16[336,128]{1,0:T(8,128)(2,1)S(1)} %bitcast_select_fusion.1), channel_id=1, source_target_pairs={{0,16},{16,0},{1,17},{17,1},{2,18},{18,2},{3,19},{19,3},{4,20},{20... | collective-permute-start | bytes 258056 | tf_op jit(solution)/shard_map/ppermute | solution.py:18
  98.0 2.1 fusion.4
  100.2 2.6 %collective-permute-start.2 = (f32[2,512,128]{2,1,0:T(8,128)S(1)}, f32[2,512,128]{2,1,0:T(8,128)S(1)}, u32[]{:S(2)}, u32[]{:S(2)}) collective-permute-start(f32[2,512,128]{2,1,0:T(8,128)S(1)} %fusion.4), channel_id=1, source_target_pairs={{0,8},{8,0},{1,9},{9,1},{2,10},{10,2},{3,11},{11,3},{4,12},{12,4},... | collective-permute-start | bytes 1572872 | tf_op jit(solution)/shard_map/ppermute | solution.py:18
  102.8 6.7 %collective-permute-done.3 = bf16[336,128]{1,0:T(8,128)(2,1)S(1)} collective-permute-done((bf16[336,128]{1,0:T(8,128)(2,1)S(1)}, bf16[336,128]{1,0:T(8,128)(2,1)S(1)}, u32[]{:S(2)}, u32[]{:S(2)}) %collective-permute-start.3) | collective-permute-done | bytes 86048 | tf_op jit(solution)/shard_map/ppermute | solution.py:18
  109.5 1.3 select_select_fusion
  110.9 1.9 convolution_convert_fusion.3
  112.8 7.6 %all-to-all-start.3 = ((bf16[32,16,1792]{2,1,0:T(8,128)(2,1)}), bf16[32,16,1792]{2,1,0:T(8,128)(2,1)S(1)}, u32[]{:S(2)}, u32[]{:S(2)}) async-start(bf16[32,16,1792]{2,1,0:T(8,128)(2,1)} %bitcast.102), calls=%async_computation.3 | async-start | bytes 3670016 | tf_op jit(solution)/shard_map/all_to_all | solution.py:57
  120.4 2.1 fusion.7
  122.6 2.1 collective-permute-start.4
  124.7 1.7 collective-permute-done.4
  126.5 1.9 convolution_convert_fusion.2
  128.3 17.0 %all-to-all-done.3 = bf16[32,16,1792]{2,1,0:T(8,128)(2,1)S(1)} async-done(((bf16[32,16,1792]{2,1,0:T(8,128)(2,1)}), bf16[32,16,1792]{2,1,0:T(8,128)(2,1)S(1)}, u32[]{:S(2)}, u32[]{:S(2)}) %all-to-all-start.3) | async-done | bytes 1835040 | tf_op jit(solution)/shard_map/all_to_all | solution.py:57
  145.3 1.2 copy-done
  146.6 5.9 %all-to-all-start.4 = ((bf16[32,16,1792]{2,1,0:T(8,128)(2,1)}), bf16[32,16,1792]{2,1,0:T(8,128)(2,1)S(1)}, u32[]{:S(2)}, u32[]{:S(2)}) async-start(bf16[32,16,1792]{2,1,0:T(8,128)(2,1)} %bitcast.101), calls=%async_computation.4 | async-start | bytes 3670016 | tf_op jit(solution)/shard_map/all_to_all | solution.py:57
  153.0 1.5 copy-done.1
  154.5 2.3 shard_map.77
  156.8 0.8 dynamic-slice_bitcast_fusion.6
  157.6 1.9 collective-permute-start.5
  159.5 1.9 collective-permute-start.6
  161.4 5.6 %collective-permute-start.7 = (bf16[2,448,128]{2,1,0:T(8,128)(2,1)S(1)}, bf16[2,448,128]{2,1,0:T(8,128)(2,1)}, u32[]{:S(2)}, u32[]{:S(2)}) collective-permute-start(bf16[2,448,128]{2,1,0:T(8,128)(2,1)S(1)} %get-tuple-element.41), channel_id=1, source_target_pairs={{0,3},{1,2},{2,1},{3,0},{4,7},{5,6},{6,5},{7,4},{8,11},{9,10},{10,... | collective-permute-start | bytes 688136 | tf_op jit(solution)/shard_map/ppermute | solution.py:115
  167.0 10.4 %all-to-all-done.4 = bf16[32,16,1792]{2,1,0:T(8,128)(2,1)S(1)} async-done(((bf16[32,16,1792]{2,1,0:T(8,128)(2,1)}), bf16[32,16,1792]{2,1,0:T(8,128)(2,1)S(1)}, u32[]{:S(2)}, u32[]{:S(2)}) %all-to-all-start.4) | async-done | bytes 1835040 | tf_op jit(solution)/shard_map/all_to_all | solution.py:57
  177.5 2.3 shard_map.78
  180.5 4.5 %all-to-all-start.5 = ((bf16[16,336,128]{2,1,0:T(8,128)(2,1)}), bf16[16,336,128]{2,1,0:T(8,128)(2,1)S(1)}, u32[]{:S(2)}, u32[]{:S(2)}) async-start(bf16[16,336,128]{2,1,0:T(8,128)(2,1)} %select_select_fusion), calls=%async_computation.5 | async-start | bytes 2752512 | tf_op jit(solution)/shard_map/all_to_all | solution.py:169
  185.0 1.9 collective-permute-start.10
  187.0 1.9 collective-permute-start.11
  188.9 4.5 %collective-permute-start.9 = (bf16[2,448,128]{2,1,0:T(8,128)(2,1)S(1)}, bf16[2,448,128]{2,1,0:T(8,128)(2,1)S(1)}, u32[]{:S(2)}, u32[]{:S(2)}) collective-permute-start(bf16[2,448,128]{2,1,0:T(8,128)(2,1)S(1)} %get-tuple-element.47), channel_id=1, source_target_pairs={{0,1},{1,0},{2,3},{3,2},{4,5},{5,4},{6,7},{7,6},{8,9},{9,8},{10,11... | collective-permute-start | bytes 688136 | tf_op jit(solution)/shard_map/ppermute | solution.py:115
  193.5 1.1 add_convert_fusion.1
  194.6 4.5 %collective-permute-start.8 = (bf16[448,128]{1,0:T(8,128)(2,1)S(1)}, bf16[448,128]{1,0:T(8,128)(2,1)S(1)}, u32[]{:S(2)}, u32[]{:S(2)}) collective-permute-start(bf16[448,128]{1,0:T(8,128)(2,1)S(1)} %dynamic-slice_bitcast_fusion.10), channel_id=1, source_target_pairs={{0,4},{4,0},{1,5},{5,1},{2,6},{6,2},{3,7},{7,3},{8,12},{12,8},{9,1... | collective-permute-start | bytes 344072 | tf_op jit(solution)/shard_map/ppermute | solution.py:18
  199.0 8.0 %collective-permute-done.9 = bf16[2,448,128]{2,1,0:T(8,128)(2,1)S(1)} collective-permute-done((bf16[2,448,128]{2,1,0:T(8,128)(2,1)S(1)}, bf16[2,448,128]{2,1,0:T(8,128)(2,1)S(1)}, u32[]{:S(2)}, u32[]{:S(2)}) %collective-permute-start.9) | collective-permute-done | bytes 229408 | tf_op jit(solution)/shard_map/ppermute | solution.py:115
  207.2 5.0 %collective-permute-start.12 = (bf16[448,128]{1,0:T(8,128)(2,1)S(1)}, bf16[448,128]{1,0:T(8,128)(2,1)S(1)}, u32[]{:S(2)}, u32[]{:S(2)}) collective-permute-start(bf16[448,128]{1,0:T(8,128)(2,1)S(1)} %get-tuple-element.48), channel_id=1, source_target_pairs={{0,23},{1,22},{2,21},{3,20},{4,19},{5,18},{6,17},{7,16},{16,7},{17... | collective-permute-start | bytes 344072 | tf_op jit(solution)/shard_map/ppermute | solution.py:22
  212.2 3.2 %collective-permute-start.13 = (bf16[448,128]{1,0:T(8,128)(2,1)S(1)}, bf16[448,128]{1,0:T(8,128)(2,1)S(1)}, u32[]{:S(2)}, u32[]{:S(2)}) collective-permute-start(bf16[448,128]{1,0:T(8,128)(2,1)S(1)} %get-tuple-element.49), channel_id=1, source_target_pairs={{0,19},{1,18},{2,17},{3,16},{4,23},{5,22},{6,21},{7,20},{16,3},{17... | collective-permute-start | bytes 344072 | tf_op jit(solution)/shard_map/ppermute | solution.py:177
  215.4 14.9 %collective-permute-done.12 = bf16[448,128]{1,0:T(8,128)(2,1)S(1)} collective-permute-done((bf16[448,128]{1,0:T(8,128)(2,1)S(1)}, bf16[448,128]{1,0:T(8,128)(2,1)S(1)}, u32[]{:S(2)}, u32[]{:S(2)}) %collective-permute-start.12) | collective-permute-done | bytes 114720 | tf_op jit(solution)/shard_map/ppermute | solution.py:22
  230.3 1.0 collective-permute-done.13
  232.0 1.1 copy.15
  (46 shorter events, 3.3 us)
Async XLA Ops:
  0.6 44.9 %all-to-all-start = ((bf16[16,336,128]{2,1,0:T(8,128)(2,1)}), bf16[16,336,128]{2,1,0:T(8,128)(2,1)S(1)}, u32[]{:S(2)}, u32[]{:S(2)}) async-start(bf16[16,336,128]{2,1,0:T(8,128)(2,1)} %bitcast.104), calls=%async_computation | async-start | bytes 2752512 | tf_op jit(solution)/shard_map/all_to_all | solution.py:149
  9.8 15.2 %copy-start.4 = (s32[32]{0:T(128)S(1)}, s32[32]{0:T(128)}, u32[]{:S(2)}) copy-start(s32[32]{0:T(128)} %param.10) | copy-start | bytes 388
  9.8 15.2 %copy-start.5 = (s32[32]{0:T(128)S(1)}, s32[32]{0:T(128)}, u32[]{:S(2)}) copy-start(s32[32]{0:T(128)} %param.11) | copy-start | bytes 388
  9.8 15.8 %copy-start.6 = (s32[128,2]{0,1:T(2,128)S(1)}, s32[128,2]{0,1:T(2,128)}, u32[]{:S(2)}) copy-start(s32[128,2]{0,1:T(2,128)} %param.7) | copy-start | bytes 3076
  9.8 16.0 %copy-start.3 = (f32[128,2]{0,1:T(2,128)S(1)}, f32[128,2]{0,1:T(2,128)}, u32[]{:S(2)}) copy-start(f32[128,2]{0,1:T(2,128)} %param.8) | copy-start | bytes 3076
  13.9 31.6 %collective-permute-start = (bf16[64,1792]{1,0:T(8,128)(2,1)S(1)}, bf16[64,1792]{1,0:T(8,128)(2,1)S(1)}, u32[]{:S(2)}, u32[]{:S(2)}) collective-permute-start(bf16[64,1792]{1,0:T(8,128)(2,1)S(1)} %constant_dynamic-slice_fusion), channel_id=1, source_target_pairs={{0,23},{1,22},{2,21},{3,20},{4,19},{5,18},{6,17},{7,16},{16,7},{17... | collective-permute-start | bytes 688136 | tf_op jit(solution)/shard_map/ppermute | solution.py:22
  25.9 19.6 %collective-permute-start.1 = (f32[4,128]{1,0:T(4,128)S(1)}, f32[4,128]{1,0:T(4,128)S(1)}, u32[]{:S(2)}, u32[]{:S(2)}) collective-permute-start(f32[4,128]{1,0:T(4,128)S(1)} %pad_maximum_fusion), channel_id=1, source_target_pairs={{0,23},{1,22},{2,21},{3,20},{4,19},{5,18},{6,17},{7,16},{16,7},{17... | collective-permute-start | bytes 6152 | tf_op jit(solution)/shard_map/ppermute | solution.py:22
  45.5 33.0 %all-to-all-start.1 = ((bf16[32,16,1792]{2,1,0:T(8,128)(2,1)}), bf16[32,16,1792]{2,1,0:T(8,128)(2,1)}, u32[]{:S(2)}, u32[]{:S(2)}) async-start(bf16[32,16,1792]{2,1,0:T(8,128)(2,1)} %bitcast.16), calls=%async_computation.1 | async-start | bytes 3670016 | tf_op jit(solution)/shard_map/all_to_all | solution.py:57
  78.5 19.6 %copy-start.2 = (bf16[1,3,1792,128]{3,2,1,0:T(8,128)(2,1)S(1)}, bf16[1,3,1792,128]{3,2,1,0:T(8,128)(2,1)}, u32[]{:S(2)}) copy-start(bf16[1,3,1792,128]{3,2,1,0:T(8,128)(2,1)} %param.9) | copy-start | bytes 4128772
  78.5 34.3 %all-to-all-start.2 = ((bf16[32,16,1792]{2,1,0:T(8,128)(2,1)}), bf16[32,16,1792]{2,1,0:T(8,128)(2,1)}, u32[]{:S(2)}, u32[]{:S(2)}) async-start(bf16[32,16,1792]{2,1,0:T(8,128)(2,1)} %bitcast.23), calls=%async_computation.2 | async-start | bytes 3670016 | tf_op jit(solution)/shard_map/all_to_all | solution.py:57
  89.1 20.4 %collective-permute-start.3 = (bf16[336,128]{1,0:T(8,128)(2,1)S(1)}, bf16[336,128]{1,0:T(8,128)(2,1)S(1)}, u32[]{:S(2)}, u32[]{:S(2)}) collective-permute-start(bf16[336,128]{1,0:T(8,128)(2,1)S(1)} %bitcast_select_fusion.1), channel_id=1, source_target_pairs={{0,16},{16,0},{1,17},{17,1},{2,18},{18,2},{3,19},{19,3},{4,20},{20... | collective-permute-start | bytes 258056 | tf_op jit(solution)/shard_map/ppermute | solution.py:18
  100.2 10.7 %collective-permute-start.2 = (f32[2,512,128]{2,1,0:T(8,128)S(1)}, f32[2,512,128]{2,1,0:T(8,128)S(1)}, u32[]{:S(2)}, u32[]{:S(2)}) collective-permute-start(f32[2,512,128]{2,1,0:T(8,128)S(1)} %fusion.4), channel_id=1, source_target_pairs={{0,8},{8,0},{1,9},{9,1},{2,10},{10,2},{3,11},{11,3},{4,12},{12,4},... | collective-permute-start | bytes 1572872 | tf_op jit(solution)/shard_map/ppermute | solution.py:18
  112.8 32.5 %all-to-all-start.3 = ((bf16[32,16,1792]{2,1,0:T(8,128)(2,1)}), bf16[32,16,1792]{2,1,0:T(8,128)(2,1)S(1)}, u32[]{:S(2)}, u32[]{:S(2)}) async-start(bf16[32,16,1792]{2,1,0:T(8,128)(2,1)} %bitcast.102), calls=%async_computation.3 | async-start | bytes 3670016 | tf_op jit(solution)/shard_map/all_to_all | solution.py:57
  122.6 3.8 %collective-permute-start.4 = (f32[2,512,128]{2,1,0:T(8,128)S(1)}, f32[2,512,128]{2,1,0:T(8,128)S(1)}, u32[]{:S(2)}, u32[]{:S(2)}) collective-permute-start(f32[2,512,128]{2,1,0:T(8,128)S(1)} %fusion.7), channel_id=1, source_target_pairs={{0,8},{8,0},{1,9},{9,1},{2,10},{10,2},{3,11},{11,3},{4,12},{12,4},... | collective-permute-start | bytes 1572872 | tf_op jit(solution)/shard_map/ppermute | solution.py:18
  145.3 1.2 copy-start
  146.6 30.9 %all-to-all-start.4 = ((bf16[32,16,1792]{2,1,0:T(8,128)(2,1)}), bf16[32,16,1792]{2,1,0:T(8,128)(2,1)S(1)}, u32[]{:S(2)}, u32[]{:S(2)}) async-start(bf16[32,16,1792]{2,1,0:T(8,128)(2,1)} %bitcast.101), calls=%async_computation.4 | async-start | bytes 3670016 | tf_op jit(solution)/shard_map/all_to_all | solution.py:57
  153.0 1.5 copy-start.1
  157.6 31.3 %collective-permute-start.5 = (bf16[2,448,128]{2,1,0:T(8,128)(2,1)}, bf16[2,448,128]{2,1,0:T(8,128)(2,1)S(1)}, u32[]{:S(2)}, u32[]{:S(2)}) collective-permute-start(bf16[2,448,128]{2,1,0:T(8,128)(2,1)} %get-tuple-element.40), channel_id=1, source_target_pairs={{0,1},{1,0},{2,3},{3,2},{4,5},{5,4},{6,7},{7,6},{8,9},{9,8},{10,11... | collective-permute-start | bytes 688136 | tf_op jit(solution)/shard_map/ppermute | solution.py:115
  159.5 34.0 %collective-permute-start.6 = (bf16[2,448,128]{2,1,0:T(8,128)(2,1)S(1)}, bf16[2,448,128]{2,1,0:T(8,128)(2,1)S(1)}, u32[]{:S(2)}, u32[]{:S(2)}) collective-permute-start(bf16[2,448,128]{2,1,0:T(8,128)(2,1)S(1)} %get-tuple-element.42), channel_id=1, source_target_pairs={{0,2},{1,3},{2,0},{3,1},{4,6},{5,7},{6,4},{7,5},{8,10},{9,11},{10,... | collective-permute-start | bytes 688136 | tf_op jit(solution)/shard_map/ppermute | solution.py:115
  161.4 32.0 %collective-permute-start.7 = (bf16[2,448,128]{2,1,0:T(8,128)(2,1)S(1)}, bf16[2,448,128]{2,1,0:T(8,128)(2,1)}, u32[]{:S(2)}, u32[]{:S(2)}) collective-permute-start(bf16[2,448,128]{2,1,0:T(8,128)(2,1)S(1)} %get-tuple-element.41), channel_id=1, source_target_pairs={{0,3},{1,2},{2,1},{3,0},{4,7},{5,6},{6,5},{7,4},{8,11},{9,10},{10,... | collective-permute-start | bytes 688136 | tf_op jit(solution)/shard_map/ppermute | solution.py:115
  180.5 51.4 %all-to-all-start.5 = ((bf16[16,336,128]{2,1,0:T(8,128)(2,1)}), bf16[16,336,128]{2,1,0:T(8,128)(2,1)S(1)}, u32[]{:S(2)}, u32[]{:S(2)}) async-start(bf16[16,336,128]{2,1,0:T(8,128)(2,1)} %select_select_fusion), calls=%async_computation.5 | async-start | bytes 2752512 | tf_op jit(solution)/shard_map/all_to_all | solution.py:169
  185.0 14.0 %collective-permute-start.10 = (bf16[2,448,128]{2,1,0:T(8,128)(2,1)}, bf16[2,448,128]{2,1,0:T(8,128)(2,1)S(1)}, u32[]{:S(2)}, u32[]{:S(2)}) collective-permute-start(bf16[2,448,128]{2,1,0:T(8,128)(2,1)} %get-tuple-element.46), channel_id=1, source_target_pairs={{0,2},{1,3},{2,0},{3,1},{4,6},{5,7},{6,4},{7,5},{8,10},{9,11},{10,... | collective-permute-start | bytes 688136 | tf_op jit(solution)/shard_map/ppermute | solution.py:115
  187.0 12.1 %collective-permute-start.11 = (bf16[2,448,128]{2,1,0:T(8,128)(2,1)S(1)}, bf16[2,448,128]{2,1,0:T(8,128)(2,1)S(1)}, u32[]{:S(2)}, u32[]{:S(2)}) collective-permute-start(bf16[2,448,128]{2,1,0:T(8,128)(2,1)S(1)} %get-tuple-element.45), channel_id=1, source_target_pairs={{0,3},{1,2},{2,1},{3,0},{4,7},{5,6},{6,5},{7,4},{8,11},{9,10},{10,... | collective-permute-start | bytes 688136 | tf_op jit(solution)/shard_map/ppermute | solution.py:115
  188.9 18.2 %collective-permute-start.9 = (bf16[2,448,128]{2,1,0:T(8,128)(2,1)S(1)}, bf16[2,448,128]{2,1,0:T(8,128)(2,1)S(1)}, u32[]{:S(2)}, u32[]{:S(2)}) collective-permute-start(bf16[2,448,128]{2,1,0:T(8,128)(2,1)S(1)} %get-tuple-element.47), channel_id=1, source_target_pairs={{0,1},{1,0},{2,3},{3,2},{4,5},{5,4},{6,7},{7,6},{8,9},{9,8},{10,11... | collective-permute-start | bytes 688136 | tf_op jit(solution)/shard_map/ppermute | solution.py:115
  194.6 20.8 %collective-permute-start.8 = (bf16[448,128]{1,0:T(8,128)(2,1)S(1)}, bf16[448,128]{1,0:T(8,128)(2,1)S(1)}, u32[]{:S(2)}, u32[]{:S(2)}) collective-permute-start(bf16[448,128]{1,0:T(8,128)(2,1)S(1)} %dynamic-slice_bitcast_fusion.10), channel_id=1, source_target_pairs={{0,4},{4,0},{1,5},{5,1},{2,6},{6,2},{3,7},{7,3},{8,12},{12,8},{9,1... | collective-permute-start | bytes 344072 | tf_op jit(solution)/shard_map/ppermute | solution.py:18
  207.2 23.1 %collective-permute-start.12 = (bf16[448,128]{1,0:T(8,128)(2,1)S(1)}, bf16[448,128]{1,0:T(8,128)(2,1)S(1)}, u32[]{:S(2)}, u32[]{:S(2)}) collective-permute-start(bf16[448,128]{1,0:T(8,128)(2,1)S(1)} %get-tuple-element.48), channel_id=1, source_target_pairs={{0,23},{1,22},{2,21},{3,20},{4,19},{5,18},{6,17},{7,16},{16,7},{17... | collective-permute-start | bytes 344072 | tf_op jit(solution)/shard_map/ppermute | solution.py:22
  212.2 19.1 %collective-permute-start.13 = (bf16[448,128]{1,0:T(8,128)(2,1)S(1)}, bf16[448,128]{1,0:T(8,128)(2,1)S(1)}, u32[]{:S(2)}, u32[]{:S(2)}) collective-permute-start(bf16[448,128]{1,0:T(8,128)(2,1)S(1)} %get-tuple-element.49), channel_id=1, source_target_pairs={{0,19},{1,18},{2,17},{3,16},{4,23},{5,22},{6,21},{7,20},{16,3},{17... | collective-permute-start | bytes 344072 | tf_op jit(solution)/shard_map/ppermute | solution.py:177
